TPU v7x, 512 devices: a whole 4x8x8 slice. The times are simulated.
512 devices in a mesh: ctx: 16 (over z, core), head: 32 (over x, y).
Axes of the slice: x: 4, y: 8, z: 8, core: 2. Of those that a mesh axis runs over, the one named last changes fastest.
Arguments:
- queries: bfloat16 [8192, 4096], P('ctx', 'head'), may hold values from -180 to 180
- key_vectors: bfloat16 [8192, 4096], P('ctx', 'head'), may hold values from -7 to 7
- values: bfloat16 [8192, 4096], P('ctx', 'head'), may hold values from -6 to 6
- kernel: float32 [32, 6, 11], P('head'), may hold values from -0.6 to 0.6
- mixing: float32 [32, 2], P('head'), may hold values from 0.3 to 1
- norm_gain: float32 [4096], P('head'), may hold values from 0.5 to 1.5
- doc_lengths: int32 [8], replicated, may hold values from 1 to 4096, 8192 in all
Outputs:
- attended: bfloat16 [8192, 4096], P('ctx', 'head')
Inputs may be any that keep to these rules, and one draw needn't show every extreme that they name: `doc_lengths`: document lengths in order, summing to 8192, the longest exactly 4096.
All inputs are finite; a program needn't handle non-finite values.
Results may differ from a plain program's by a relative error of at most 0.007.
Values may be sent and summed in bfloat16 or wider, within the bound.
No kernel may reach another device: no remote copies, remote signals or barrier semaphores. Data moves between devices by JAX's collectives and lax.ppermute only.
A program may use at most 64 MiB of HBM per device.

v0:
```python
import math

import jax
import jax.numpy as jnp
from jax import lax
from jax.sharding import PartitionSpec as P

HEAD_DIM = 128


NEG_FILL = -1e30


def partner(value, axis, apart):
    return lax.ppermute(value, axis, [(i, i ^ 1 << apart) for i in range(lax.axis_size(axis))])


def from_behind(value, axis, steps):
    count = lax.axis_size(axis)
    leading, last = (max(0, -steps), min(count, count - steps))
    return lax.ppermute(value, axis, [(source, source + steps) for source in range(leading, last)])


def doc_ids(positions, doc_ends):
    return jnp.sum((positions[:, None] >= doc_ends[None, :]).astype(jnp.int32), axis=1)


def block_update(running, query_ext, first_row, key_blk, value_blk, first_col, kernel, doc_ends):
    run_max, run_total, run_acc = running
    rim_q = kernel.shape[1] - 1
    rim_k = (kernel.shape[2] - 1) // 2
    rows_blk = query_ext.shape[0] - rim_q
    cols_blk = value_blk.shape[0]
    scores = jnp.einsum(
        "ahd,bhd->hab", query_ext, key_blk, preferred_element_type=jnp.float32
    ) * HEAD_DIM ** (-0.5)
    row_pos = first_row - rim_q + jnp.arange(rows_blk + rim_q, dtype=jnp.int32)
    col_pos = first_col - rim_k + jnp.arange(cols_blk + 2 * rim_k, dtype=jnp.int32)
    allowed = (
        (col_pos[None, :] >= 0)
        & (col_pos[None, :] <= row_pos[:, None])
        & (doc_ids(row_pos, doc_ends)[:, None] == doc_ids(col_pos, doc_ends)[None, :])
    )
    masked = jnp.where(allowed[None], scores, 0.0)
    conv = masked[:, rim_q:, rim_k : rim_k + cols_blk]
    for tap_q in range(kernel.shape[1]):
        for tap_k in range(kernel.shape[2]):
            conv = (
                conv
                + kernel[:, tap_q, tap_k][:, None, None]
                * masked[
                    :,
                    rim_q - tap_q : rim_q - tap_q + rows_blk,
                    2 * rim_k - tap_k : 2 * rim_k - tap_k + cols_blk,
                ]
            )
    logits = jnp.where(allowed[None, rim_q:, rim_k : rim_k + cols_blk], conv, NEG_FILL)
    new_max = jnp.maximum(run_max, jnp.max(logits, axis=2))
    factor = jnp.exp(run_max - new_max)
    weights = jnp.exp(logits - new_max[:, :, None])
    new_total = run_total * factor + jnp.sum(weights, axis=2)
    products = jnp.einsum(
        "hij,jhe->ihe", weights.astype(jnp.bfloat16), value_blk, preferred_element_type=jnp.float32
    )
    new_acc = run_acc * jnp.transpose(factor)[:, :, None] + products
    return (new_max, new_total, new_acc)


def sweep_keys(runnings, query_sets, key_ext, value_all, key_start, block_len, kernel, doc_ends):
    rim_q = kernel.shape[1] - 1
    rim_k = (kernel.shape[2] - 1) // 2
    total_blocks = value_all.shape[0] // block_len
    results = []
    for running, query_set in zip(runnings, query_sets):
        query_ext, first_row = query_set
        limit = first_row + query_ext.shape[0] - rim_q
        block_count = jnp.clip((limit - key_start + block_len - 1) // block_len, 0, total_blocks)

        def advance(step_idx, current, query_ext=query_ext, first_row=first_row):
            offset = step_idx * block_len
            key_blk = lax.dynamic_slice_in_dim(key_ext, offset, block_len + 2 * rim_k, 0)
            value_blk = lax.dynamic_slice_in_dim(value_all, offset, block_len, 0)
            return block_update(
                current,
                query_ext,
                first_row,
                key_blk,
                value_blk,
                key_start + offset,
                kernel,
                doc_ends,
            )

        results.append(lax.fori_loop(0, block_count, advance, running))
    return tuple(results)


def body(queries, key_vectors, values, kernel, mixing, norm_gain, doc_lengths):
    rows_dev = queries.shape[0]
    heads_dev = queries.shape[1] // HEAD_DIM
    rim_q = kernel.shape[1] - 1
    rim_k = (kernel.shape[2] - 1) // 2
    my_group = lax.axis_index("ctx")
    top_bit = lax.axis_size("head").bit_length() - 2
    doc_ends = jnp.cumsum(doc_lengths)
    block_keys = 2 * rows_dev
    partner_vals = partner(values, "head", top_bit)
    query_heads = queries.reshape(rows_dev, heads_dev, HEAD_DIM)
    key_heads = key_vectors.reshape(rows_dev, heads_dev, HEAD_DIM)
    value_pairs = jnp.concatenate(
        [
            values.reshape(rows_dev, heads_dev, HEAD_DIM),
            partner_vals.reshape(rows_dev, heads_dev, HEAD_DIM),
        ],
        axis=2,
    )
    rim_rows = from_behind(query_heads[rows_dev - rim_q :], "ctx", 1)
    query_sets = [(jnp.concatenate([rim_rows, query_heads], axis=0), my_group * rows_dev)]
    runnings = []
    for query_set in query_sets:
        rows_set = query_set[0].shape[0] - rim_q
        runnings.append(
            (
                jnp.full((heads_dev, rows_set), NEG_FILL, jnp.float32),
                jnp.zeros((heads_dev, rows_set), jnp.float32),
                jnp.zeros((rows_set, heads_dev, 2 * HEAD_DIM), jnp.float32),
            )
        )
    runnings = tuple(runnings)
    key_all, pairs_all = (
        lax.all_gather(key_heads, "ctx", axis=0, tiled=True),
        lax.all_gather(value_pairs, "ctx", axis=0, tiled=True),
    )
    key_pad = jnp.pad(key_all, ((rim_k, rim_k), (0, 0), (0, 0)))
    runnings = sweep_keys(
        runnings,
        query_sets,
        key_pad,
        pairs_all,
        0,
        math.gcd(block_keys, key_all.shape[0]),
        kernel,
        doc_ends,
    )
    own_parts = []
    cross_parts = []
    for running in runnings:
        scale_rows = jnp.transpose(running[1])[:, :, None]
        own_parts.append(running[2][:, :, :HEAD_DIM] / scale_rows)
        cross_parts.append(running[2][:, :, HEAD_DIM:] / scale_rows)
    own_terms = own_parts[0]
    cross_terms = cross_parts[0].astype(jnp.bfloat16).reshape(rows_dev, heads_dev * HEAD_DIM)
    received = partner(cross_terms, "head", top_bit)
    received = received.reshape(rows_dev, heads_dev, HEAD_DIM).astype(jnp.float32)
    mixed = mixing[:, 0][None, :, None] * own_terms + mixing[:, 1][None, :, None] * received
    normed = (
        mixed
        * lax.rsqrt(jnp.mean(mixed * mixed, axis=2, keepdims=True) + 1e-05)
        * norm_gain.reshape(heads_dev, HEAD_DIM)[None]
    )
    finished = normed.astype(jnp.bfloat16).reshape(rows_dev, heads_dev * HEAD_DIM)
    return finished


def solution(mesh):
    return jax.shard_map(
        body,
        mesh=mesh,
        in_specs=(
            P("ctx", "head"),
            P("ctx", "head"),
            P("ctx", "head"),
            P("head", None, None),
            P("head", None),
            P("head"),
            P(),
        ),
        out_specs=P("ctx", "head"),
        check_vma=False,
    )
```

profile of v0, /device:TPU:448, one launch (start us, length us, event | category | flops | bytes accessed | tf_op | source)
XLA Modules:
  0.0 803.1 jit_solution(13410139564128758797)
XLA Ops:
  6.5 0.7 all-gather.6.cloned.1.call-update
  7.3 4.9 collective-permute-start.1
  12.2 3.9 collective-permute-done.1
  16.1 1.7 pad_maximum_fusion
  18.5 1.9 collective-permute-start
  20.4 0.8 reduce-window.9
  21.3 2.1 collective-permute-done
  23.4 0.9 pad_maximum_fusion.1
  24.4 25.1 %all-gather.6.cloned.1.call-done = bf16[8192,128]{1,0:T(8,128)(2,1)} async-done(((bf16[512,128]{1,0:T(8,128)(2,1)}), bf16[8192,128]{1,0:T(8,128)(2,1)}) %all-gather.6.cloned.1.call-update) | async-done | bytes 2097168 | tf_op jit(solution)/shard_map/all_gather | solution.py:131
  49.5 2.8 pad.4
  52.3 43.4 %all-gather.4.cloned.1.call-done = bf16[8192,1,256]{2,0,1:T(8,128)(2,1)} async-done(((bf16[512,1,256]{2,0,1:T(8,128)(2,1)}), bf16[8192,1,256]{2,0,1:T(8,128)(2,1)}) %all-gather.4.cloned.1.call-update) | async-done | bytes 4194320 | tf_op jit(solution)/shard_map/all_gather | solution.py:132
  95.9 688.6 %while.17 = (s32[]{:T(128)}, f32[1,512]{1,0:T(1,128)S(1)}, f32[1,512]{1,0:T(1,128)S(1)}, f32[512,1,256]{0,2,1:T(8,128)S(1)}, s32[]{:T(128)}, /*index=5*/s32[]{:T...) while((s32[]{:T(128)}, f32[1,512]{1,0:T(1,128)S(1)}, ...), condition=%wide.region_6.7_spmd, body=%wide.region_1.6_spmd.sunk | while | flops 483287392 | bytes 149952528 | solution.py:94
  96.1 1.8 fusion.112
  98.6 0.7 fusion.113
  99.4 0.7 fusion.114
  100.1 0.7 fusion.115
  101.5 78.1 %fusion.117 = (f32[512]{0:T(512)S(1)}, f32[1,512,1024]{2,1,0:T(8,128)S(1)}) fusion(f32[1,517,1034]{2,1,0:T(8,128)S(1)} %fusion.112, f32[]{:T(128)} %bitcast.203, f32[]{:T(128)} %bitcast.204, f32[]{:T(128)} %bitcast.205, f32[]{:T(128)} %bitcast.206, f32[]{:T(128)} %bitcast.207, f32[]{:T(128)} %bitcast.208, f32[]{:T(128)} %bitcast.209, f32[]{:T(128)} %bitcast.210, ...), kind=kLoop, calls=%fused_computation.172.clone.1 | loop fusion | flops 70254080 | bytes 141035776 | tf_op jit(solution)/shard_map/while/body/reduce_max | solution.py:58
  180.1 1.8 fusion.119
  182.2 1.8 fusion.112
  184.7 0.7 fusion.113
  185.4 0.7 fusion.114
  186.2 0.7 fusion.115
  187.6 78.1 %fusion.117 = (f32[512]{0:T(512)S(1)}, f32[1,512,1024]{2,1,0:T(8,128)S(1)}) fusion(f32[1,517,1034]{2,1,0:T(8,128)S(1)} %fusion.112, f32[]{:T(128)} %bitcast.203, f32[]{:T(128)} %bitcast.204, f32[]{:T(128)} %bitcast.205, f32[]{:T(128)} %bitcast.206, f32[]{:T(128)} %bitcast.207, f32[]{:T(128)} %bitcast.208, f32[]{:T(128)} %bitcast.209, f32[]{:T(128)} %bitcast.210, ...), kind=kLoop, calls=%fused_computation.172.clone.1 | loop fusion | flops 70254080 | bytes 141035776 | tf_op jit(solution)/shard_map/while/body/reduce_max | solution.py:58
  266.2 1.8 fusion.119
  268.3 1.8 fusion.112
  270.8 0.7 fusion.113
  271.5 0.7 fusion.114
  272.2 0.7 fusion.115
  273.7 78.1 %fusion.117 = (f32[512]{0:T(512)S(1)}, f32[1,512,1024]{2,1,0:T(8,128)S(1)}) fusion(f32[1,517,1034]{2,1,0:T(8,128)S(1)} %fusion.112, f32[]{:T(128)} %bitcast.203, f32[]{:T(128)} %bitcast.204, f32[]{:T(128)} %bitcast.205, f32[]{:T(128)} %bitcast.206, f32[]{:T(128)} %bitcast.207, f32[]{:T(128)} %bitcast.208, f32[]{:T(128)} %bitcast.209, f32[]{:T(128)} %bitcast.210, ...), kind=kLoop, calls=%fused_computation.172.clone.1 | loop fusion | flops 70254080 | bytes 141035776 | tf_op jit(solution)/shard_map/while/body/reduce_max | solution.py:58
  352.3 1.8 fusion.119
  354.3 1.8 fusion.112
  356.9 0.7 fusion.113
  357.6 0.7 fusion.114
  358.3 0.7 fusion.115
  359.7 78.1 %fusion.117 = (f32[512]{0:T(512)S(1)}, f32[1,512,1024]{2,1,0:T(8,128)S(1)}) fusion(f32[1,517,1034]{2,1,0:T(8,128)S(1)} %fusion.112, f32[]{:T(128)} %bitcast.203, f32[]{:T(128)} %bitcast.204, f32[]{:T(128)} %bitcast.205, f32[]{:T(128)} %bitcast.206, f32[]{:T(128)} %bitcast.207, f32[]{:T(128)} %bitcast.208, f32[]{:T(128)} %bitcast.209, f32[]{:T(128)} %bitcast.210, ...), kind=kLoop, calls=%fused_computation.172.clone.1 | loop fusion | flops 70254080 | bytes 141035776 | tf_op jit(solution)/shard_map/while/body/reduce_max | solution.py:58
  438.4 1.8 fusion.119
  440.4 1.8 fusion.112
  442.9 0.7 fusion.113
  443.7 0.7 fusion.114
  444.4 0.7 fusion.115
  445.8 78.1 %fusion.117 = (f32[512]{0:T(512)S(1)}, f32[1,512,1024]{2,1,0:T(8,128)S(1)}) fusion(f32[1,517,1034]{2,1,0:T(8,128)S(1)} %fusion.112, f32[]{:T(128)} %bitcast.203, f32[]{:T(128)} %bitcast.204, f32[]{:T(128)} %bitcast.205, f32[]{:T(128)} %bitcast.206, f32[]{:T(128)} %bitcast.207, f32[]{:T(128)} %bitcast.208, f32[]{:T(128)} %bitcast.209, f32[]{:T(128)} %bitcast.210, ...), kind=kLoop, calls=%fused_computation.172.clone.1 | loop fusion | flops 70254080 | bytes 141035776 | tf_op jit(solution)/shard_map/while/body/reduce_max | solution.py:58
  524.5 1.8 fusion.119
  526.5 1.8 fusion.112
  529.0 0.7 fusion.113
  529.8 0.7 fusion.114
  530.5 0.7 fusion.115
  531.9 78.1 %fusion.117 = (f32[512]{0:T(512)S(1)}, f32[1,512,1024]{2,1,0:T(8,128)S(1)}) fusion(f32[1,517,1034]{2,1,0:T(8,128)S(1)} %fusion.112, f32[]{:T(128)} %bitcast.203, f32[]{:T(128)} %bitcast.204, f32[]{:T(128)} %bitcast.205, f32[]{:T(128)} %bitcast.206, f32[]{:T(128)} %bitcast.207, f32[]{:T(128)} %bitcast.208, f32[]{:T(128)} %bitcast.209, f32[]{:T(128)} %bitcast.210, ...), kind=kLoop, calls=%fused_computation.172.clone.1 | loop fusion | flops 70254080 | bytes 141035776 | tf_op jit(solution)/shard_map/while/body/reduce_max | solution.py:58
  610.5 1.8 fusion.119
  612.6 1.8 fusion.112
  615.1 0.7 fusion.113
  615.8 0.7 fusion.114
  616.6 0.7 fusion.115
  618.0 78.1 %fusion.117 = (f32[512]{0:T(512)S(1)}, f32[1,512,1024]{2,1,0:T(8,128)S(1)}) fusion(f32[1,517,1034]{2,1,0:T(8,128)S(1)} %fusion.112, f32[]{:T(128)} %bitcast.203, f32[]{:T(128)} %bitcast.204, f32[]{:T(128)} %bitcast.205, f32[]{:T(128)} %bitcast.206, f32[]{:T(128)} %bitcast.207, f32[]{:T(128)} %bitcast.208, f32[]{:T(128)} %bitcast.209, f32[]{:T(128)} %bitcast.210, ...), kind=kLoop, calls=%fused_computation.172.clone.1 | loop fusion | flops 70254080 | bytes 141035776 | tf_op jit(solution)/shard_map/while/body/reduce_max | solution.py:58
  696.6 1.8 fusion.119
  698.7 1.8 fusion.112
  701.2 0.7 fusion.113
  701.9 0.7 fusion.114
  702.6 0.7 fusion.115
  704.1 78.1 %fusion.117 = (f32[512]{0:T(512)S(1)}, f32[1,512,1024]{2,1,0:T(8,128)S(1)}) fusion(f32[1,517,1034]{2,1,0:T(8,128)S(1)} %fusion.112, f32[]{:T(128)} %bitcast.203, f32[]{:T(128)} %bitcast.204, f32[]{:T(128)} %bitcast.205, f32[]{:T(128)} %bitcast.206, f32[]{:T(128)} %bitcast.207, f32[]{:T(128)} %bitcast.208, f32[]{:T(128)} %bitcast.209, f32[]{:T(128)} %bitcast.210, ...), kind=kLoop, calls=%fused_computation.172.clone.1 | loop fusion | flops 70254080 | bytes 141035776 | tf_op jit(solution)/shard_map/while/body/reduce_max | solution.py:58
  782.7 1.8 fusion.119
  784.9 4.9 collective-permute-start.2
  790.4 3.5 collective-permute-done.2
  793.9 1.5 multiply_reduce_fusion
  795.4 0.8 fusion.86
  (105 shorter events, 18.6 us)
Async XLA Ops:
  6.5 42.9 %all-gather.6.cloned.1.call-start = ((), (), s32[]{:S(2)}) async-start(), calls=%async_computation.1 | async-start | bytes 2228224 | tf_op jit(solution)/shard_map/all_gather | solution.py:131
  7.3 88.5 %all-gather.4.cloned.1.call-start = ((), (), s32[]{:S(2)}) async-start(), calls=%async_computation | async-start | bytes 4456448 | tf_op jit(solution)/shard_map/all_gather | solution.py:132
  7.3 8.8 %collective-permute-start.1 = (bf16[512,128]{1,0:T(8,128)(2,1)}, bf16[512,128]{1,0:T(8,128)(2,1)S(1)}, u32[]{:S(2)}, u32[]{:S(2)}) collective-permute-start(bf16[512,128]{1,0:T(8,128)(2,1)} %param.11), channel_id=1, source_target_pairs={{0,16},{1,17},{2,18},{3,19},{4,20},{5,21},{6,22},{7,23},{8,24},{9,... | collective-permute-start | bytes 393224 | tf_op jit(solution)/shard_map/ppermute | solution.py:15
  18.5 4.9 collective-permute-start
  49.5 46.4 %copy-start = (f32[1,6,11]{2,0,1:T(1,128)S(1)}, f32[1,6,11]{2,0,1:T(1,128)}, u32[]{:S(2)}) copy-start(f32[1,6,11]{2,0,1:T(1,128)} %param.12) | copy-start | bytes 796
  95.8 693.9 %copy-start.1 = (f32[1,2]{1,0:T(1,128)S(1)}, f32[1,2]{1,0:T(1,128)}, u32[]{:S(2)}) copy-start(f32[1,2]{1,0:T(1,128)} %param.13) | copy-start | bytes 28
  784.5 10.9 %copy-start.2 = (f32[128]{0:T(128)S(1)}, f32[128]{0:T(128)}, u32[]{:S(2)}) copy-start(f32[128]{0:T(128)} %param.14) | copy-start | bytes 1540
  784.9 9.0 %collective-permute-start.2 = (bf16[512,128]{1,0:T(8,128)(2,1)S(1)}, bf16[512,128]{1,0:T(8,128)(2,1)S(1)}, u32[]{:S(2)}, u32[]{:S(2)}) collective-permute-start(bf16[512,128]{1,0:T(8,128)(2,1)S(1)} %fusion.87), channel_id=1, source_target_pairs={{0,16},{1,17},{2,18},{3,19},{4,20},{5,21},{6,22},{7,23},{8,24},{9,... | collective-permute-start | bytes 393224 | tf_op jit(solution)/shard_map/ppermute | solution.py:15
Sparse Core Ops, SparseCore 0:
  9.5 39.9 all-gather.5
  51.6 44.1 all-gather.3
where the time goes:
time: 809 us; the launch traced here: 803 us
  other arithmetic  642 us (79%)
  waiting for transfers between devices  78.8 us (10%)
  matrix products  28.9 us (4%)
  local copies, waits for them, and re-layouts  27.3 us (3%)
  between operations  13.5 us (2%)
  starting transfers between devices  11.8 us (1%)
    reduce_max x8, other arithmetic, block_update(): new_max = jnp.maximum(run_max, jnp.max(logits, axis=2))  625 us
    all_gather x1, waiting for transfers between devices, body(): lax.all_gather(value_pairs, 'ctx', axis=0, tiled=True)  43.4 us
    all_gather x1, waiting for transfers between devices, body(): lax.all_gather(key_heads, 'ctx', axis=0, tiled=True)  25.1 us
    slice x32, local copies, waits for them, and re-layouts, block_update(): kernel[:, tap_q, tap_k][:, None, None]  22.9 us
  transfers between devices with their start and end apart: 5, of which 5 were waited for; matrix products, arithmetic and copies ran while one was open for 1% of the time, Pallas kernels for 0%

commit v1 on v0

v1 whole, which is shorter than its diff:
```python
import functools

import jax
import jax.numpy as jnp
from jax import lax
from jax.experimental import pallas as pl
from jax.experimental.pallas import tpu as pltpu
from jax.sharding import PartitionSpec as P

HEAD_DIM = 128
SCALE = HEAD_DIM ** (-0.5)
MASKED = -1e30
FLOOR = -1e20
HALO = 16
BAND = 64
GROUP = 128
WIDE = 256
REACH = 10
HOPS = 4


def dot(a, b):
    return lax.dot_general(a, b, (((1,), (0,)), ((), ())), preferred_element_type=jnp.float32)


def dot_t(a, b):
    return lax.dot_general(a, b, (((1,), (1,)), ((), ())), preferred_element_type=jnp.float32)


def starts_of(position, ends):
    start = jnp.zeros_like(position)
    for end in ends:
        start = jnp.where(position >= end, end, start)
    return start


def widen(column, times):
    return jnp.concatenate([column] * times, axis=1) if times > 1 else column


def absorb(rows, logits, values, m_ref, l_ref, acc_ref):
    m_old = m_ref[rows, :]
    m_new = jnp.maximum(m_old, jnp.max(logits, axis=1, keepdims=True))
    weights = jnp.exp(logits - widen(m_new, logits.shape[1] // 128))
    factor = jnp.exp(m_old - m_new)
    m_ref[rows, :] = m_new
    l_ref[rows, :] = l_ref[rows, :] * factor + jnp.sum(weights, axis=1, keepdims=True)
    acc_ref[rows, :] = acc_ref[rows, :] * widen(factor, 2) + dot(
        weights.astype(jnp.bfloat16), values
    )


def lay_keys(k_ref, vh_ref, kx_ref, vx_ref):
    keys = k_ref.shape[0]
    kx_ref[0:HALO, :] = vh_ref[keys : keys + HALO, 0:HEAD_DIM]
    kx_ref[HALO : HALO + keys, :] = k_ref[...]
    kx_ref[HALO + keys : 2 * HALO + keys, :] = vh_ref[keys : keys + HALO, HEAD_DIM:]
    vx_ref[0:HALO, :] = jnp.zeros((HALO, 2 * HEAD_DIM), jnp.bfloat16)
    vx_ref[HALO : HALO + keys, :] = vh_ref[0:keys, :]
    vx_ref[HALO + keys :, :] = jnp.zeros((HALO, 2 * HEAD_DIM), jnp.bfloat16)


def near(a, chip_row, block, ends, taps_ref, qp_ref, kx_ref, vx_ref, m_ref, l_ref, acc_ref):
    keys = vx_ref.shape[0] - 2 * HALO
    query_taps, key_taps = qp_ref.shape[1] // HEAD_DIM, taps_ref.shape[0] // (qp_ref.shape[1] // HEAD_DIM)
    rim = (key_taps - 1) // 2
    low = pl.multiple_of(jnp.clip(a - 32, 0, keys + 2 * HALO - GROUP), 16)
    rows = pl.ds(pl.multiple_of(block - chip_row + a, 16), BAND)
    window = kx_ref[pl.ds(low, GROUP), :]
    shape = (BAND, GROUP)
    row = block + a + lax.broadcasted_iota(jnp.int32, shape, 0)
    col = block - HALO + low + lax.broadcasted_iota(jnp.int32, shape, 1)
    sums = [None] * key_taps
    own_start = None
    for u in range(query_taps):
        scores = dot_t(qp_ref[rows, u * HEAD_DIM : (u + 1) * HEAD_DIM], window)
        start = starts_of(row - u, ends)
        if u == 0:
            own_start = start
        scores = jnp.where((col <= row - u) & (col >= start), scores, 0.0)
        for t in range(key_taps):
            tap = taps_ref[u * key_taps + t] * SCALE
            if u == 0 and t == rim:
                tap = tap + SCALE
            sums[t] = scores * tap if u == 0 else sums[t] + scores * tap
    conv = sums[rim]
    for t in range(key_taps):
        if t != rim:
            conv = conv + pltpu.roll(sums[t], (t - rim) % GROUP, 1)
    inside = (col >= block) & (col < block + keys)
    inside = inside & (col <= row) & (col > row - REACH) & (col >= own_start)
    logits = jnp.where(inside, conv, MASKED)
    absorb(rows, logits, vx_ref[pl.ds(low, GROUP), :], m_ref, l_ref, acc_ref)


def convolve(local, block, first_start, ends, th_ref, tl_ref, kx_ref, kp_ref):
    total = kx_ref.shape[0]
    keys = kp_ref.shape[0]
    width = kp_ref.shape[1] // 2
    taps = width // HEAD_DIM
    depth = th_ref.shape[1]
    if local:
        for g in range(keys // GROUP):
            shape = (GROUP, depth)
            out = block + g * GROUP + lax.broadcasted_iota(jnp.int32, shape, 0)
            inp = block + g * GROUP - HALO + lax.broadcasted_iota(jnp.int32, shape, 1)
            keep = inp >= starts_of(out, ends)
            window = kx_ref[g * GROUP : g * GROUP + depth, :]
            for u in range(taps):
                part = slice(u * GROUP, (u + 1) * GROUP)
                high = jnp.where(keep, th_ref[part, :].astype(jnp.float32), 0.0).astype(jnp.bfloat16)
                rest = jnp.where(keep, tl_ref[part, :].astype(jnp.float32), 0.0).astype(jnp.bfloat16)
                done = dot(high, window) + dot(rest, window)
                top = done.astype(jnp.bfloat16)
                here = slice(g * GROUP, (g + 1) * GROUP)
                kp_ref[here, u * HEAD_DIM : (u + 1) * HEAD_DIM] = top
                kp_ref[here, width + u * HEAD_DIM : width + (u + 1) * HEAD_DIM] = (
                    done - top.astype(jnp.float32)
                ).astype(jnp.bfloat16)
        return
    place = block - HALO + lax.broadcasted_iota(jnp.int32, (total, HEAD_DIM), 0)
    kx_ref[...] = jnp.where(place >= first_start, kx_ref[...].astype(jnp.float32), 0.0).astype(
        jnp.bfloat16
    )
    for g in range(0, keys // GROUP, 2):
        window = jnp.concatenate(
            [kx_ref[n * GROUP : n * GROUP + depth, :] for n in (g, g + 1)], axis=1
        )
        for u in range(taps):
            part = slice(u * GROUP, (u + 1) * GROUP)
            done = dot(th_ref[part, :], window) + dot(tl_ref[part, :], window)
            top = done.astype(jnp.bfloat16)
            rest = (done - top.astype(jnp.float32)).astype(jnp.bfloat16)
            for n in (0, 1):
                here = slice((g + n) * GROUP, (g + n + 1) * GROUP)
                lanes = slice(n * HEAD_DIM, (n + 1) * HEAD_DIM)
                kp_ref[here, u * HEAD_DIM : (u + 1) * HEAD_DIM] = top[:, lanes]
                kp_ref[here, width + u * HEAD_DIM : width + (u + 1) * HEAD_DIM] = rest[:, lanes]


def far(chip_row, block, ends, qp_ref, kp_ref, vx_ref, m_ref, l_ref, acc_ref):
    keys = kp_ref.shape[0]
    width = qp_ref.shape[1]

    @pl.loop(0, qp_ref.shape[0] // WIDE)
    def _(tile):
        first = tile * WIDE
        top = chip_row + first
        needed = (top + WIDE - 1 >= block + REACH) & (block + keys > starts_of(top, ends))

        @pl.when(needed)
        def _():
            rows = pl.ds(pl.multiple_of(first, WIDE), WIDE)
            query = qp_ref[rows, :]
            conv = dot_t(query, kp_ref[:, 0:width]) + dot_t(query, kp_ref[:, width:])
            shape = (WIDE, GROUP)
            row = top + lax.broadcasted_iota(jnp.int32, shape, 0)
            start = widen(starts_of(row, ends) - block, keys // GROUP)
            row = widen(row - (REACH + block), keys // GROUP)
            col = lax.broadcasted_iota(jnp.int32, (WIDE, keys), 1)
            logits = jnp.where((col <= row) & (col >= start), conv, MASKED)
            absorb(rows, logits, vx_ref[HALO : HALO + keys, :], m_ref, l_ref, acc_ref)


def ends_of(place_ref):
    return [place_ref[2 + d] for d in range(7)]


def local_kernel(
    place_ref, taps_ref, qx_ref, k_ref, vh_ref,
    qp_ref, th_ref, tl_ref, m_ref, l_ref, acc_ref,
    kx_ref, vx_ref, kp_ref,
):
    chip_row, block = place_ref[0], place_ref[1]
    ends = ends_of(place_ref)
    keys = k_ref.shape[0]
    taps = qp_ref.shape[1] // HEAD_DIM
    key_taps = taps_ref.shape[0] // taps
    rim = (key_taps - 1) // 2
    queries = qx_ref[...].astype(jnp.float32)
    for u in range(taps):
        shifted = queries if u == 0 else pltpu.roll(queries, u, 0)
        qp_ref[:, u * HEAD_DIM : (u + 1) * HEAD_DIM] = shifted[HALO:, :].astype(jnp.bfloat16)
    shape = (GROUP, th_ref.shape[1])
    ahead = lax.broadcasted_iota(jnp.int32, shape, 1) - lax.broadcasted_iota(jnp.int32, shape, 0)
    for u in range(taps):
        band = jnp.zeros(shape, jnp.float32)
        for t in range(key_taps):
            tap = taps_ref[u * key_taps + t] * SCALE
            if u == 0 and t == rim:
                tap = tap + SCALE
            band = jnp.where(ahead == HALO + rim - t, tap, band)
        high = band.astype(jnp.bfloat16)
        th_ref[u * GROUP : (u + 1) * GROUP, :] = high
        tl_ref[u * GROUP : (u + 1) * GROUP, :] = (band - high.astype(jnp.float32)).astype(
            jnp.bfloat16
        )
    m_ref[...] = jnp.full(m_ref.shape, FLOOR, jnp.float32)
    l_ref[...] = jnp.zeros(l_ref.shape, jnp.float32)
    acc_ref[...] = jnp.zeros(acc_ref.shape, jnp.float32)
    kx_ref[...] = jnp.zeros(kx_ref.shape, jnp.bfloat16)
    lay_keys(k_ref, vh_ref, kx_ref, vx_ref)

    @pl.loop(0, keys // BAND + 1)
    def _(tile):
        a = tile * BAND

        @pl.when(block - chip_row + a < qp_ref.shape[0])
        def _():
            near(
                a, chip_row, block, ends, taps_ref, qp_ref, kx_ref, vx_ref, m_ref, l_ref, acc_ref
            )

    convolve(True, block, 0, ends, th_ref, tl_ref, kx_ref, kp_ref)
    far(chip_row, block, ends, qp_ref, kp_ref, vx_ref, m_ref, l_ref, acc_ref)


def hop_kernel(
    last, place_ref, taps_ref, qp_ref, th_ref, tl_ref, k_ref, vh_ref, m_in, l_in, acc_in, *rest
):
    if last:
        keep_ref, send_ref, kx_ref, vx_ref, kp_ref, m_ref, l_ref, acc_ref = rest
    else:
        m_ref, l_ref, acc_ref, kx_ref, vx_ref, kp_ref = rest
    chip_row, block = place_ref[0], place_ref[1]
    ends = ends_of(place_ref)
    keys = k_ref.shape[0]
    first_start = starts_of(chip_row, ends)
    m_ref[...] = m_in[...]
    l_ref[...] = l_in[...]
    acc_ref[...] = acc_in[...]

    @pl.when(block + keys > first_start)
    def _():
        kx_ref[...] = jnp.zeros(kx_ref.shape, jnp.bfloat16)
        lay_keys(k_ref, vh_ref, kx_ref, vx_ref)

        @pl.when(block + keys == chip_row)
        def _():
            near(
                keys, chip_row, block, ends, taps_ref, qp_ref, kx_ref, vx_ref, m_ref, l_ref, acc_ref
            )

        convolve(False, block, first_start, ends, th_ref, tl_ref, kx_ref, kp_ref)
        far(chip_row, block, ends, qp_ref, kp_ref, vx_ref, m_ref, l_ref, acc_ref)

    if last:
        core = place_ref[9]
        lane = lax.broadcasted_iota(jnp.int32, (keys, 128), 1)
        for ref, side in ((keep_ref, core), (send_ref, 1 - core)):
            rows = pl.ds(pl.multiple_of(side * keys, keys), keys)
            ref[:, 0 : 2 * HEAD_DIM] = acc_ref[rows, :]
            ref[:, 2 * HEAD_DIM :] = jnp.where(lane < 64, m_ref[rows, :], l_ref[rows, :])


def join_kernel(keep_ref, other_ref, own_ref, cross_ref):
    wide = 2 * HEAD_DIM
    stats, more = keep_ref[:, wide:], other_ref[:, wide:]
    m_a, l_a = stats[:, 0:1], stats[:, 64:65]
    m_b, l_b = more[:, 0:1], more[:, 64:65]
    m = jnp.maximum(m_a, m_b)
    f_a, f_b = jnp.exp(m_a - m), jnp.exp(m_b - m)
    share = 1.0 / (l_a * f_a + l_b * f_b)
    f_a, f_b = f_a * share, f_b * share
    own_ref[...] = keep_ref[:, :HEAD_DIM] * f_a + other_ref[:, :HEAD_DIM] * f_b
    cross_ref[...] = (
        keep_ref[:, HEAD_DIM:wide] * f_a + other_ref[:, HEAD_DIM:wide] * f_b
    ).astype(jnp.bfloat16)


def finish_kernel(mixing_ref, own_ref, cross_ref, gain_ref, out_ref):
    mixed = mixing_ref[0] * own_ref[...] + mixing_ref[1] * cross_ref[...].astype(jnp.float32)
    mean = jnp.mean(mixed * mixed, axis=1, keepdims=True)
    out_ref[...] = (mixed * lax.rsqrt(mean + 1e-05) * gain_ref[...]).astype(jnp.bfloat16)


VMEM = pl.BlockSpec(memory_space=pltpu.VMEM)
SMEM = pl.BlockSpec(memory_space=pltpu.SMEM)


def call(kernel, specs, out, scratch, args, aliases=None, flops=0):
    shapes = [jax.ShapeDtypeStruct(shape, dtype) for shape, dtype in out]
    return pl.pallas_call(
        kernel,
        out_shape=shapes,
        in_specs=specs,
        out_specs=[VMEM] * len(shapes),
        scratch_shapes=scratch,
        input_output_aliases=aliases or {},
        cost_estimate=pl.CostEstimate(flops=flops, bytes_accessed=4 << 20, transcendentals=0),
        compiler_params=pltpu.CompilerParams(vmem_limit_bytes=40 << 20),
    )(*args)


def body(queries, key_vectors, values, kernel, mixing, norm_gain, doc_lengths):
    rows = queries.shape[0]
    bf16, f32 = jnp.bfloat16, jnp.float32
    count = lax.axis_size("ctx")
    heads = lax.axis_size("head")
    group = lax.axis_index("ctx")
    core = group % 2
    taps = kernel.shape[1]
    width = taps * HEAD_DIM

    def permute(value, pairs):
        return lax.ppermute(value, "ctx", pairs)

    def onward(value):
        return permute(value, [(i, (i + 2) % count) for i in range(count)])

    def partner(value):
        return lax.ppermute(value, "head", [(i, i ^ (heads // 2)) for i in range(heads)])

    across = [(2 * i + 1, (2 * i + 2) % count) for i in range(count // 2)]
    across = across + [(b, a) for a, b in across]
    edge = permute(
        jnp.concatenate([key_vectors[:HALO], key_vectors[rows - HALO :], queries[rows - HALO :]]),
        across,
    )
    other_values = partner(values)
    sibling = permute(
        jnp.concatenate(
            [queries, key_vectors[:HALO], key_vectors[rows - HALO :], edge[2 * HALO :]]
        ),
        [(i, i ^ 1) for i in range(count)],
    )
    even = core == 0
    behind = jnp.where(even, edge[HALO : 2 * HALO], sibling[rows + HALO : rows + 2 * HALO])
    beyond = jnp.where(even, sibling[rows : rows + HALO], edge[:HALO])
    query_ext = jnp.where(
        even,
        jnp.concatenate([edge[2 * HALO :], queries, sibling[:rows]]),
        jnp.concatenate([sibling[rows + 2 * HALO :], sibling[:rows], queries]),
    )
    pairs = jnp.concatenate(
        [
            jnp.concatenate([values, other_values], axis=1),
            jnp.concatenate([behind, beyond], axis=1),
        ]
    )
    doc_ends = jnp.cumsum(doc_lengths)[:7]
    chip = group // 2

    def place(hop):
        head = jnp.stack([chip * 2 * rows, (chip - hop) * 2 * rows + core * rows])
        return jnp.concatenate([head, doc_ends, core[None]]).astype(jnp.int32)

    flat = kernel.reshape(-1)
    state = [((2 * rows, 128), f32), ((2 * rows, 128), f32), ((2 * rows, 2 * HEAD_DIM), f32)]
    scratch = [
        pltpu.VMEM((rows + 128, HEAD_DIM), bf16),
        pltpu.VMEM((rows + 2 * HALO, 2 * HEAD_DIM), bf16),
        pltpu.VMEM((rows, 2 * width), bf16),
    ]
    keys = key_vectors
    flops = 2 * 2 * rows * rows * (2 * width + 2 * HEAD_DIM)
    qp, high, low, m, l, acc = call(
        local_kernel,
        [SMEM, SMEM, VMEM, VMEM, VMEM],
        [((2 * rows, width), bf16), ((taps * GROUP, 256), bf16), ((taps * GROUP, 256), bf16)]
        + state,
        scratch,
        (place(0), flat, query_ext, keys, pairs),
        flops=flops,
    )
    for hop in range(1, HOPS + 1):
        keys, pairs = onward(keys), onward(pairs)
        last = hop == HOPS
        out = [((rows, 3 * HEAD_DIM), f32)] * 2 if last else state
        extra = [pltpu.VMEM(shape, dtype) for shape, dtype in state] if last else []
        result = call(
            functools.partial(hop_kernel, last),
            [SMEM, SMEM] + [VMEM] * 8,
            out,
            scratch + extra,
            (place(hop), flat, qp, high, low, keys, pairs, m, l, acc),
            aliases=None if last else {7: 0, 8: 1, 9: 2},
            flops=flops,
        )
        if not last:
            m, l, acc = result
    keep, send = result
    other = permute(send, [(i, i ^ 1) for i in range(count)])
    own, cross = call(
        join_kernel,
        [VMEM, VMEM],
        [((rows, HEAD_DIM), f32), ((rows, HEAD_DIM), bf16)],
        [],
        (keep, other),
    )
    (finished,) = call(
        finish_kernel,
        [SMEM, VMEM, VMEM, VMEM],
        [((rows, HEAD_DIM), bf16)],
        [],
        (mixing.reshape(-1), own, partner(cross), norm_gain.reshape(1, HEAD_DIM)),
    )
    return finished


def solution(mesh):
    return jax.shard_map(
        body,
        mesh=mesh,
        in_specs=(
            P("ctx", "head"),
            P("ctx", "head"),
            P("ctx", "head"),
            P("head", None, None),
            P("head", None),
            P("head"),
            P(),
        ),
        out_specs=P("ctx", "head"),
        check_vma=False,
    )
```

time: 809 us -> 102 us (0.13)
  the two profiles are of different devices: /device:TPU:448 before, /device:TPU:430 now
where the time goes in v1:
time: 102 us; the launch traced here: 101 us
  starting transfers between devices  38.2 us (37%)
  Pallas kernels  31.8 us (31%)
  waiting for transfers between devices  24.7 us (24%)
  other arithmetic  4.69 us (5%)
  local copies, waits for them, and re-layouts  1.56 us (2%)
    pallas_call x7, Pallas kernels, call(): pl.pallas_call(kernel, out_shape=shapes, in_specs=specs, out_specs=[VMEM]...  31.8 us
    ppermute x11, starting transfers between devices, permute(): return lax.ppermute(value, 'ctx', pairs)  31.6 us
    ppermute x11, waiting for transfers between devices, permute(): return lax.ppermute(value, 'ctx', pairs)  14.5 us
    ppermute x2, waiting for transfers between devices, partner(): lax.ppermute(value, 'head', [(i, i ^ heads // 2) for i in range(heads)])  10.2 us
    ppermute x2, starting transfers between devices, partner(): lax.ppermute(value, 'head', [(i, i ^ heads // 2) for i in range(heads)])  6.63 us
  transfers between devices with their start and end apart: 13, of which 6 were waited for; matrix products, arithmetic and copies ran while one was open for 4% of the time, Pallas kernels for 29%

profile of v1, /device:TPU:430, one launch (start us, length us, event | category | flops | bytes accessed | tf_op | source)
XLA Modules:
  0.0 101.2 jit_solution(17876339050845501074)
XLA Ops:
  0.0 0.0 copy-start
  0.0 0.8 fusion
  0.8 0.7 slice.44
  1.5 1.9 %collective-permute-start = (bf16[48,128]{1,0:T(8,128)(2,1)S(1)}, bf16[48,128]{1,0:T(8,128)(2,1)S(1)}, u32[]{:S(2)}, u32[]{:S(2)}) collective-permute-start(bf16[48,128]{1,0:T(8,128)(2,1)S(1)} %pad_maximum_fusion.1), channel_id=1, source_target_pairs={{32,64},{96,128},{160,192},{224,256},{288,320},{352,384},{416,448}... | collective-permute-start | bytes 36872 | tf_op jit(solution)/shard_map/ppermute | solution.py:306
  3.4 3.1 %collective-permute-done = bf16[48,128]{1,0:T(8,128)(2,1)S(1)} collective-permute-done((bf16[48,128]{1,0:T(8,128)(2,1)S(1)}, bf16[48,128]{1,0:T(8,128)(2,1)S(1)}, u32[]{:S(2)}, u32[]{:S(2)}) %collective-permute-start) | collective-permute-done | bytes 12320 | tf_op jit(solution)/shard_map/ppermute | solution.py:306
  6.5 0.9 pad_maximum_fusion
  7.4 2.0 %collective-permute-start.1 = (bf16[560,128]{1,0:T(8,128)(2,1)S(1)}, bf16[560,128]{1,0:T(8,128)(2,1)S(1)}, u32[]{:S(2)}, u32[]{:S(2)}) collective-permute-start(bf16[560,128]{1,0:T(8,128)(2,1)S(1)} %pad_maximum_fusion), channel_id=1, source_target_pairs={{0,32},{32,0},{64,96},{96,64},{128,160},{160,128},{192,224},{224,1... | collective-permute-start | bytes 430088 | tf_op jit(solution)/shard_map/ppermute | solution.py:306
  9.4 4.3 %collective-permute-start.3 = (bf16[512,128]{1,0:T(8,128)(2,1)}, bf16[512,128]{1,0:T(8,128)(2,1)S(1)}, u32[]{:S(2)}, u32[]{:S(2)}) collective-permute-start(bf16[512,128]{1,0:T(8,128)(2,1)} %k_ref.1), channel_id=1, source_target_pairs={{0,64},{32,96},{64,128},{96,160},{128,192},{160,224},{192,256},{22... | collective-permute-start | bytes 393224 | tf_op jit(solution)/shard_map/ppermute | solution.py:306
  13.7 3.3 %collective-permute-start.2 = (bf16[512,128]{1,0:T(8,128)(2,1)}, bf16[512,128]{1,0:T(8,128)(2,1)S(1)}, u32[]{:S(2)}, u32[]{:S(2)}) collective-permute-start(bf16[512,128]{1,0:T(8,128)(2,1)} %param.9), channel_id=1, source_target_pairs={{0,16},{1,17},{2,18},{3,19},{4,20},{5,21},{6,22},{7,23},{8,24},{9,... | collective-permute-start | bytes 393224 | tf_op jit(solution)/shard_map/ppermute | solution.py:312
  17.1 0.8 reduce-window.4
  17.9 0.0 collective-permute-done.1
  17.9 4.6 %collective-permute-done.2 = bf16[512,128]{1,0:T(8,128)(2,1)S(1)} collective-permute-done((bf16[512,128]{1,0:T(8,128)(2,1)}, bf16[512,128]{1,0:T(8,128)(2,1)S(1)}, u32[]{:S(2)}, u32[]{:S(2)}) %collective-permute-start.2) | collective-permute-done | bytes 131104 | tf_op jit(solution)/shard_map/ppermute | solution.py:312
  22.5 0.9 maximum_maximum_fusion.vh_ref
  23.4 2.3 %collective-permute-start.7 = (bf16[528,256]{1,0:T(8,128)(2,1)S(1)}, bf16[528,256]{1,0:T(8,128)(2,1)S(1)}, u32[]{:S(2)}, u32[]{:S(2)}) collective-permute-start(bf16[528,256]{1,0:T(8,128)(2,1)S(1)} %maximum_maximum_fusion.vh_ref), channel_id=1, source_target_pairs={{0,64},{32,96},{64,128},{96,160},{128,192},{160,224},{192,256},{22... | collective-permute-start | bytes 811016 | tf_op jit(solution)/shard_map/ppermute | solution.py:306
  25.8 0.1 add_add_fusion.4
  25.9 0.1 add_add_fusion.3
  26.0 6.6 %collective-permute-done.7.vh_ref = bf16[528,256]{1,0:T(8,128)(2,1)S(1)} collective-permute-done((bf16[528,256]{1,0:T(8,128)(2,1)S(1)}, bf16[528,256]{1,0:T(8,128)(2,1)S(1)}, u32[]{:S(2)}, u32[]{:S(2)}) %collective-permute-start.7) | collective-permute-done | bytes 270368 | tf_op jit(solution)/shard_map/ppermute | solution.py:306
  32.5 2.8 %collective-permute-start.8 = (bf16[528,256]{1,0:T(8,128)(2,1)S(1)}, bf16[528,256]{1,0:T(8,128)(2,1)S(1)}, u32[]{:S(2)}, u32[]{:S(2)}) collective-permute-start(bf16[528,256]{1,0:T(8,128)(2,1)S(1)} %collective-permute-done.7.vh_ref), channel_id=1, source_target_pairs={{0,64},{32,96},{64,128},{96,160},{128,192},{160,224},{192,256},{22... | collective-permute-start | bytes 811016 | tf_op jit(solution)/shard_map/ppermute | solution.py:306
  35.3 0.1 add_add_fusion.place_ref
  35.4 0.7 reduce
  36.1 0.1 reshape.16.taps_ref
  36.2 0.0 collective-permute-done.3.k_ref
  36.2 3.8 %collective-permute-start.4 = (bf16[512,128]{1,0:T(8,128)(2,1)S(1)}, bf16[512,128]{1,0:T(8,128)(2,1)S(1)}, u32[]{:S(2)}, u32[]{:S(2)}) collective-permute-start(bf16[512,128]{1,0:T(8,128)(2,1)S(1)} %collective-permute-done.3.k_ref), channel_id=1, source_target_pairs={{0,64},{32,96},{64,128},{96,160},{128,192},{160,224},{192,256},{22... | collective-permute-start | bytes 393224 | tf_op jit(solution)/shard_map/ppermute | solution.py:306
  40.0 1.1 %maximum_select_fusion.qx_ref = bf16[1040,128]{1,0:T(8,128)(2,1)S(1)} fusion(bf16[512,128]{1,0:T(8,128)(2,1)S(1)} %slice.53, bf16[512,128]{1,0:T(8,128)(2,1)} %param.7, bf16[16,128]{1,0:T(8,128)(2,1)S(1)} %slice.52, bf16[16,128]{1,0:T(8,128)(2,1)S(1)} %get-tuple-element.45, pred[]{:T(512)S(6)} %eq.5), kind=kLoop, calls=%fused_computation.1 | loop fusion | flops 1730560 | bytes 536577 | tf_op jit(solution)/shard_map/jit(_where)/select_n | solution.py:330
  41.1 2.6 %collective-permute-done.4.k_ref = bf16[512,128]{1,0:T(8,128)(2,1)S(1)} collective-permute-done((bf16[512,128]{1,0:T(8,128)(2,1)S(1)}, bf16[512,128]{1,0:T(8,128)(2,1)S(1)}, u32[]{:S(2)}, u32[]{:S(2)}) %collective-permute-start.4) | collective-permute-done | bytes 131104 | tf_op jit(solution)/shard_map/ppermute | solution.py:306
  43.7 3.2 %collective-permute-start.5 = (bf16[512,128]{1,0:T(8,128)(2,1)S(1)}, bf16[512,128]{1,0:T(8,128)(2,1)S(1)}, u32[]{:S(2)}, u32[]{:S(2)}) collective-permute-start(bf16[512,128]{1,0:T(8,128)(2,1)S(1)} %collective-permute-done.4.k_ref), channel_id=1, source_target_pairs={{0,64},{32,96},{64,128},{96,160},{128,192},{160,224},{192,256},{22... | collective-permute-start | bytes 393224 | tf_op jit(solution)/shard_map/ppermute | solution.py:306
  46.9 0.0 collective-permute-done.8.vh_ref
  46.9 5.4 %collective-permute-start.9 = (bf16[528,256]{1,0:T(8,128)(2,1)S(1)}, bf16[528,256]{1,0:T(8,128)(2,1)S(1)}, u32[]{:S(2)}, u32[]{:S(2)}) collective-permute-start(bf16[528,256]{1,0:T(8,128)(2,1)S(1)} %collective-permute-done.8.vh_ref), channel_id=1, source_target_pairs={{0,64},{32,96},{64,128},{96,160},{128,192},{160,224},{192,256},{22... | collective-permute-start | bytes 811016 | tf_op jit(solution)/shard_map/ppermute | solution.py:306
  52.3 0.0 copy-done
  52.3 12.6 %shard_map.73 = (bf16[1024,768]{1,0:T(8,128)(2,1)S(1)}, bf16[768,256]{1,0:T(8,128)(2,1)S(1)}, bf16[768,256]{1,0:T(8,128)(2,1)S(1)}, f32[1024,128]{1,0:T(8,128)S(...) custom-call(s32[10]{0:T(128)S(1)} %get-tuple-element.49.place_ref, f32[66]{0:T(128)S(1)} %reshape.16.taps_ref, ...), custom_call_target="tpu_custom_call" | custom-call | flops 1879048192 | bytes 4194304 | tf_op jit(solution)/shard_map/pallas_call | solution.py:283
  64.9 0.0 collective-permute-done.5.k_ref
  64.9 1.9 %collective-permute-start.6 = (bf16[512,128]{1,0:T(8,128)(2,1)S(1)}, bf16[512,128]{1,0:T(8,128)(2,1)S(1)}, u32[]{:S(2)}, u32[]{:S(2)}) collective-permute-start(bf16[512,128]{1,0:T(8,128)(2,1)S(1)} %collective-permute-done.5.k_ref), channel_id=1, source_target_pairs={{0,64},{32,96},{64,128},{96,160},{128,192},{160,224},{192,256},{22... | collective-permute-start | bytes 393224 | tf_op jit(solution)/shard_map/ppermute | solution.py:306
  66.8 5.6 %shard_map.74 = (f32[1024,128]{1,0:T(8,128)S(1)}, f32[1024,128]{1,0:T(8,128)S(1)}, f32[1024,256]{1,0:T(8,128)S(1)}) custom-call(s32[10]{0:T(128)S(1)} %get-tuple-element.48.place_ref, f32[66]{0:T(128)S(1)} %reshape.16.taps_ref, bf16[1024,768]{1,0:T(8,128)(2,1)S(1)} %get-tuple-element.24.qp_ref, ...), custom_call_target="tpu_custom_call", output_to_operand_aliasing={{0}: (7, {}), {1}: (8, {}), {2}: (9, {})} | custom-call | flops 1879048192 | bytes 4194304 | tf_op jit(solution)/shard_map/pallas_call | solution.py:283
  72.4 0.0 collective-permute-done.9.vh_ref
  72.4 1.9 %collective-permute-start.10 = (bf16[528,256]{1,0:T(8,128)(2,1)S(1)}, bf16[528,256]{1,0:T(8,128)(2,1)S(1)}, u32[]{:S(2)}, u32[]{:S(2)}) collective-permute-start(bf16[528,256]{1,0:T(8,128)(2,1)S(1)} %collective-permute-done.9.vh_ref), channel_id=1, source_target_pairs={{0,64},{32,96},{64,128},{96,160},{128,192},{160,224},{192,256},{22... | collective-permute-start | bytes 811016 | tf_op jit(solution)/shard_map/ppermute | solution.py:306
  74.3 5.5 %shard_map.75 = (f32[1024,128]{1,0:T(8,128)S(1)}, f32[1024,128]{1,0:T(8,128)S(1)}, f32[1024,256]{1,0:T(8,128)S(1)}) custom-call(s32[10]{0:T(128)S(1)} %get-tuple-element.50.place_ref, f32[66]{0:T(128)S(1)} %reshape.16.taps_ref, bf16[1024,768]{1,0:T(8,128)(2,1)S(1)} %get-tuple-element.24.qp_ref, ...), custom_call_target="tpu_custom_call", output_to_operand_aliasing={{0}: (7, {}), {1}: (8, {}), {2}: (9, {})} | custom-call | flops 1879048192 | bytes 4194304 | tf_op jit(solution)/shard_map/pallas_call | solution.py:283
  79.9 5.5 %shard_map.76 = (f32[1024,128]{1,0:T(8,128)S(1)}, f32[1024,128]{1,0:T(8,128)S(1)}, f32[1024,256]{1,0:T(8,128)S(1)}) custom-call(s32[10]{0:T(128)S(1)} %get-tuple-element.51.place_ref, f32[66]{0:T(128)S(1)} %reshape.16.taps_ref, bf16[1024,768]{1,0:T(8,128)(2,1)S(1)} %get-tuple-element.24.qp_ref, ...), custom_call_target="tpu_custom_call", output_to_operand_aliasing={{0}: (7, {}), {1}: (8, {}), {2}: (9, {})} | custom-call | flops 1879048192 | bytes 4194304 | tf_op jit(solution)/shard_map/pallas_call | solution.py:283
  85.4 0.0 collective-permute-done.6.k_ref
  85.4 0.0 collective-permute-done.10.vh_ref
  85.5 0.8 shard_map.77
  86.3 0.0 copy-start.1
  86.3 0.0 copy-start.2
  86.3 2.0 %collective-permute-start.11 = (f32[512,384]{1,0:T(8,128)S(1)}, f32[512,384]{1,0:T(8,128)S(1)}, u32[]{:S(2)}, u32[]{:S(2)}) collective-permute-start(f32[512,384]{1,0:T(8,128)S(1)} %get-tuple-element.40), channel_id=1, source_target_pairs={{0,32},{32,0},{64,96},{96,64},{128,160},{160,128},{192,224},{224,1... | collective-permute-start | bytes 2359304 | tf_op jit(solution)/shard_map/ppermute | solution.py:306
  88.3 2.2 %collective-permute-done.11.other_ref = f32[512,384]{1,0:T(8,128)S(1)} collective-permute-done((f32[512,384]{1,0:T(8,128)S(1)}, f32[512,384]{1,0:T(8,128)S(1)}, u32[]{:S(2)}, u32[]{:S(2)}) %collective-permute-start.11) | collective-permute-done | bytes 786464 | tf_op jit(solution)/shard_map/ppermute | solution.py:306
  90.5 0.4 shard_map.78
  90.9 3.3 %collective-permute-start.12 = (bf16[512,128]{1,0:T(8,128)(2,1)S(1)}, bf16[512,128]{1,0:T(8,128)(2,1)S(1)}, u32[]{:S(2)}, u32[]{:S(2)}) collective-permute-start(bf16[512,128]{1,0:T(8,128)(2,1)S(1)} %get-tuple-element.42), channel_id=1, source_target_pairs={{0,16},{1,17},{2,18},{3,19},{4,20},{5,21},{6,22},{7,23},{8,24},{9,... | collective-permute-start | bytes 393224 | tf_op jit(solution)/shard_map/ppermute | solution.py:312
  94.2 5.6 %collective-permute-done.12.cross_ref = bf16[512,128]{1,0:T(8,128)(2,1)S(1)} collective-permute-done((bf16[512,128]{1,0:T(8,128)(2,1)S(1)}, bf16[512,128]{1,0:T(8,128)(2,1)S(1)}, u32[]{:S(2)}, u32[]{:S(2)}) %collective-permute-start.12) | collective-permute-done | bytes 131104 | tf_op jit(solution)/shard_map/ppermute | solution.py:312
  99.8 0.0 copy-done.1
  99.8 0.0 copy-done.2
  99.9 1.4 %shard_map.79 = bf16[512,128]{1,0:T(8,128)(2,1)} custom-call(f32[2]{0:T(128)S(1)} %bitcast.12, f32[512,128]{1,0:T(8,128)S(1)} %get-tuple-element.41.own_ref, bf16[512,128]{1,0:T(8,128)(2,1)S(1)} %collective-permute-done.12.cross_ref, f32[1,128]{1,0:T(1,128)S(1)} %bitcast.13), custom_call_target="tpu_custom_call" | custom-call | bytes 4194304 | tf_op jit(solution)/shard_map/pallas_call | solution.py:283
  (5 shorter events, 0.0 us)
Async XLA Ops:
  0.0 52.3 %copy-start = (bf16[512,128]{1,0:T(8,128)(2,1)S(1)}, bf16[512,128]{1,0:T(8,128)(2,1)}, u32[]{:S(2)}) copy-start(bf16[512,128]{1,0:T(8,128)(2,1)} %k_ref.1) | copy-start | bytes 393220
  1.5 5.0 %collective-permute-start = (bf16[48,128]{1,0:T(8,128)(2,1)S(1)}, bf16[48,128]{1,0:T(8,128)(2,1)S(1)}, u32[]{:S(2)}, u32[]{:S(2)}) collective-permute-start(bf16[48,128]{1,0:T(8,128)(2,1)S(1)} %pad_maximum_fusion.1), channel_id=1, source_target_pairs={{32,64},{96,128},{160,192},{224,256},{288,320},{352,384},{416,448}... | collective-permute-start | bytes 36872 | tf_op jit(solution)/shard_map/ppermute | solution.py:306
  7.4 10.5 %collective-permute-start.1 = (bf16[560,128]{1,0:T(8,128)(2,1)S(1)}, bf16[560,128]{1,0:T(8,128)(2,1)S(1)}, u32[]{:S(2)}, u32[]{:S(2)}) collective-permute-start(bf16[560,128]{1,0:T(8,128)(2,1)S(1)} %pad_maximum_fusion), channel_id=1, source_target_pairs={{0,32},{32,0},{64,96},{96,64},{128,160},{160,128},{192,224},{224,1... | collective-permute-start | bytes 430088 | tf_op jit(solution)/shard_map/ppermute | solution.py:306
  9.4 26.8 %collective-permute-start.3 = (bf16[512,128]{1,0:T(8,128)(2,1)}, bf16[512,128]{1,0:T(8,128)(2,1)S(1)}, u32[]{:S(2)}, u32[]{:S(2)}) collective-permute-start(bf16[512,128]{1,0:T(8,128)(2,1)} %k_ref.1), channel_id=1, source_target_pairs={{0,64},{32,96},{64,128},{96,160},{128,192},{160,224},{192,256},{22... | collective-permute-start | bytes 393224 | tf_op jit(solution)/shard_map/ppermute | solution.py:306
  13.7 8.7 %collective-permute-start.2 = (bf16[512,128]{1,0:T(8,128)(2,1)}, bf16[512,128]{1,0:T(8,128)(2,1)S(1)}, u32[]{:S(2)}, u32[]{:S(2)}) collective-permute-start(bf16[512,128]{1,0:T(8,128)(2,1)} %param.9), channel_id=1, source_target_pairs={{0,16},{1,17},{2,18},{3,19},{4,20},{5,21},{6,22},{7,23},{8,24},{9,... | collective-permute-start | bytes 393224 | tf_op jit(solution)/shard_map/ppermute | solution.py:312
  23.4 9.1 %collective-permute-start.7 = (bf16[528,256]{1,0:T(8,128)(2,1)S(1)}, bf16[528,256]{1,0:T(8,128)(2,1)S(1)}, u32[]{:S(2)}, u32[]{:S(2)}) collective-permute-start(bf16[528,256]{1,0:T(8,128)(2,1)S(1)} %maximum_maximum_fusion.vh_ref), channel_id=1, source_target_pairs={{0,64},{32,96},{64,128},{96,160},{128,192},{160,224},{192,256},{22... | collective-permute-start | bytes 811016 | tf_op jit(solution)/shard_map/ppermute | solution.py:306
  32.5 14.3 %collective-permute-start.8 = (bf16[528,256]{1,0:T(8,128)(2,1)S(1)}, bf16[528,256]{1,0:T(8,128)(2,1)S(1)}, u32[]{:S(2)}, u32[]{:S(2)}) collective-permute-start(bf16[528,256]{1,0:T(8,128)(2,1)S(1)} %collective-permute-done.7.vh_ref), channel_id=1, source_target_pairs={{0,64},{32,96},{64,128},{96,160},{128,192},{160,224},{192,256},{22... | collective-permute-start | bytes 811016 | tf_op jit(solution)/shard_map/ppermute | solution.py:306
  36.2 7.5 %collective-permute-start.4 = (bf16[512,128]{1,0:T(8,128)(2,1)S(1)}, bf16[512,128]{1,0:T(8,128)(2,1)S(1)}, u32[]{:S(2)}, u32[]{:S(2)}) collective-permute-start(bf16[512,128]{1,0:T(8,128)(2,1)S(1)} %collective-permute-done.3.k_ref), channel_id=1, source_target_pairs={{0,64},{32,96},{64,128},{96,160},{128,192},{160,224},{192,256},{22... | collective-permute-start | bytes 393224 | tf_op jit(solution)/shard_map/ppermute | solution.py:306
  43.7 21.2 %collective-permute-start.5 = (bf16[512,128]{1,0:T(8,128)(2,1)S(1)}, bf16[512,128]{1,0:T(8,128)(2,1)S(1)}, u32[]{:S(2)}, u32[]{:S(2)}) collective-permute-start(bf16[512,128]{1,0:T(8,128)(2,1)S(1)} %collective-permute-done.4.k_ref), channel_id=1, source_target_pairs={{0,64},{32,96},{64,128},{96,160},{128,192},{160,224},{192,256},{22... | collective-permute-start | bytes 393224 | tf_op jit(solution)/shard_map/ppermute | solution.py:306
  46.9 25.5 %collective-permute-start.9 = (bf16[528,256]{1,0:T(8,128)(2,1)S(1)}, bf16[528,256]{1,0:T(8,128)(2,1)S(1)}, u32[]{:S(2)}, u32[]{:S(2)}) collective-permute-start(bf16[528,256]{1,0:T(8,128)(2,1)S(1)} %collective-permute-done.8.vh_ref), channel_id=1, source_target_pairs={{0,64},{32,96},{64,128},{96,160},{128,192},{160,224},{192,256},{22... | collective-permute-start | bytes 811016 | tf_op jit(solution)/shard_map/ppermute | solution.py:306
  64.9 20.6 %collective-permute-start.6 = (bf16[512,128]{1,0:T(8,128)(2,1)S(1)}, bf16[512,128]{1,0:T(8,128)(2,1)S(1)}, u32[]{:S(2)}, u32[]{:S(2)}) collective-permute-start(bf16[512,128]{1,0:T(8,128)(2,1)S(1)} %collective-permute-done.5.k_ref), channel_id=1, source_target_pairs={{0,64},{32,96},{64,128},{96,160},{128,192},{160,224},{192,256},{22... | collective-permute-start | bytes 393224 | tf_op jit(solution)/shard_map/ppermute | solution.py:306
  72.4 13.1 %collective-permute-start.10 = (bf16[528,256]{1,0:T(8,128)(2,1)S(1)}, bf16[528,256]{1,0:T(8,128)(2,1)S(1)}, u32[]{:S(2)}, u32[]{:S(2)}) collective-permute-start(bf16[528,256]{1,0:T(8,128)(2,1)S(1)} %collective-permute-done.9.vh_ref), channel_id=1, source_target_pairs={{0,64},{32,96},{64,128},{96,160},{128,192},{160,224},{192,256},{22... | collective-permute-start | bytes 811016 | tf_op jit(solution)/shard_map/ppermute | solution.py:306
  86.3 13.6 %copy-start.1 = (f32[1,2]{1,0:T(1,128)S(1)}, f32[1,2]{1,0:T(1,128)}, u32[]{:S(2)}) copy-start(f32[1,2]{1,0:T(1,128)} %param.11) | copy-start | bytes 28
  86.3 13.6 %copy-start.2 = (f32[128]{0:T(128)S(1)}, f32[128]{0:T(128)}, u32[]{:S(2)}) copy-start(f32[128]{0:T(128)} %param.12) | copy-start | bytes 1540
  86.3 4.2 %collective-permute-start.11 = (f32[512,384]{1,0:T(8,128)S(1)}, f32[512,384]{1,0:T(8,128)S(1)}, u32[]{:S(2)}, u32[]{:S(2)}) collective-permute-start(f32[512,384]{1,0:T(8,128)S(1)} %get-tuple-element.40), channel_id=1, source_target_pairs={{0,32},{32,0},{64,96},{96,64},{128,160},{160,128},{192,224},{224,1... | collective-permute-start | bytes 2359304 | tf_op jit(solution)/shard_map/ppermute | solution.py:306
  90.9 8.9 %collective-permute-start.12 = (bf16[512,128]{1,0:T(8,128)(2,1)S(1)}, bf16[512,128]{1,0:T(8,128)(2,1)S(1)}, u32[]{:S(2)}, u32[]{:S(2)}) collective-permute-start(bf16[512,128]{1,0:T(8,128)(2,1)S(1)} %get-tuple-element.42), channel_id=1, source_target_pairs={{0,16},{1,17},{2,18},{3,19},{4,20},{5,21},{6,22},{7,23},{8,24},{9,... | collective-permute-start | bytes 393224 | tf_op jit(solution)/shard_map/ppermute | solution.py:312

commit v2 on v1

v2 whole, which is shorter than its diff:
```python
import functools

import jax
import jax.numpy as jnp
from jax import lax
from jax.experimental import pallas as pl
from jax.experimental.pallas import tpu as pltpu
from jax.sharding import PartitionSpec as P

HEAD_DIM = 128
SCALE = HEAD_DIM ** (-0.5)
MASKED = -1e30
FLOOR = -1e20
HALO = 16
BAND = 64
GROUP = 128
WIDE = 256
REACH = 10
HOPS = 4


def dot(a, b):
    return lax.dot_general(a, b, (((1,), (0,)), ((), ())), preferred_element_type=jnp.float32)


def dot_t(a, b):
    return lax.dot_general(a, b, (((1,), (1,)), ((), ())), preferred_element_type=jnp.float32)


def starts_of(position, ends):
    start = jnp.zeros_like(position)
    for end in ends:
        start = jnp.where(position >= end, end, start)
    return start


def widen(column, times):
    return jnp.concatenate([column] * times, axis=1) if times > 1 else column


def absorb(tiles, state_ref):
    wide = 2 * HEAD_DIM
    done = []
    for rows, logits, values in tiles:
        m_old = state_ref[rows, wide : wide + 128]
        m_new = jnp.maximum(m_old, jnp.max(logits, axis=1, keepdims=True))
        weights = jnp.exp(logits - widen(m_new, logits.shape[1] // 128))
        factor = jnp.exp(m_old - m_new)
        total = state_ref[rows, wide + 128 :] * factor + jnp.sum(weights, axis=1, keepdims=True)
        product = dot(weights.astype(jnp.bfloat16), values)
        product = state_ref[rows, 0:wide] * widen(factor, 2) + product
        done.append((rows, m_new, total, product))
    for rows, m_new, total, product in done:
        state_ref[rows, 0:wide] = product
        state_ref[rows, wide : wide + 128] = m_new
        state_ref[rows, wide + 128 :] = total


def taps_at(qp_ref, rest, u):
    most = qp_ref.shape[1] // 256
    sets = qp_ref.shape[1] // HEAD_DIM // most
    row = qp_ref.shape[0] - (2 - rest) * sets * GROUP + u // most * GROUP
    return slice(row, row + GROUP), slice(u % most * 256, u % most * 256 + 256)


def lay_keys(a_ref, b_ref, kx_ref, vx_ref):
    keys = vx_ref.shape[0] - 2 * HALO
    own = a_ref.shape[0] - keys - 2 * HALO
    kx_ref[0:HALO, :] = a_ref[keys : keys + HALO, :]
    kx_ref[HALO : HALO + keys, :] = a_ref[0:keys, :]
    kx_ref[HALO + keys : 2 * HALO + keys, :] = a_ref[keys + HALO : keys + 2 * HALO, :]
    vx_ref[0:HALO, :] = jnp.zeros((HALO, 2 * HEAD_DIM), jnp.bfloat16)
    vx_ref[HALO : HALO + own, 0:HEAD_DIM] = a_ref[keys + 2 * HALO :, :]
    vx_ref[HALO + own : HALO + keys, 0:HEAD_DIM] = b_ref[0 : keys - own, :]
    vx_ref[HALO : HALO + keys, HEAD_DIM:] = b_ref[keys - own :, :]
    vx_ref[HALO + keys :, :] = jnp.zeros((HALO, 2 * HEAD_DIM), jnp.bfloat16)


def near(a, chip_row, block, ends, taps_ref, qp_ref, kx_ref, vx_ref, state_ref):
    keys = vx_ref.shape[0] - 2 * HALO
    query_taps, key_taps = taps_ref.shape[1:]
    rim = (key_taps - 1) // 2
    low = pl.multiple_of(jnp.clip(a - 32, 0, keys + 2 * HALO - GROUP), 16)
    rows = pl.ds(pl.multiple_of(block - chip_row + a, 16), BAND)
    window = kx_ref[pl.ds(low, GROUP), :]
    shape = (BAND, GROUP)
    row = block + a + lax.broadcasted_iota(jnp.int32, shape, 0)
    col = block - HALO + low + lax.broadcasted_iota(jnp.int32, shape, 1)
    sums = [None] * key_taps
    own_start = None
    for u in range(query_taps):
        scores = dot_t(qp_ref[rows, u * HEAD_DIM : (u + 1) * HEAD_DIM], window)
        start = starts_of(row - u, ends)
        if u == 0:
            own_start = start
        scores = jnp.where((col <= row - u) & (col >= start), scores, 0.0)
        for t in range(key_taps):
            tap = taps_ref[0, u, t] * SCALE
            if u == 0 and t == rim:
                tap = tap + SCALE
            sums[t] = scores * tap if u == 0 else sums[t] + scores * tap
    conv = sums[rim]
    for t in range(key_taps):
        if t != rim:
            conv = conv + pltpu.roll(sums[t], (t - rim) % GROUP, 1)
    inside = (col >= block) & (col < block + keys)
    inside = inside & (col <= row) & (col > row - REACH) & (col >= own_start)
    logits = jnp.where(inside, conv, MASKED)
    absorb([(rows, logits, vx_ref[pl.ds(low, GROUP), :])], state_ref)


def convolve(local, block, first_start, ends, qp_ref, kx_ref, kp_ref):
    total = kx_ref.shape[0]
    keys = kp_ref.shape[0]
    width = kp_ref.shape[1] // 2
    taps = width // HEAD_DIM
    depth = 256
    def put(g, u, done):
        top = done.astype(jnp.bfloat16)
        rest = (done - top.astype(jnp.float32)).astype(jnp.bfloat16)
        for n in range(done.shape[1] // HEAD_DIM):
            here = slice((g + n) * GROUP, (g + n + 1) * GROUP)
            lanes = slice(n * HEAD_DIM, (n + 1) * HEAD_DIM)
            kp_ref[here, u * HEAD_DIM : (u + 1) * HEAD_DIM] = top[:, lanes]
            kp_ref[here, width + u * HEAD_DIM : width + (u + 1) * HEAD_DIM] = rest[:, lanes]

    def whole():
        for g in range(0, keys // GROUP, 2):
            window = jnp.concatenate(
                [kx_ref[n * GROUP : n * GROUP + depth, :] for n in (g, g + 1)], axis=1
            )
            for u in range(taps):
                high, rest = (qp_ref[taps_at(qp_ref, n, u)] for n in (0, 1))
                put(g, u, dot(high, window) + dot(rest, window))

    def cut():
        for g in range(keys // GROUP):
            shape = (GROUP, depth)
            out = block + g * GROUP + lax.broadcasted_iota(jnp.int32, shape, 0)
            inp = block + g * GROUP - HALO + lax.broadcasted_iota(jnp.int32, shape, 1)
            keep = inp >= starts_of(out, ends)
            window = kx_ref[g * GROUP : g * GROUP + depth, :]
            for u in range(taps):
                high, rest = (
                    jnp.where(keep, qp_ref[taps_at(qp_ref, n, u)].astype(jnp.float32), 0.0).astype(
                        jnp.bfloat16
                    )
                    for n in (0, 1)
                )
                put(g, u, dot(high, window) + dot(rest, window))

    if local:
        unbroken = starts_of(block + keys - 1, ends) <= block - HALO

        @pl.when(unbroken)
        def _():
            whole()

        @pl.when(jnp.logical_not(unbroken))
        def _():
            cut()

        return
    place = block - HALO + lax.broadcasted_iota(jnp.int32, (total, HEAD_DIM), 0)
    kx_ref[...] = jnp.where(place >= first_start, kx_ref[...].astype(jnp.float32), 0.0).astype(
        jnp.bfloat16
    )
    whole()


def far(chip_row, block, ends, qp_ref, kp_ref, vx_ref, state_ref):
    keys = kp_ref.shape[0]
    width = qp_ref.shape[1]

    @pl.loop(0, state_ref.shape[0] // (2 * WIDE))
    def _(tile):
        first = tile * 2 * WIDE
        top = chip_row + first
        needed = (top + 2 * WIDE - 1 >= block + REACH) & (block + keys > starts_of(top, ends))

        @pl.when(needed)
        def _():
            tiles = []
            shape = (WIDE, GROUP)
            col = lax.broadcasted_iota(jnp.int32, (WIDE, keys), 1)
            for half in (0, WIDE):
                rows = pl.ds(pl.multiple_of(first + half, WIDE), WIDE)
                query = qp_ref[rows, :]
                conv = dot_t(query, kp_ref[:, 0:width]) + dot_t(query, kp_ref[:, width:])
                row = top + half + lax.broadcasted_iota(jnp.int32, shape, 0)
                start = widen(starts_of(row, ends) - block, keys // GROUP)
                row = widen(row - (REACH + block), keys // GROUP)
                logits = jnp.where((col <= row) & (col >= start), conv, MASKED)
                tiles.append((rows, logits, vx_ref[HALO : HALO + keys, :]))
            absorb(tiles, state_ref)


def ends_of(place_ref):
    ends = [place_ref[2]]
    for d in range(1, 7):
        ends.append(ends[-1] + place_ref[2 + d])
    return ends


def local_kernel(
    place_ref, taps_ref, qx_ref, a_ref, b_ref,
    qp_ref, state_ref, done_ref,
    kx_ref, vx_ref, kp_ref,
):
    chip_row, block = place_ref[0], place_ref[1]
    ends = ends_of(place_ref)
    keys = kp_ref.shape[0]
    taps, key_taps = taps_ref.shape[1:]
    rim = (key_taps - 1) // 2
    queries = qx_ref[...].astype(jnp.float32)
    for u in range(taps):
        shifted = queries if u == 0 else pltpu.roll(queries, u, 0)
        qp_ref[0 : state_ref.shape[0], u * HEAD_DIM : (u + 1) * HEAD_DIM] = shifted[
            HALO:, :
        ].astype(jnp.bfloat16)
    shape = (GROUP, 256)
    ahead = lax.broadcasted_iota(jnp.int32, shape, 1) - lax.broadcasted_iota(jnp.int32, shape, 0)
    for u in range(taps):
        band = jnp.zeros(shape, jnp.float32)
        for t in range(key_taps):
            tap = taps_ref[0, u, t] * SCALE
            if u == 0 and t == rim:
                tap = tap + SCALE
            band = jnp.where(ahead == HALO + rim - t, tap, band)
        high = band.astype(jnp.bfloat16)
        qp_ref[taps_at(qp_ref, 0, u)] = high
        qp_ref[taps_at(qp_ref, 1, u)] = (band - high.astype(jnp.float32)).astype(jnp.bfloat16)
    done_ref[...] = jnp.zeros(done_ref.shape, jnp.float32)
    lane = lax.broadcasted_iota(jnp.int32, state_ref.shape, 1)
    floor = (lane >= 2 * HEAD_DIM) & (lane < 2 * HEAD_DIM + 128)
    state_ref[...] = jnp.where(floor, FLOOR, 0.0)
    kx_ref[...] = jnp.zeros(kx_ref.shape, jnp.bfloat16)
    lay_keys(a_ref, b_ref, kx_ref, vx_ref)

    @pl.loop(0, keys // BAND + 1)
    def _(tile):
        a = tile * BAND

        @pl.when(block - chip_row + a < state_ref.shape[0])
        def _():
            near(
                a, chip_row, block, ends, taps_ref, qp_ref, kx_ref, vx_ref, state_ref
            )

    convolve(True, block, 0, ends, qp_ref, kx_ref, kp_ref)
    far(chip_row, block, ends, qp_ref, kp_ref, vx_ref, state_ref)


def hop_kernel(
    last, place_ref, taps_ref, qp_ref, a_ref, b_ref, state_in, *rest
):
    if last:
        keep_ref, send_ref, kx_ref, vx_ref, kp_ref, state_ref = rest
    else:
        state_ref, done_ref, kx_ref, vx_ref, kp_ref = rest
        done_ref[...] = jnp.zeros(done_ref.shape, jnp.float32)
    chip_row, block = place_ref[0], place_ref[1]
    ends = ends_of(place_ref)
    keys = kp_ref.shape[0]
    first_start = starts_of(chip_row, ends)
    state_ref[...] = state_in[...]

    @pl.when(block + keys > first_start)
    def _():
        kx_ref[...] = jnp.zeros(kx_ref.shape, jnp.bfloat16)
        lay_keys(a_ref, b_ref, kx_ref, vx_ref)

        @pl.when(block + keys == chip_row)
        def _():
            near(
                keys, chip_row, block, ends, taps_ref, qp_ref, kx_ref, vx_ref, state_ref
            )

        convolve(False, block, first_start, ends, qp_ref, kx_ref, kp_ref)
        far(chip_row, block, ends, qp_ref, kp_ref, vx_ref, state_ref)

    if last:
        core = place_ref[9]
        lane = lax.broadcasted_iota(jnp.int32, (keys, 128), 1)
        for ref, side in ((keep_ref, core), (send_ref, 1 - core)):
            rows = pl.ds(pl.multiple_of(side * keys, keys), keys)
            wide = 2 * HEAD_DIM
            ref[:, 0:wide] = state_ref[rows, 0:wide]
            ref[:, wide:] = jnp.where(
                lane < 64, state_ref[rows, wide : wide + 128], state_ref[rows, wide + 128 :]
            )


def join_kernel(keep_ref, other_ref, own_ref, cross_ref):
    wide = 2 * HEAD_DIM
    stats, more = keep_ref[:, wide:], other_ref[:, wide:]
    m_a, l_a = stats[:, 0:1], stats[:, 64:65]
    m_b, l_b = more[:, 0:1], more[:, 64:65]
    m = jnp.maximum(m_a, m_b)
    f_a, f_b = jnp.exp(m_a - m), jnp.exp(m_b - m)
    share = 1.0 / (l_a * f_a + l_b * f_b)
    f_a, f_b = f_a * share, f_b * share
    own_ref[...] = keep_ref[:, :HEAD_DIM] * f_a + other_ref[:, :HEAD_DIM] * f_b
    cross_ref[...] = (
        keep_ref[:, HEAD_DIM:wide] * f_a + other_ref[:, HEAD_DIM:wide] * f_b
    ).astype(jnp.bfloat16)


def finish_kernel(mixing_ref, own_ref, cross_ref, gain_ref, out_ref):
    mixed = mixing_ref[0] * own_ref[...] + mixing_ref[1] * cross_ref[...].astype(jnp.float32)
    mean = jnp.mean(mixed * mixed, axis=1, keepdims=True)
    out_ref[...] = (mixed * lax.rsqrt(mean + 1e-05) * gain_ref[...]).astype(jnp.bfloat16)


VMEM = pl.BlockSpec(memory_space=pltpu.VMEM)
SMEM = pl.BlockSpec(memory_space=pltpu.SMEM)


def call(kernel, specs, out, scratch, args, aliases=None, flops=0):
    shapes = [jax.ShapeDtypeStruct(shape, dtype) for shape, dtype in out]
    return pl.pallas_call(
        kernel,
        out_shape=shapes,
        in_specs=specs,
        out_specs=[VMEM] * len(shapes),
        scratch_shapes=scratch,
        input_output_aliases=aliases or {},
        cost_estimate=pl.CostEstimate(flops=flops, bytes_accessed=4 << 20, transcendentals=0),
        compiler_params=pltpu.CompilerParams(vmem_limit_bytes=20 << 20),
    )(*args)


def body(queries, key_vectors, values, kernel, mixing, norm_gain, doc_lengths):
    rows = queries.shape[0]
    bf16, f32 = jnp.bfloat16, jnp.float32
    count = lax.axis_size("ctx")
    heads = lax.axis_size("head")
    group = lax.axis_index("ctx")
    core = group % 2
    taps = kernel.shape[1]
    width = taps * HEAD_DIM

    def permute(value, pairs):
        return lax.ppermute(value, "ctx", pairs)

    def onward(value):
        return permute(value, [(i, (i + 2) % count) for i in range(count)])

    def partner(value):
        return lax.ppermute(value, "head", [(i, i ^ (heads // 2)) for i in range(heads)])

    def step(value, by):
        return permute(value, [(i, (i + by) % count) for i in range(count)])

    other_values = partner(values)
    beyond = step(key_vectors[:HALO], -1)
    behind = step(jnp.concatenate([key_vectors[rows - HALO :], queries[rows - HALO :]]), 1)
    sibling = permute(
        jnp.concatenate([queries, behind[HALO:]]), [(i, i ^ 1) for i in range(count)]
    )
    query_ext = jnp.where(
        core == 0,
        jnp.concatenate([behind[HALO:], queries, sibling[:rows]]),
        jnp.concatenate([sibling[rows:], sibling[:rows], queries]),
    )
    own = (rows - 2 * HALO) // 2
    ring_a = jnp.concatenate([key_vectors, behind[:HALO], beyond, values[:own]])
    ring_b = jnp.concatenate([values[own:], other_values])
    chip = group // 2

    def place(hop):
        head = jnp.stack([chip * 2 * rows, (chip - hop) * 2 * rows + core * rows])
        return jnp.concatenate([head, doc_lengths[:7], core[None]]).astype(jnp.int32)

    state = [((2 * rows, 2 * HEAD_DIM + 256), f32)]
    mark = [((8, 128), f32)]
    scratch = [
        pltpu.VMEM((rows + 128, HEAD_DIM), bf16),
        pltpu.VMEM((rows + 2 * HALO, 2 * HEAD_DIM), bf16),
        pltpu.VMEM((rows, 2 * width), bf16),
    ]
    flops = 2 * 2 * rows * rows * (2 * width + 2 * HEAD_DIM)
    operand, running, done = call(
        local_kernel,
        [SMEM, SMEM, VMEM, VMEM, VMEM],
        [((2 * rows + 2 * taps * GROUP * 256 // width, width), bf16)]
        + state
        + mark,
        scratch,
        (place(0), kernel, query_ext, ring_a, ring_b),
        flops=flops,
    )
    for hop in range(1, HOPS + 1):
        ring_a, ring_b = onward(ring_a), onward(ring_b)
        ring_a, _ = lax.optimization_barrier((ring_a, done))
        ring_b, _ = lax.optimization_barrier((ring_b, done))
        last = hop == HOPS
        out = [((rows, 3 * HEAD_DIM), f32)] * 2 if last else state + mark
        extra = [pltpu.VMEM(shape, dtype) for shape, dtype in state] if last else []
        result = call(
            functools.partial(hop_kernel, last),
            [SMEM, SMEM] + [VMEM] * 4,
            out,
            scratch + extra,
            (place(hop), kernel, operand, ring_a, ring_b, running),
            aliases=None if last else {5: 0},
            flops=flops,
        )
        if not last:
            running, done = result
    keep, send = result
    other = permute(send, [(i, i ^ 1) for i in range(count)])
    own, cross = call(
        join_kernel,
        [VMEM, VMEM],
        [((rows, HEAD_DIM), f32), ((rows, HEAD_DIM), bf16)],
        [],
        (keep, other),
    )
    (finished,) = call(
        finish_kernel,
        [SMEM, VMEM, VMEM, VMEM],
        [((rows, HEAD_DIM), bf16)],
        [],
        (mixing.reshape(-1), own, partner(cross), norm_gain.reshape(1, HEAD_DIM)),
    )
    return finished


def solution(mesh):
    return jax.shard_map(
        body,
        mesh=mesh,
        in_specs=(
            P("ctx", "head"),
            P("ctx", "head"),
            P("ctx", "head"),
            P("head", None, None),
            P("head", None),
            P("head"),
            P(),
        ),
        out_specs=P("ctx", "head"),
        check_vma=False,
    )
```

time: 102 us -> 95.8 us (0.939)
  the two profiles are of different devices: /device:TPU:430 before, /device:TPU:1 now
where the time goes in v2:
time: 95.8 us; the launch traced here: 95.1 us
  starting transfers between devices  47.8 us (50%)
  Pallas kernels  17.7 us (18%)
  waiting for transfers between devices  15.7 us (16%)
  local copies, waits for them, and re-layouts  9.71 us (10%)
  other arithmetic  3.81 us (4%)
    ppermute x12, starting transfers between devices, permute(): return lax.ppermute(value, 'ctx', pairs)  43.8 us
    pallas_call x7, Pallas kernels, call(): pl.pallas_call(kernel, out_shape=shapes, in_specs=specs, out_specs=[VMEM]...  17.7 us
    ppermute x12, waiting for transfers between devices, permute(): return lax.ppermute(value, 'ctx', pairs)  9.79 us
    unnamed x15, local copies, waits for them, and re-layouts  6.58 us
    ppermute x2, waiting for transfers between devices, partner(): lax.ppermute(value, 'head', [(i, i ^ heads // 2) for i in range(heads)])  5.94 us
    ppermute x2, starting transfers between devices, partner(): lax.ppermute(value, 'head', [(i, i ^ heads // 2) for i in range(heads)])  4.07 us
  transfers between devices with their start and end apart: 14, of which 4 were waited for; matrix products, arithmetic and copies ran while one was open for 7% of the time, Pallas kernels for 16%

profile of v2, /device:TPU:1, one launch (start us, length us, event | category | flops | bytes accessed | tf_op | source)
XLA Modules:
  0.0 95.1 jit_solution(737525686437849793)
XLA Ops:
  0.0 0.7 fusion
  0.7 0.7 slice.38
  1.4 3.5 %collective-permute-start = (bf16[32,128]{1,0:T(8,128)(2,1)S(1)}, bf16[32,128]{1,0:T(8,128)(2,1)S(1)}, u32[]{:S(2)}, u32[]{:S(2)}) collective-permute-start(bf16[32,128]{1,0:T(8,128)(2,1)S(1)} %pad_maximum_fusion.3), channel_id=1, source_target_pairs={{0,32},{32,64},{64,96},{96,128},{128,160},{160,192},{192,224},{224... | collective-permute-start | bytes 24584 | tf_op jit(solution)/shard_map/ppermute | solution.py:344
  4.9 3.4 %collective-permute-start.2 = (bf16[16,128]{1,0:T(8,128)(2,1)S(1)}, bf16[16,128]{1,0:T(8,128)(2,1)S(1)}, u32[]{:S(2)}, u32[]{:S(2)}) collective-permute-start(bf16[16,128]{1,0:T(8,128)(2,1)S(1)} %get-tuple-element.47), channel_id=1, source_target_pairs={{0,480},{32,0},{64,32},{96,64},{128,96},{160,128},{192,160},{224,1... | collective-permute-start | bytes 12296 | tf_op jit(solution)/shard_map/ppermute | solution.py:344
  8.3 1.9 %collective-permute-start.3 = (bf16[512,128]{1,0:T(8,128)(2,1)}, bf16[512,128]{1,0:T(8,128)(2,1)S(1)}, u32[]{:S(2)}, u32[]{:S(2)}) collective-permute-start(bf16[512,128]{1,0:T(8,128)(2,1)} %param.9), channel_id=1, source_target_pairs={{0,16},{1,17},{2,18},{3,19},{4,20},{5,21},{6,22},{7,23},{8,24},{9,... | collective-permute-start | bytes 393224 | tf_op jit(solution)/shard_map/ppermute | solution.py:350
  10.2 0.7 add_add_fusion.4
  11.0 0.8 slice.44
  11.8 0.9 slice.45
  12.7 0.7 copy.15.taps_ref
  13.4 0.0 collective-permute-done
  13.4 0.9 pad_maximum_fusion.2
  14.3 8.0 %collective-permute-start.1 = (bf16[528,128]{1,0:T(8,128)(2,1)S(1)}, bf16[528,128]{1,0:T(8,128)(2,1)S(1)}, u32[]{:S(2)}, u32[]{:S(2)}) collective-permute-start(bf16[528,128]{1,0:T(8,128)(2,1)S(1)} %pad_maximum_fusion.2), channel_id=1, source_target_pairs={{0,32},{32,0},{64,96},{96,64},{128,160},{160,128},{192,224},{224,1... | collective-permute-start | bytes 405512 | tf_op jit(solution)/shard_map/ppermute | solution.py:344
  22.3 0.0 collective-permute-done.2
  22.3 0.9 pad_maximum_fusion.a_ref
  23.3 1.9 %collective-permute-start.4 = (bf16[784,128]{1,0:T(8,128)(2,1)S(1)}, bf16[784,128]{1,0:T(8,128)(2,1)S(1)}, u32[]{:S(2)}, u32[]{:S(2)}) collective-permute-start(bf16[784,128]{1,0:T(8,128)(2,1)S(1)} %pad_maximum_fusion.a_ref), channel_id=1, source_target_pairs={{0,64},{32,96},{64,128},{96,160},{128,192},{160,224},{192,256},{22... | collective-permute-start | bytes 602120 | tf_op jit(solution)/shard_map/ppermute | solution.py:344
  25.2 0.0 collective-permute-done.3
  25.2 1.9 %collective-permute-start.6 = (bf16[784,128]{1,0:T(8,128)(2,1)S(1)}, bf16[784,128]{1,0:T(8,128)(2,1)S(1)}, u32[]{:S(2)}, u32[]{:S(2)}) collective-permute-start(bf16[784,128]{1,0:T(8,128)(2,1)S(1)} %pad_maximum_fusion.1.b_ref), channel_id=1, source_target_pairs={{0,64},{32,96},{64,128},{96,160},{128,192},{160,224},{192,256},{22... | collective-permute-start | bytes 602120 | tf_op jit(solution)/shard_map/ppermute | solution.py:344
  27.2 0.0 collective-permute-done.1
  27.2 1.1 %maximum_select_fusion.qx_ref = bf16[1040,128]{1,0:T(8,128)(2,1)S(1)} fusion(bf16[512,128]{1,0:T(8,128)(2,1)S(1)} %slice.47, bf16[512,128]{1,0:T(8,128)(2,1)} %param.7, bf16[16,128]{1,0:T(8,128)(2,1)S(1)} %get-tuple-element.50, bf16[16,128]{1,0:T(8,128)(2,1)S(1)} %slice.48, pred[]{:T(512)S(6)} %eq.5), kind=kLoop, calls=%fused_computation | loop fusion | flops 1730560 | bytes 536577 | tf_op jit(solution)/shard_map/jit(_where)/select_n | solution.py:361
  28.2 0.0 copy-start.6
  28.3 10.2 %shard_map.73 = (bf16[1536,768]{1,0:T(8,128)(2,1)S(1)}, f32[1024,512]{1,0:T(8,128)S(1)}, f32[8,128]{1,0:T(8,128)}) custom-call(s32[10]{0:T(128)S(1)} %get-tuple-element.52.place_ref, f32[1,6,11]{2,1,0:T(8,128)S(1)} %copy.15.taps_ref, bf16[1040,128]{1,0:T(8,128)(2,1)S(1)} %maximum_select_fusion.qx_ref, bf16[784,128]{1,0:T(8,128)(2,1)S(1)} %pad_maximum_fusion.a_ref, ...), custom_call_target="tpu_custom_call" | custom-call | flops 1879048192 | bytes 4194304 | tf_op jit(solution)/shard_map/pallas_call | solution.py:321
  38.5 0.0 collective-permute-done.4.a_ref
  38.5 2.6 %collective-permute-start.5 = (bf16[784,128]{1,0:T(8,128)(2,1)S(1)}, bf16[784,128]{1,0:T(8,128)(2,1)S(1)}, u32[]{:S(2)}, u32[]{:S(2)}) collective-permute-start(bf16[784,128]{1,0:T(8,128)(2,1)S(1)} %collective-permute-done.4.a_ref), channel_id=1, source_target_pairs={{0,64},{32,96},{64,128},{96,160},{128,192},{160,224},{192,256},{22... | collective-permute-start | bytes 602120 | tf_op jit(solution)/shard_map/ppermute | solution.py:344
  41.1 0.0 collective-permute-done.6.b_ref
  41.1 5.2 %collective-permute-start.8 = (bf16[784,128]{1,0:T(8,128)(2,1)S(1)}, bf16[784,128]{1,0:T(8,128)(2,1)S(1)}, u32[]{:S(2)}, u32[]{:S(2)}) collective-permute-start(bf16[784,128]{1,0:T(8,128)(2,1)S(1)} %collective-permute-done.6.b_ref), channel_id=1, source_target_pairs={{0,64},{32,96},{64,128},{96,160},{128,192},{160,224},{192,256},{22... | collective-permute-start | bytes 602120 | tf_op jit(solution)/shard_map/ppermute | solution.py:344
  46.4 0.0 copy-done.6
  46.4 0.1 add_add_fusion.3
  46.4 1.5 %shard_map.74 = (f32[1024,512]{1,0:T(8,128)S(1)}, f32[8,128]{1,0:T(8,128)}) custom-call(s32[10]{0:T(128)S(1)} %get-tuple-element.54.place_ref, f32[1,6,11]{2,1,0:T(8,128)S(1)} %copy.15.taps_ref, bf16[1536,768]{1,0:T(8,128)(2,1)S(1)} %get-tuple-element.26.qp_ref, bf16[784,128]{1,0:T(8,128)(2,1)S(1)} %collective-permute-done.4.a_ref, ...), custom_call_target="tpu_custom_call", output_to_operand_aliasing={{0}: (5, {})} | custom-call | flops 1879048192 | bytes 4194304 | tf_op jit(solution)/shard_map/pallas_call | solution.py:321
  48.0 0.0 copy-start.2
  48.0 1.4 %copy-done.2 = f32[1024,512]{1,0:T(8,128)} copy-done((f32[1024,512]{1,0:T(8,128)}, f32[1024,512]{1,0:T(8,128)S(1)}, u32[]{:S(2)}) %copy-start.2) | copy-done | bytes 2097176
  49.3 0.0 collective-permute-done.5.a_ref
  49.3 6.5 %collective-permute-start.7 = (bf16[784,128]{1,0:T(8,128)(2,1)S(1)}, bf16[784,128]{1,0:T(8,128)(2,1)S(1)}, u32[]{:S(2)}, u32[]{:S(2)}) collective-permute-start(bf16[784,128]{1,0:T(8,128)(2,1)S(1)} %collective-permute-done.5.a_ref), channel_id=1, source_target_pairs={{0,64},{32,96},{64,128},{96,160},{128,192},{160,224},{192,256},{22... | collective-permute-start | bytes 602120 | tf_op jit(solution)/shard_map/ppermute | solution.py:344
  55.9 0.0 collective-permute-done.8.b_ref
  55.9 2.7 %collective-permute-start.10 = (bf16[784,128]{1,0:T(8,128)(2,1)S(1)}, bf16[784,128]{1,0:T(8,128)(2,1)S(1)}, u32[]{:S(2)}, u32[]{:S(2)}) collective-permute-start(bf16[784,128]{1,0:T(8,128)(2,1)S(1)} %collective-permute-done.8.b_ref), channel_id=1, source_target_pairs={{0,64},{32,96},{64,128},{96,160},{128,192},{160,224},{192,256},{22... | collective-permute-start | bytes 602120 | tf_op jit(solution)/shard_map/ppermute | solution.py:344
  58.6 0.0 copy-start.3
  58.6 1.6 %copy-done.3 = f32[1024,512]{1,0:T(8,128)S(1)} copy-done((f32[1024,512]{1,0:T(8,128)S(1)}, f32[1024,512]{1,0:T(8,128)}, u32[]{:S(2)}) %copy-start.3) | copy-done | bytes 2097176
  60.2 1.5 %shard_map.75 = (f32[1024,512]{1,0:T(8,128)S(1)}, f32[8,128]{1,0:T(8,128)}) custom-call(s32[10]{0:T(128)S(1)} %get-tuple-element.53.place_ref, f32[1,6,11]{2,1,0:T(8,128)S(1)} %copy.15.taps_ref, bf16[1536,768]{1,0:T(8,128)(2,1)S(1)} %get-tuple-element.26.qp_ref, bf16[784,128]{1,0:T(8,128)(2,1)S(1)} %collective-permute-done.5.a_ref, ...), custom_call_target="tpu_custom_call", output_to_operand_aliasing={{0}: (5, {})} | custom-call | flops 1879048192 | bytes 4194304 | tf_op jit(solution)/shard_map/pallas_call | solution.py:321
  61.7 0.0 copy-start.4
  61.7 1.4 %copy-done.4 = f32[1024,512]{1,0:T(8,128)} copy-done((f32[1024,512]{1,0:T(8,128)}, f32[1024,512]{1,0:T(8,128)S(1)}, u32[]{:S(2)}) %copy-start.4) | copy-done | bytes 2097176
  63.1 0.0 collective-permute-done.7.a_ref
  63.1 3.1 %collective-permute-start.9 = (bf16[784,128]{1,0:T(8,128)(2,1)S(1)}, bf16[784,128]{1,0:T(8,128)(2,1)S(1)}, u32[]{:S(2)}, u32[]{:S(2)}) collective-permute-start(bf16[784,128]{1,0:T(8,128)(2,1)S(1)} %collective-permute-done.7.a_ref), channel_id=1, source_target_pairs={{0,64},{32,96},{64,128},{96,160},{128,192},{160,224},{192,256},{22... | collective-permute-start | bytes 602120 | tf_op jit(solution)/shard_map/ppermute | solution.py:344
  66.2 0.0 collective-permute-done.10.b_ref
  66.2 2.6 %collective-permute-start.11 = (bf16[784,128]{1,0:T(8,128)(2,1)S(1)}, bf16[784,128]{1,0:T(8,128)(2,1)S(1)}, u32[]{:S(2)}, u32[]{:S(2)}) collective-permute-start(bf16[784,128]{1,0:T(8,128)(2,1)S(1)} %collective-permute-done.10.b_ref), channel_id=1, source_target_pairs={{0,64},{32,96},{64,128},{96,160},{128,192},{160,224},{192,256},{22... | collective-permute-start | bytes 602120 | tf_op jit(solution)/shard_map/ppermute | solution.py:344
  68.8 0.1 add_add_fusion.place_ref
  68.8 0.0 copy-start.5
  68.8 1.6 %copy-done.5 = f32[1024,512]{1,0:T(8,128)S(1)} copy-done((f32[1024,512]{1,0:T(8,128)S(1)}, f32[1024,512]{1,0:T(8,128)}, u32[]{:S(2)}) %copy-start.5) | copy-done | bytes 2097176
  70.4 1.8 %shard_map.76 = (f32[1024,512]{1,0:T(8,128)S(1)}, f32[8,128]{1,0:T(8,128)}) custom-call(s32[10]{0:T(128)S(1)} %get-tuple-element.51.place_ref, f32[1,6,11]{2,1,0:T(8,128)S(1)} %copy.15.taps_ref, bf16[1536,768]{1,0:T(8,128)(2,1)S(1)} %get-tuple-element.26.qp_ref, bf16[784,128]{1,0:T(8,128)(2,1)S(1)} %collective-permute-done.7.a_ref, ...), custom_call_target="tpu_custom_call", output_to_operand_aliasing={{0}: (5, {})} | custom-call | flops 1879048192 | bytes 4194304 | tf_op jit(solution)/shard_map/pallas_call | solution.py:321
  72.2 4.1 %collective-permute-done.9.a_ref = bf16[784,128]{1,0:T(8,128)(2,1)S(1)} collective-permute-done((bf16[784,128]{1,0:T(8,128)(2,1)S(1)}, bf16[784,128]{1,0:T(8,128)(2,1)S(1)}, u32[]{:S(2)}, u32[]{:S(2)}) %collective-permute-start.9) | collective-permute-done | bytes 200736 | tf_op jit(solution)/shard_map/ppermute | solution.py:344
  76.3 3.7 %collective-permute-done.11.b_ref = bf16[784,128]{1,0:T(8,128)(2,1)S(1)} collective-permute-done((bf16[784,128]{1,0:T(8,128)(2,1)S(1)}, bf16[784,128]{1,0:T(8,128)(2,1)S(1)}, u32[]{:S(2)}, u32[]{:S(2)}) %collective-permute-start.11) | collective-permute-done | bytes 200736 | tf_op jit(solution)/shard_map/ppermute | solution.py:344
  80.1 0.0 copy-start
  80.1 0.0 copy-start.1
  80.1 0.9 shard_map.77
  81.0 2.3 %collective-permute-start.12 = (f32[512,384]{1,0:T(8,128)S(1)}, f32[512,384]{1,0:T(8,128)S(1)}, u32[]{:S(2)}, u32[]{:S(2)}) collective-permute-start(f32[512,384]{1,0:T(8,128)S(1)} %get-tuple-element.44), channel_id=1, source_target_pairs={{0,32},{32,0},{64,96},{96,64},{128,160},{160,128},{192,224},{224,1... | collective-permute-start | bytes 2359304 | tf_op jit(solution)/shard_map/ppermute | solution.py:344
  83.3 1.9 %collective-permute-done.12.other_ref = f32[512,384]{1,0:T(8,128)S(1)} collective-permute-done((f32[512,384]{1,0:T(8,128)S(1)}, f32[512,384]{1,0:T(8,128)S(1)}, u32[]{:S(2)}, u32[]{:S(2)}) %collective-permute-start.12) | collective-permute-done | bytes 786464 | tf_op jit(solution)/shard_map/ppermute | solution.py:344
  85.2 0.4 shard_map.78
  85.6 2.2 %collective-permute-start.13 = (bf16[512,128]{1,0:T(8,128)(2,1)S(1)}, bf16[512,128]{1,0:T(8,128)(2,1)S(1)}, u32[]{:S(2)}, u32[]{:S(2)}) collective-permute-start(bf16[512,128]{1,0:T(8,128)(2,1)S(1)} %get-tuple-element.46), channel_id=1, source_target_pairs={{0,16},{1,17},{2,18},{3,19},{4,20},{5,21},{6,22},{7,23},{8,24},{9,... | collective-permute-start | bytes 393224 | tf_op jit(solution)/shard_map/ppermute | solution.py:350
  87.8 5.9 %collective-permute-done.13.cross_ref = bf16[512,128]{1,0:T(8,128)(2,1)S(1)} collective-permute-done((bf16[512,128]{1,0:T(8,128)(2,1)S(1)}, bf16[512,128]{1,0:T(8,128)(2,1)S(1)}, u32[]{:S(2)}, u32[]{:S(2)}) %collective-permute-start.13) | collective-permute-done | bytes 131104 | tf_op jit(solution)/shard_map/ppermute | solution.py:350
  93.7 0.0 copy-done
  93.7 0.0 copy-done.1
  93.7 1.4 %shard_map.79 = bf16[512,128]{1,0:T(8,128)(2,1)} custom-call(f32[2]{0:T(128)S(1)} %bitcast.10, f32[512,128]{1,0:T(8,128)S(1)} %get-tuple-element.45.own_ref, bf16[512,128]{1,0:T(8,128)(2,1)S(1)} %collective-permute-done.13.cross_ref, f32[1,128]{1,0:T(1,128)S(1)} %bitcast.11), custom_call_target="tpu_custom_call" | custom-call | bytes 4194304 | tf_op jit(solution)/shard_map/pallas_call | solution.py:321
  (5 shorter events, 0.0 us)
Async XLA Ops:
  1.4 12.0 %collective-permute-start = (bf16[32,128]{1,0:T(8,128)(2,1)S(1)}, bf16[32,128]{1,0:T(8,128)(2,1)S(1)}, u32[]{:S(2)}, u32[]{:S(2)}) collective-permute-start(bf16[32,128]{1,0:T(8,128)(2,1)S(1)} %pad_maximum_fusion.3), channel_id=1, source_target_pairs={{0,32},{32,64},{64,96},{96,128},{128,160},{160,192},{192,224},{224... | collective-permute-start | bytes 24584 | tf_op jit(solution)/shard_map/ppermute | solution.py:344
  4.9 17.4 %collective-permute-start.2 = (bf16[16,128]{1,0:T(8,128)(2,1)S(1)}, bf16[16,128]{1,0:T(8,128)(2,1)S(1)}, u32[]{:S(2)}, u32[]{:S(2)}) collective-permute-start(bf16[16,128]{1,0:T(8,128)(2,1)S(1)} %get-tuple-element.47), channel_id=1, source_target_pairs={{0,480},{32,0},{64,32},{96,64},{128,96},{160,128},{192,160},{224,1... | collective-permute-start | bytes 12296 | tf_op jit(solution)/shard_map/ppermute | solution.py:344
  8.3 16.9 %collective-permute-start.3 = (bf16[512,128]{1,0:T(8,128)(2,1)}, bf16[512,128]{1,0:T(8,128)(2,1)S(1)}, u32[]{:S(2)}, u32[]{:S(2)}) collective-permute-start(bf16[512,128]{1,0:T(8,128)(2,1)} %param.9), channel_id=1, source_target_pairs={{0,16},{1,17},{2,18},{3,19},{4,20},{5,21},{6,22},{7,23},{8,24},{9,... | collective-permute-start | bytes 393224 | tf_op jit(solution)/shard_map/ppermute | solution.py:350
  14.3 12.9 %collective-permute-start.1 = (bf16[528,128]{1,0:T(8,128)(2,1)S(1)}, bf16[528,128]{1,0:T(8,128)(2,1)S(1)}, u32[]{:S(2)}, u32[]{:S(2)}) collective-permute-start(bf16[528,128]{1,0:T(8,128)(2,1)S(1)} %pad_maximum_fusion.2), channel_id=1, source_target_pairs={{0,32},{32,0},{64,96},{96,64},{128,160},{160,128},{192,224},{224,1... | collective-permute-start | bytes 405512 | tf_op jit(solution)/shard_map/ppermute | solution.py:344
  23.3 15.2 %collective-permute-start.4 = (bf16[784,128]{1,0:T(8,128)(2,1)S(1)}, bf16[784,128]{1,0:T(8,128)(2,1)S(1)}, u32[]{:S(2)}, u32[]{:S(2)}) collective-permute-start(bf16[784,128]{1,0:T(8,128)(2,1)S(1)} %pad_maximum_fusion.a_ref), channel_id=1, source_target_pairs={{0,64},{32,96},{64,128},{96,160},{128,192},{160,224},{192,256},{22... | collective-permute-start | bytes 602120 | tf_op jit(solution)/shard_map/ppermute | solution.py:344
  25.2 15.9 %collective-permute-start.6 = (bf16[784,128]{1,0:T(8,128)(2,1)S(1)}, bf16[784,128]{1,0:T(8,128)(2,1)S(1)}, u32[]{:S(2)}, u32[]{:S(2)}) collective-permute-start(bf16[784,128]{1,0:T(8,128)(2,1)S(1)} %pad_maximum_fusion.1.b_ref), channel_id=1, source_target_pairs={{0,64},{32,96},{64,128},{96,160},{128,192},{160,224},{192,256},{22... | collective-permute-start | bytes 602120 | tf_op jit(solution)/shard_map/ppermute | solution.py:344
  28.2 18.1 %copy-start.6 = (s32[8]{0:T(128)S(1)}, s32[8]{0:T(128)}, u32[]{:S(2)}) copy-start(s32[8]{0:T(128)} %param.13) | copy-start | bytes 100
  38.5 10.8 %collective-permute-start.5 = (bf16[784,128]{1,0:T(8,128)(2,1)S(1)}, bf16[784,128]{1,0:T(8,128)(2,1)S(1)}, u32[]{:S(2)}, u32[]{:S(2)}) collective-permute-start(bf16[784,128]{1,0:T(8,128)(2,1)S(1)} %collective-permute-done.4.a_ref), channel_id=1, source_target_pairs={{0,64},{32,96},{64,128},{96,160},{128,192},{160,224},{192,256},{22... | collective-permute-start | bytes 602120 | tf_op jit(solution)/shard_map/ppermute | solution.py:344
  41.1 14.8 %collective-permute-start.8 = (bf16[784,128]{1,0:T(8,128)(2,1)S(1)}, bf16[784,128]{1,0:T(8,128)(2,1)S(1)}, u32[]{:S(2)}, u32[]{:S(2)}) collective-permute-start(bf16[784,128]{1,0:T(8,128)(2,1)S(1)} %collective-permute-done.6.b_ref), channel_id=1, source_target_pairs={{0,64},{32,96},{64,128},{96,160},{128,192},{160,224},{192,256},{22... | collective-permute-start | bytes 602120 | tf_op jit(solution)/shard_map/ppermute | solution.py:344
  48.0 1.4 %copy-start.2 = (f32[1024,512]{1,0:T(8,128)}, f32[1024,512]{1,0:T(8,128)S(1)}, u32[]{:S(2)}) copy-start(f32[1024,512]{1,0:T(8,128)S(1)} %get-tuple-element.34.state_in) | copy-start | bytes 6291460
  49.3 13.7 %collective-permute-start.7 = (bf16[784,128]{1,0:T(8,128)(2,1)S(1)}, bf16[784,128]{1,0:T(8,128)(2,1)S(1)}, u32[]{:S(2)}, u32[]{:S(2)}) collective-permute-start(bf16[784,128]{1,0:T(8,128)(2,1)S(1)} %collective-permute-done.5.a_ref), channel_id=1, source_target_pairs={{0,64},{32,96},{64,128},{96,160},{128,192},{160,224},{192,256},{22... | collective-permute-start | bytes 602120 | tf_op jit(solution)/shard_map/ppermute | solution.py:344
  55.9 10.3 %collective-permute-start.10 = (bf16[784,128]{1,0:T(8,128)(2,1)S(1)}, bf16[784,128]{1,0:T(8,128)(2,1)S(1)}, u32[]{:S(2)}, u32[]{:S(2)}) collective-permute-start(bf16[784,128]{1,0:T(8,128)(2,1)S(1)} %collective-permute-done.8.b_ref), channel_id=1, source_target_pairs={{0,64},{32,96},{64,128},{96,160},{128,192},{160,224},{192,256},{22... | collective-permute-start | bytes 602120 | tf_op jit(solution)/shard_map/ppermute | solution.py:344
  58.6 1.6 %copy-start.3 = (f32[1024,512]{1,0:T(8,128)S(1)}, f32[1024,512]{1,0:T(8,128)}, u32[]{:S(2)}) copy-start(f32[1024,512]{1,0:T(8,128)} %copy-done.2) | copy-start | bytes 6291460
  61.7 1.4 %copy-start.4 = (f32[1024,512]{1,0:T(8,128)}, f32[1024,512]{1,0:T(8,128)S(1)}, u32[]{:S(2)}) copy-start(f32[1024,512]{1,0:T(8,128)S(1)} %get-tuple-element.38.state_in) | copy-start | bytes 6291460
  63.1 13.3 %collective-permute-start.9 = (bf16[784,128]{1,0:T(8,128)(2,1)S(1)}, bf16[784,128]{1,0:T(8,128)(2,1)S(1)}, u32[]{:S(2)}, u32[]{:S(2)}) collective-permute-start(bf16[784,128]{1,0:T(8,128)(2,1)S(1)} %collective-permute-done.7.a_ref), channel_id=1, source_target_pairs={{0,64},{32,96},{64,128},{96,160},{128,192},{160,224},{192,256},{22... | collective-permute-start | bytes 602120 | tf_op jit(solution)/shard_map/ppermute | solution.py:344
  66.2 13.9 %collective-permute-start.11 = (bf16[784,128]{1,0:T(8,128)(2,1)S(1)}, bf16[784,128]{1,0:T(8,128)(2,1)S(1)}, u32[]{:S(2)}, u32[]{:S(2)}) collective-permute-start(bf16[784,128]{1,0:T(8,128)(2,1)S(1)} %collective-permute-done.10.b_ref), channel_id=1, source_target_pairs={{0,64},{32,96},{64,128},{96,160},{128,192},{160,224},{192,256},{22... | collective-permute-start | bytes 602120 | tf_op jit(solution)/shard_map/ppermute | solution.py:344
  68.8 1.6 %copy-start.5 = (f32[1024,512]{1,0:T(8,128)S(1)}, f32[1024,512]{1,0:T(8,128)}, u32[]{:S(2)}) copy-start(f32[1024,512]{1,0:T(8,128)} %copy-done.4) | copy-start | bytes 6291460
  80.1 13.6 %copy-start = (f32[1,2]{1,0:T(1,128)S(1)}, f32[1,2]{1,0:T(1,128)}, u32[]{:S(2)}) copy-start(f32[1,2]{1,0:T(1,128)} %param.11) | copy-start | bytes 28
  80.1 13.6 %copy-start.1 = (f32[128]{0:T(128)S(1)}, f32[128]{0:T(128)}, u32[]{:S(2)}) copy-start(f32[128]{0:T(128)} %param.12) | copy-start | bytes 1540
  81.0 4.2 %collective-permute-start.12 = (f32[512,384]{1,0:T(8,128)S(1)}, f32[512,384]{1,0:T(8,128)S(1)}, u32[]{:S(2)}, u32[]{:S(2)}) collective-permute-start(f32[512,384]{1,0:T(8,128)S(1)} %get-tuple-element.44), channel_id=1, source_target_pairs={{0,32},{32,0},{64,96},{96,64},{128,160},{160,128},{192,224},{224,1... | collective-permute-start | bytes 2359304 | tf_op jit(solution)/shard_map/ppermute | solution.py:344
  85.6 8.1 %collective-permute-start.13 = (bf16[512,128]{1,0:T(8,128)(2,1)S(1)}, bf16[512,128]{1,0:T(8,128)(2,1)S(1)}, u32[]{:S(2)}, u32[]{:S(2)}) collective-permute-start(bf16[512,128]{1,0:T(8,128)(2,1)S(1)} %get-tuple-element.46), channel_id=1, source_target_pairs={{0,16},{1,17},{2,18},{3,19},{4,20},{5,21},{6,22},{7,23},{8,24},{9,... | collective-permute-start | bytes 393224 | tf_op jit(solution)/shard_map/ppermute | solution.py:350

commit v3 on v2

--- a/solution.py
+++ b/solution.py
@@ -38,22 +38,23 @@
     return jnp.concatenate([column] * times, axis=1) if times > 1 else column
 
 
-def absorb(tiles, state_ref):
+def absorb(tiles, source_ref, state_ref):
     wide = 2 * HEAD_DIM
     done = []
     for rows, logits, values in tiles:
-        m_old = state_ref[rows, wide : wide + 128]
+        m_old = source_ref[rows, wide : wide + 1]
         m_new = jnp.maximum(m_old, jnp.max(logits, axis=1, keepdims=True))
-        weights = jnp.exp(logits - widen(m_new, logits.shape[1] // 128))
+        weights = jnp.exp(logits - m_new)
         factor = jnp.exp(m_old - m_new)
-        total = state_ref[rows, wide + 128 :] * factor + jnp.sum(weights, axis=1, keepdims=True)
+        total = source_ref[rows, wide + 64 : wide + 65] * factor
+        total = total + jnp.sum(weights, axis=1, keepdims=True)
         product = dot(weights.astype(jnp.bfloat16), values)
-        product = state_ref[rows, 0:wide] * widen(factor, 2) + product
-        done.append((rows, m_new, total, product))
-    for rows, m_new, total, product in done:
+        product = source_ref[rows, 0:wide] * factor + product
+        lane = lax.broadcasted_iota(jnp.int32, (logits.shape[0], 128), 1)
+        done.append((rows, jnp.where(lane < 64, m_new, total), product))
+    for rows, stats, product in done:
         state_ref[rows, 0:wide] = product
-        state_ref[rows, wide : wide + 128] = m_new
-        state_ref[rows, wide + 128 :] = total
+        state_ref[rows, wide:] = stats
 
 
 def taps_at(qp_ref, rest, u):
@@ -64,19 +65,18 @@
 
 
 def lay_keys(a_ref, b_ref, kx_ref, vx_ref):
-    keys = vx_ref.shape[0] - 2 * HALO
-    own = a_ref.shape[0] - keys - 2 * HALO
+    keys = b_ref.shape[0] // 2
     kx_ref[0:HALO, :] = a_ref[keys : keys + HALO, :]
     kx_ref[HALO : HALO + keys, :] = a_ref[0:keys, :]
     kx_ref[HALO + keys : 2 * HALO + keys, :] = a_ref[keys + HALO : keys + 2 * HALO, :]
+    kx_ref[2 * HALO + keys :, :] = jnp.zeros_like(kx_ref[2 * HALO + keys :, :])
     vx_ref[0:HALO, :] = jnp.zeros((HALO, 2 * HEAD_DIM), jnp.bfloat16)
-    vx_ref[HALO : HALO + own, 0:HEAD_DIM] = a_ref[keys + 2 * HALO :, :]
-    vx_ref[HALO + own : HALO + keys, 0:HEAD_DIM] = b_ref[0 : keys - own, :]
-    vx_ref[HALO : HALO + keys, HEAD_DIM:] = b_ref[keys - own :, :]
+    vx_ref[HALO : HALO + keys, 0:HEAD_DIM] = b_ref[0:keys, :]
+    vx_ref[HALO : HALO + keys, HEAD_DIM:] = b_ref[keys:, :]
     vx_ref[HALO + keys :, :] = jnp.zeros((HALO, 2 * HEAD_DIM), jnp.bfloat16)
 
 
-def near(a, chip_row, block, ends, taps_ref, qp_ref, kx_ref, vx_ref, state_ref):
+def near(a, chip_row, block, ends, taps_ref, qp_ref, kx_ref, vx_ref, start_ref, state_ref):
     keys = vx_ref.shape[0] - 2 * HALO
     query_taps, key_taps = taps_ref.shape[1:]
     rim = (key_taps - 1) // 2
@@ -84,29 +84,44 @@
     rows = pl.ds(pl.multiple_of(block - chip_row + a, 16), BAND)
     window = kx_ref[pl.ds(low, GROUP), :]
     shape = (BAND, GROUP)
-    row = block + a + lax.broadcasted_iota(jnp.int32, shape, 0)
+    top = block + a
+    one_start = starts_of(top + BAND - 1, ends)
+    one = starts_of(top - 8, ends) == one_start
+
+    @pl.when(one)
+    def _():
+        start_ref[...] = jnp.full(start_ref.shape, one_start, jnp.int32)
+
+    @pl.when(jnp.logical_not(one))
+    def _():
+        position = top - 8 + lax.broadcasted_iota(jnp.int32, start_ref.shape, 0)
+        start_ref[...] = starts_of(position, ends)
+
+    row = top + lax.broadcasted_iota(jnp.int32, shape, 0)
     col = block - HALO + low + lax.broadcasted_iota(jnp.int32, shape, 1)
-    sums = [None] * key_taps
-    own_start = None
+    behind = row - col
+    stacked = jnp.concatenate(
+        [qp_ref[rows, u * HEAD_DIM : (u + 1) * HEAD_DIM] for u in range(query_taps)], axis=0
+    )
+    products = dot_t(stacked, window)
+    scores = []
     for u in range(query_taps):
-        scores = dot_t(qp_ref[rows, u * HEAD_DIM : (u + 1) * HEAD_DIM], window)
-        start = starts_of(row - u, ends)
-        if u == 0:
-            own_start = start
-        scores = jnp.where((col <= row - u) & (col >= start), scores, 0.0)
-        for t in range(key_taps):
+        allowed = (behind >= u) & (col >= start_ref[8 - u : 8 - u + BAND, :])
+        scores.append(jnp.where(allowed, products[u * BAND : (u + 1) * BAND, :], 0.0))
+    conv = None
+    for t in range(key_taps):
+        terms = None
+        for u in range(query_taps):
             tap = taps_ref[0, u, t] * SCALE
             if u == 0 and t == rim:
                 tap = tap + SCALE
-            sums[t] = scores * tap if u == 0 else sums[t] + scores * tap
-    conv = sums[rim]
-    for t in range(key_taps):
+            terms = scores[u] * tap if terms is None else terms + scores[u] * tap
         if t != rim:
-            conv = conv + pltpu.roll(sums[t], (t - rim) % GROUP, 1)
-    inside = (col >= block) & (col < block + keys)
-    inside = inside & (col <= row) & (col > row - REACH) & (col >= own_start)
-    logits = jnp.where(inside, conv, MASKED)
-    absorb([(rows, logits, vx_ref[pl.ds(low, GROUP), :])], state_ref)
+            terms = pltpu.roll(terms, (t - rim) % GROUP, 1)
+        conv = terms if conv is None else conv + terms
+    inside = (col >= block) & (col < block + keys) & (col >= start_ref[8 : 8 + BAND, :])
+    logits = jnp.where(inside & (behind >= 0) & (behind < REACH), conv, MASKED)
+    absorb([(rows, logits, vx_ref[pl.ds(low, GROUP), :])], state_ref, state_ref)
 
 
 def convolve(local, block, first_start, ends, qp_ref, kx_ref, kp_ref):
@@ -168,7 +183,7 @@
     whole()
 
 
-def far(chip_row, block, ends, qp_ref, kp_ref, vx_ref, state_ref):
+def far(chip_row, block, ends, qp_ref, kp_ref, vx_ref, source_ref, state_ref):
     keys = kp_ref.shape[0]
     width = qp_ref.shape[1]
 
@@ -192,7 +207,14 @@
                 row = widen(row - (REACH + block), keys // GROUP)
                 logits = jnp.where((col <= row) & (col >= start), conv, MASKED)
                 tiles.append((rows, logits, vx_ref[HALO : HALO + keys, :]))
-            absorb(tiles, state_ref)
+            absorb(tiles, source_ref, state_ref)
+
+        if source_ref is not state_ref:
+
+            @pl.when(jnp.logical_not(needed))
+            def _():
+                rows = pl.ds(pl.multiple_of(first, WIDE), 2 * WIDE)
+                state_ref[rows, :] = source_ref[rows, :]
 
 
 def ends_of(place_ref):
@@ -203,92 +225,104 @@
 
 
 def local_kernel(
-    place_ref, taps_ref, qx_ref, a_ref, b_ref,
+    place_ref, taps_ref, own_ref, other_ref, edge_ref, a_ref, b_ref,
     qp_ref, state_ref, done_ref,
-    kx_ref, vx_ref, kp_ref,
+    qx_ref, start_ref, kx_ref, vx_ref, kp_ref,
 ):
     chip_row, block = place_ref[0], place_ref[1]
+    core = place_ref[9]
     ends = ends_of(place_ref)
     keys = kp_ref.shape[0]
     taps, key_taps = taps_ref.shape[1:]
     rim = (key_taps - 1) // 2
-    queries = qx_ref[...].astype(jnp.float32)
+    done_ref[...] = jnp.zeros(done_ref.shape, jnp.float32)
+
+    @pl.when(core == 0)
+    def _():
+        qx_ref[0:HALO, :] = edge_ref[HALO:, :].astype(jnp.float32)
+        qx_ref[HALO : HALO + keys, :] = own_ref[...].astype(jnp.float32)
+        qx_ref[HALO + keys :, :] = other_ref[0:keys, :].astype(jnp.float32)
+
+    @pl.when(core != 0)
+    def _():
+        qx_ref[0:HALO, :] = other_ref[keys:, :].astype(jnp.float32)
+        qx_ref[HALO : HALO + keys, :] = other_ref[0:keys, :].astype(jnp.float32)
+        qx_ref[HALO + keys :, :] = own_ref[...].astype(jnp.float32)
+
+    count = state_ref.shape[0]
     for u in range(taps):
-        shifted = queries if u == 0 else pltpu.roll(queries, u, 0)
-        qp_ref[0 : state_ref.shape[0], u * HEAD_DIM : (u + 1) * HEAD_DIM] = shifted[
-            HALO:, :
+        qp_ref[0:count, u * HEAD_DIM : (u + 1) * HEAD_DIM] = qx_ref[
+            HALO - u : HALO - u + count, :
         ].astype(jnp.bfloat16)
-    shape = (GROUP, 256)
-    ahead = lax.broadcasted_iota(jnp.int32, shape, 1) - lax.broadcasted_iota(jnp.int32, shape, 0)
+    lane = lax.broadcasted_iota(jnp.int32, (8, 256), 1)
     for u in range(taps):
-        band = jnp.zeros(shape, jnp.float32)
+        base = jnp.zeros(lane.shape, jnp.float32)
         for t in range(key_taps):
             tap = taps_ref[0, u, t] * SCALE
             if u == 0 and t == rim:
                 tap = tap + SCALE
-            band = jnp.where(ahead == HALO + rim - t, tap, band)
+            base = jnp.where(lane == HALO + rim - t, tap, base)
+        band = jnp.concatenate([base] * (GROUP // 8), axis=0)
+        band = pltpu.roll(band, 0, 1, stride=1, stride_axis=0)
         high = band.astype(jnp.bfloat16)
         qp_ref[taps_at(qp_ref, 0, u)] = high
         qp_ref[taps_at(qp_ref, 1, u)] = (band - high.astype(jnp.float32)).astype(jnp.bfloat16)
-    done_ref[...] = jnp.zeros(done_ref.shape, jnp.float32)
-    lane = lax.broadcasted_iota(jnp.int32, state_ref.shape, 1)
-    floor = (lane >= 2 * HEAD_DIM) & (lane < 2 * HEAD_DIM + 128)
-    state_ref[...] = jnp.where(floor, FLOOR, 0.0)
-    kx_ref[...] = jnp.zeros(kx_ref.shape, jnp.bfloat16)
+    lane = lax.broadcasted_iota(jnp.int32, (count, 128), 1)
+    state_ref[:, 0 : 2 * HEAD_DIM] = jnp.zeros((count, 2 * HEAD_DIM), jnp.float32)
+    state_ref[:, 2 * HEAD_DIM :] = jnp.where(lane < 64, FLOOR, 0.0)
     lay_keys(a_ref, b_ref, kx_ref, vx_ref)
 
     @pl.loop(0, keys // BAND + 1)
     def _(tile):
         a = tile * BAND
 
-        @pl.when(block - chip_row + a < state_ref.shape[0])
+        @pl.when(block - chip_row + a < count)
         def _():
-            near(
-                a, chip_row, block, ends, taps_ref, qp_ref, kx_ref, vx_ref, state_ref
-            )
+            near(a, chip_row, block, ends, taps_ref, qp_ref, kx_ref, vx_ref, start_ref, state_ref)
 
     convolve(True, block, 0, ends, qp_ref, kx_ref, kp_ref)
-    far(chip_row, block, ends, qp_ref, kp_ref, vx_ref, state_ref)
-
-
-def hop_kernel(
-    last, place_ref, taps_ref, qp_ref, a_ref, b_ref, state_in, *rest
-):
+    far(chip_row, block, ends, qp_ref, kp_ref, vx_ref, state_ref, state_ref)
+
+
+def hop_kernel(first, last, place_ref, taps_ref, qp_ref, a_ref, b_ref, state_in, *rest):
     if last:
-        keep_ref, send_ref, kx_ref, vx_ref, kp_ref, state_ref = rest
+        keep_ref, send_ref, start_ref, kx_ref, vx_ref, kp_ref, state_ref = rest
     else:
-        state_ref, done_ref, kx_ref, vx_ref, kp_ref = rest
+        state_ref, done_ref, start_ref, kx_ref, vx_ref, kp_ref = rest
         done_ref[...] = jnp.zeros(done_ref.shape, jnp.float32)
     chip_row, block = place_ref[0], place_ref[1]
     ends = ends_of(place_ref)
     keys = kp_ref.shape[0]
     first_start = starts_of(chip_row, ends)
-    state_ref[...] = state_in[...]
-
-    @pl.when(block + keys > first_start)
+    active = block + keys > first_start
+    if first:
+        state_ref[...] = state_in[...]
+    else:
+
+        @pl.when(jnp.logical_not(active))
+        def _():
+            state_ref[...] = state_in[...]
+
+    @pl.when(active)
     def _():
-        kx_ref[...] = jnp.zeros(kx_ref.shape, jnp.bfloat16)
         lay_keys(a_ref, b_ref, kx_ref, vx_ref)
-
-        @pl.when(block + keys == chip_row)
-        def _():
-            near(
-                keys, chip_row, block, ends, taps_ref, qp_ref, kx_ref, vx_ref, state_ref
-            )
+        if first:
+
+            @pl.when(block + keys == chip_row)
+            def _():
+                near(
+                    keys, chip_row, block, ends, taps_ref, qp_ref, kx_ref, vx_ref, start_ref,
+                    state_ref,
+                )
 
         convolve(False, block, first_start, ends, qp_ref, kx_ref, kp_ref)
-        far(chip_row, block, ends, qp_ref, kp_ref, vx_ref, state_ref)
+        source = state_ref if first else state_in
+        far(chip_row, block, ends, qp_ref, kp_ref, vx_ref, source, state_ref)
 
     if last:
         core = place_ref[9]
-        lane = lax.broadcasted_iota(jnp.int32, (keys, 128), 1)
         for ref, side in ((keep_ref, core), (send_ref, 1 - core)):
-            rows = pl.ds(pl.multiple_of(side * keys, keys), keys)
-            wide = 2 * HEAD_DIM
-            ref[:, 0:wide] = state_ref[rows, 0:wide]
-            ref[:, wide:] = jnp.where(
-                lane < 64, state_ref[rows, wide : wide + 128], state_ref[rows, wide + 128 :]
-            )
+            ref[...] = state_ref[pl.ds(pl.multiple_of(side * keys, keys), keys), :]
 
 
 def join_kernel(keep_ref, other_ref, own_ref, cross_ref):
@@ -316,7 +350,7 @@
 SMEM = pl.BlockSpec(memory_space=pltpu.SMEM)
 
 
-def call(kernel, specs, out, scratch, args, aliases=None, flops=0):
+def call(kernel, specs, out, scratch, args, flops=0):
     shapes = [jax.ShapeDtypeStruct(shape, dtype) for shape, dtype in out]
     return pl.pallas_call(
         kernel,
@@ -324,7 +358,6 @@
         in_specs=specs,
         out_specs=[VMEM] * len(shapes),
         scratch_shapes=scratch,
-        input_output_aliases=aliases or {},
         cost_estimate=pl.CostEstimate(flops=flops, bytes_accessed=4 << 20, transcendentals=0),
         compiler_params=pltpu.CompilerParams(vmem_limit_bytes=20 << 20),
     )(*args)
@@ -358,23 +391,18 @@
     sibling = permute(
         jnp.concatenate([queries, behind[HALO:]]), [(i, i ^ 1) for i in range(count)]
     )
-    query_ext = jnp.where(
-        core == 0,
-        jnp.concatenate([behind[HALO:], queries, sibling[:rows]]),
-        jnp.concatenate([sibling[rows:], sibling[:rows], queries]),
-    )
-    own = (rows - 2 * HALO) // 2
-    ring_a = jnp.concatenate([key_vectors, behind[:HALO], beyond, values[:own]])
-    ring_b = jnp.concatenate([values[own:], other_values])
+    ring_a = jnp.concatenate([key_vectors, behind[:HALO], beyond])
+    ring_b = jnp.concatenate([values, other_values])
     chip = group // 2
 
     def place(hop):
         head = jnp.stack([chip * 2 * rows, (chip - hop) * 2 * rows + core * rows])
         return jnp.concatenate([head, doc_lengths[:7], core[None]]).astype(jnp.int32)
 
-    state = [((2 * rows, 2 * HEAD_DIM + 256), f32)]
+    state = [((2 * rows, 3 * HEAD_DIM), f32)]
     mark = [((8, 128), f32)]
     scratch = [
+        pltpu.VMEM((BAND + 8, GROUP), jnp.int32),
         pltpu.VMEM((rows + 128, HEAD_DIM), bf16),
         pltpu.VMEM((rows + 2 * HALO, 2 * HEAD_DIM), bf16),
         pltpu.VMEM((rows, 2 * width), bf16),
@@ -382,12 +410,12 @@
     flops = 2 * 2 * rows * rows * (2 * width + 2 * HEAD_DIM)
     operand, running, done = call(
         local_kernel,
-        [SMEM, SMEM, VMEM, VMEM, VMEM],
+        [SMEM, SMEM] + [VMEM] * 5,
         [((2 * rows + 2 * taps * GROUP * 256 // width, width), bf16)]
         + state
         + mark,
-        scratch,
-        (place(0), kernel, query_ext, ring_a, ring_b),
+        [pltpu.VMEM((2 * rows + HALO, HEAD_DIM), f32)] + scratch,
+        (place(0), kernel, queries, sibling, behind, ring_a, ring_b),
         flops=flops,
     )
     for hop in range(1, HOPS + 1):
@@ -398,12 +426,11 @@
         out = [((rows, 3 * HEAD_DIM), f32)] * 2 if last else state + mark
         extra = [pltpu.VMEM(shape, dtype) for shape, dtype in state] if last else []
         result = call(
-            functools.partial(hop_kernel, last),
+            functools.partial(hop_kernel, hop == 1, last),
             [SMEM, SMEM] + [VMEM] * 4,
             out,
             scratch + extra,
             (place(hop), kernel, operand, ring_a, ring_b, running),
-            aliases=None if last else {5: 0},
             flops=flops,
         )
         if not last:

time: 95.8 us -> 90.6 us (0.946)
  starting transfers between devices: 47.8 us -> 54.8 us
  waiting for transfers between devices: 15.7 us -> 8.87 us
  local copies, waits for them, and re-layouts: 9.71 us -> 6.55 us
  other arithmetic: 3.81 us -> 2.74 us
  Pallas kernels: 17.7 us -> 16.7 us
    ppermute x12, starting transfers between devices: 43.8 us -> 50.1 us  [permute(): return lax.ppermute(value, 'ctx', pairs)]
    ppermute x12, waiting for transfers between devices: 9.79 us -> 3.52 us  [permute(): return lax.ppermute(value, 'ctx', pairs)]
    slice x5 -> x1, local copies, waits for them, and re-layouts: 1.74 us -> 0.01 us  [body(): ring_a = jnp.concatenate([key_vectors, behind[:HALO], beyond])]
    unnamed x15 -> x14, local copies, waits for them, and re-layouts: 6.58 us -> 5.14 us
    select_n x1 -> x0, other arithmetic: 1.05 us -> none  [body(): jnp.where(core == 0, jnp.concatenate([behind[HALO:], queries, sibling[:ro...]
    pallas_call x7, Pallas kernels: 17.7 us -> 16.7 us  [call(): pl.pallas_call(kernel, out_shape=shapes, in_specs=specs, out_specs=[VMEM]...]
  transfers between devices with their start and end apart: 14 -> 14, of which waited for: 4 -> 3; matrix products, arithmetic and copies ran while one was open for 7% -> 5% of each run, Pallas kernels for 16% -> 16%
where the time goes in v3:
time: 90.6 us; the launch traced here: 90 us
  starting transfers between devices  54.8 us (60%)
  Pallas kernels  16.7 us (18%)
  waiting for transfers between devices  8.87 us (10%)
  local copies, waits for them, and re-layouts  6.55 us (7%)
  other arithmetic  2.74 us (3%)
    ppermute x12, starting transfers between devices, permute(): return lax.ppermute(value, 'ctx', pairs)  50.1 us
    pallas_call x7, Pallas kernels, call(): pl.pallas_call(kernel, out_shape=shapes, in_specs=specs, out_specs=[VMEM]...  16.7 us
    ppermute x2, waiting for transfers between devices, partner(): lax.ppermute(value, 'head', [(i, i ^ heads // 2) for i in range(heads)])  5.35 us
    unnamed x14, local copies, waits for them, and re-layouts  5.14 us
    ppermute x2, starting transfers between devices, partner(): lax.ppermute(value, 'head', [(i, i ^ heads // 2) for i in range(heads)])  4.66 us
    ppermute x12, waiting for transfers between devices, permute(): return lax.ppermute(value, 'ctx', pairs)  3.52 us
  transfers between devices with their start and end apart: 14, of which 3 were waited for; matrix products, arithmetic and copies ran while one was open for 5% of the time, Pallas kernels for 16%

profile of v3, /device:TPU:1, one launch (start us, length us, event | category | flops | bytes accessed | tf_op | source)
XLA Modules:
  0.0 90.0 jit_solution(4759743643291031995)
XLA Ops:
  0.0 0.7 fusion
  0.7 0.7 slice.24
  1.4 3.5 %collective-permute-start = (bf16[32,128]{1,0:T(8,128)(2,1)S(1)}, bf16[32,128]{1,0:T(8,128)(2,1)S(1)}, u32[]{:S(2)}, u32[]{:S(2)}) collective-permute-start(bf16[32,128]{1,0:T(8,128)(2,1)S(1)} %pad_maximum_fusion.2), channel_id=1, source_target_pairs={{0,32},{32,64},{64,96},{96,128},{128,160},{160,192},{192,224},{224... | collective-permute-start | bytes 24584 | tf_op jit(solution)/shard_map/ppermute | solution.py:377
  4.9 3.4 %collective-permute-start.2 = (bf16[16,128]{1,0:T(8,128)(2,1)S(1)}, bf16[16,128]{1,0:T(8,128)(2,1)S(1)}, u32[]{:S(2)}, u32[]{:S(2)}) collective-permute-start(bf16[16,128]{1,0:T(8,128)(2,1)S(1)} %get-tuple-element.47), channel_id=1, source_target_pairs={{0,480},{32,0},{64,32},{96,64},{128,96},{160,128},{192,160},{224,1... | collective-permute-start | bytes 12296 | tf_op jit(solution)/shard_map/ppermute | solution.py:377
  8.3 1.9 %collective-permute-start.3 = (bf16[512,128]{1,0:T(8,128)(2,1)}, bf16[512,128]{1,0:T(8,128)(2,1)S(1)}, u32[]{:S(2)}, u32[]{:S(2)}) collective-permute-start(bf16[512,128]{1,0:T(8,128)(2,1)} %param.9), channel_id=1, source_target_pairs={{0,16},{1,17},{2,18},{3,19},{4,20},{5,21},{6,22},{7,23},{8,24},{9,... | collective-permute-start | bytes 393224 | tf_op jit(solution)/shard_map/ppermute | solution.py:383
  10.2 1.0 %constant_dynamic-update-slice_fusion.1 = bf16[1024,128]{1,0:T(8,128)(2,1)S(1)} fusion(bf16[512,128]{1,0:T(8,128)(2,1)} %param.9), kind=kLoop, calls=%fused_computation.4 | loop fusion | bytes 262144
  11.2 0.7 add_add_fusion.4
  11.9 0.7 copy.12.taps_ref
  12.6 0.0 collective-permute-done.edge_ref
  12.6 0.9 %pad_maximum_fusion.1 = bf16[528,128]{1,0:T(8,128)(2,1)S(1)} fusion(bf16[16,128]{1,0:T(8,128)(2,1)S(1)} %get-tuple-element.50, bf16[512,128]{1,0:T(8,128)(2,1)} %own_ref.1), kind=kLoop, calls=%fused_computation.1 | loop fusion | flops 270336 | bytes 270336 | tf_op jit(solution)/shard_map/concatenate | solution.py:392
  13.5 8.0 %collective-permute-start.1 = (bf16[528,128]{1,0:T(8,128)(2,1)S(1)}, bf16[528,128]{1,0:T(8,128)(2,1)S(1)}, u32[]{:S(2)}, u32[]{:S(2)}) collective-permute-start(bf16[528,128]{1,0:T(8,128)(2,1)S(1)} %pad_maximum_fusion.1), channel_id=1, source_target_pairs={{0,32},{32,0},{64,96},{96,64},{128,160},{160,128},{192,224},{224,1... | collective-permute-start | bytes 405512 | tf_op jit(solution)/shard_map/ppermute | solution.py:377
  21.6 0.0 collective-permute-done.3
  21.6 1.9 %collective-permute-start.6 = (bf16[1024,128]{1,0:T(8,128)(2,1)S(1)}, bf16[1024,128]{1,0:T(8,128)(2,1)S(1)}, u32[]{:S(2)}, u32[]{:S(2)}) collective-permute-start(bf16[1024,128]{1,0:T(8,128)(2,1)S(1)} %constant_dynamic-update-slice_fusion.b_ref), channel_id=1, source_target_pairs={{0,64},{32,96},{64,128},{96,160},{128,192},{160,224},{192,256},{22... | collective-permute-start | bytes 786440 | tf_op jit(solution)/shard_map/ppermute | solution.py:377
  23.5 0.0 collective-permute-done.2
  23.6 0.9 %pad_maximum_fusion.a_ref = bf16[544,128]{1,0:T(8,128)(2,1)S(1)} fusion(bf16[16,128]{1,0:T(8,128)(2,1)S(1)} %collective-permute-done.2, bf16[16,128]{1,0:T(8,128)(2,1)S(1)} %get-tuple-element.49, bf16[512,128]{1,0:T(8,128)(2,1)} %param.8), kind=kLoop, calls=%fused_computation | loop fusion | flops 417792 | bytes 278528 | tf_op jit(solution)/shard_map/concatenate | solution.py:394
  24.5 1.9 %collective-permute-start.4 = (bf16[544,128]{1,0:T(8,128)(2,1)S(1)}, bf16[544,128]{1,0:T(8,128)(2,1)S(1)}, u32[]{:S(2)}, u32[]{:S(2)}) collective-permute-start(bf16[544,128]{1,0:T(8,128)(2,1)S(1)} %pad_maximum_fusion.a_ref), channel_id=1, source_target_pairs={{0,64},{32,96},{64,128},{96,160},{128,192},{160,224},{192,256},{22... | collective-permute-start | bytes 417800 | tf_op jit(solution)/shard_map/ppermute | solution.py:377
  26.4 0.0 collective-permute-done.1.other_ref
  26.4 0.0 copy-start
  26.4 0.9 copy-done
  27.3 0.0 copy-start.5
  27.3 10.0 %shard_map.73 = (bf16[1536,768]{1,0:T(8,128)(2,1)S(1)}, f32[1024,384]{1,0:T(8,128)S(1)}, f32[8,128]{1,0:T(8,128)}) custom-call(s32[10]{0:T(128)S(1)} %get-tuple-element.52.place_ref, f32[1,6,11]{2,1,0:T(8,128)S(1)} %copy.12.taps_ref, bf16[512,128]{1,0:T(8,128)(2,1)S(1)} %copy-done, bf16[528,128]{1,0:T(8,128)(2,1)S(1)} %collective-permute-done.1.other_ref, ...), custom_call_target="tpu_custom_call" | custom-call | flops 1879048192 | bytes 4194304 | tf_op jit(solution)/shard_map/pallas_call | solution.py:355
  37.3 0.0 collective-permute-done.6.b_ref
  37.3 2.2 %collective-permute-start.8 = (bf16[1024,128]{1,0:T(8,128)(2,1)S(1)}, bf16[1024,128]{1,0:T(8,128)(2,1)S(1)}, u32[]{:S(2)}, u32[]{:S(2)}) collective-permute-start(bf16[1024,128]{1,0:T(8,128)(2,1)S(1)} %collective-permute-done.6.b_ref), channel_id=1, source_target_pairs={{0,64},{32,96},{64,128},{96,160},{128,192},{160,224},{192,256},{22... | collective-permute-start | bytes 786440 | tf_op jit(solution)/shard_map/ppermute | solution.py:377
  39.6 0.0 copy-done.5
  39.6 0.1 add_add_fusion.3
  39.6 0.0 collective-permute-done.4.a_ref
  39.7 5.2 %collective-permute-start.5 = (bf16[544,128]{1,0:T(8,128)(2,1)S(1)}, bf16[544,128]{1,0:T(8,128)(2,1)S(1)}, u32[]{:S(2)}, u32[]{:S(2)}) collective-permute-start(bf16[544,128]{1,0:T(8,128)(2,1)S(1)} %collective-permute-done.4.a_ref), channel_id=1, source_target_pairs={{0,64},{32,96},{64,128},{96,160},{128,192},{160,224},{192,256},{22... | collective-permute-start | bytes 417800 | tf_op jit(solution)/shard_map/ppermute | solution.py:377
  44.9 1.3 %shard_map.74 = (f32[1024,384]{1,0:T(8,128)S(1)}, f32[8,128]{1,0:T(8,128)}) custom-call(s32[10]{0:T(128)S(1)} %get-tuple-element.54.place_ref, f32[1,6,11]{2,1,0:T(8,128)S(1)} %copy.12.taps_ref, bf16[1536,768]{1,0:T(8,128)(2,1)S(1)} %get-tuple-element.26.qp_ref, bf16[544,128]{1,0:T(8,128)(2,1)S(1)} %collective-permute-done.4.a_ref, ...), custom_call_target="tpu_custom_call" | custom-call | flops 1879048192 | bytes 4194304 | tf_op jit(solution)/shard_map/pallas_call | solution.py:355
  46.2 0.0 copy-start.3
  46.2 1.2 %copy-done.3 = f32[1024,384]{1,0:T(8,128)} copy-done((f32[1024,384]{1,0:T(8,128)}, f32[1024,384]{1,0:T(8,128)S(1)}, u32[]{:S(2)}) %copy-start.3) | copy-done | bytes 1572888
  47.4 0.0 collective-permute-done.8.b_ref
  47.4 6.6 %collective-permute-start.10 = (bf16[1024,128]{1,0:T(8,128)(2,1)S(1)}, bf16[1024,128]{1,0:T(8,128)(2,1)S(1)}, u32[]{:S(2)}, u32[]{:S(2)}) collective-permute-start(bf16[1024,128]{1,0:T(8,128)(2,1)S(1)} %collective-permute-done.8.b_ref), channel_id=1, source_target_pairs={{0,64},{32,96},{64,128},{96,160},{128,192},{160,224},{192,256},{22... | collective-permute-start | bytes 786440 | tf_op jit(solution)/shard_map/ppermute | solution.py:377
  54.0 0.0 collective-permute-done.5.a_ref
  54.0 3.5 %collective-permute-start.7 = (bf16[544,128]{1,0:T(8,128)(2,1)S(1)}, bf16[544,128]{1,0:T(8,128)(2,1)S(1)}, u32[]{:S(2)}, u32[]{:S(2)}) collective-permute-start(bf16[544,128]{1,0:T(8,128)(2,1)S(1)} %collective-permute-done.5.a_ref), channel_id=1, source_target_pairs={{0,64},{32,96},{64,128},{96,160},{128,192},{160,224},{192,256},{22... | collective-permute-start | bytes 417800 | tf_op jit(solution)/shard_map/ppermute | solution.py:377
  57.5 0.0 copy-start.4
  57.5 1.4 %copy-done.4 = f32[1024,384]{1,0:T(8,128)S(1)} copy-done((f32[1024,384]{1,0:T(8,128)S(1)}, f32[1024,384]{1,0:T(8,128)}, u32[]{:S(2)}) %copy-start.4) | copy-done | bytes 1572888
  58.9 1.3 %shard_map.75 = (f32[1024,384]{1,0:T(8,128)S(1)}, f32[8,128]{1,0:T(8,128)}) custom-call(s32[10]{0:T(128)S(1)} %get-tuple-element.53.place_ref, f32[1,6,11]{2,1,0:T(8,128)S(1)} %copy.12.taps_ref, bf16[1536,768]{1,0:T(8,128)(2,1)S(1)} %get-tuple-element.26.qp_ref, bf16[544,128]{1,0:T(8,128)(2,1)S(1)} %collective-permute-done.5.a_ref, ...), custom_call_target="tpu_custom_call" | custom-call | flops 1879048192 | bytes 4194304 | tf_op jit(solution)/shard_map/pallas_call | solution.py:355
  60.2 0.0 collective-permute-done.10.b_ref
  60.2 3.1 %collective-permute-start.11 = (bf16[1024,128]{1,0:T(8,128)(2,1)S(1)}, bf16[1024,128]{1,0:T(8,128)(2,1)S(1)}, u32[]{:S(2)}, u32[]{:S(2)}) collective-permute-start(bf16[1024,128]{1,0:T(8,128)(2,1)S(1)} %collective-permute-done.10.b_ref), channel_id=1, source_target_pairs={{0,64},{32,96},{64,128},{96,160},{128,192},{160,224},{192,256},{22... | collective-permute-start | bytes 786440 | tf_op jit(solution)/shard_map/ppermute | solution.py:377
  63.3 0.1 add_add_fusion.place_ref
  63.4 0.0 collective-permute-done.7.a_ref
  63.4 6.4 %collective-permute-start.9 = (bf16[544,128]{1,0:T(8,128)(2,1)S(1)}, bf16[544,128]{1,0:T(8,128)(2,1)S(1)}, u32[]{:S(2)}, u32[]{:S(2)}) collective-permute-start(bf16[544,128]{1,0:T(8,128)(2,1)S(1)} %collective-permute-done.7.a_ref), channel_id=1, source_target_pairs={{0,64},{32,96},{64,128},{96,160},{128,192},{160,224},{192,256},{22... | collective-permute-start | bytes 417800 | tf_op jit(solution)/shard_map/ppermute | solution.py:377
  69.8 1.5 %shard_map.76 = (f32[1024,384]{1,0:T(8,128)S(1)}, f32[8,128]{1,0:T(8,128)}) custom-call(s32[10]{0:T(128)S(1)} %get-tuple-element.51.place_ref, f32[1,6,11]{2,1,0:T(8,128)S(1)} %copy.12.taps_ref, bf16[1536,768]{1,0:T(8,128)(2,1)S(1)} %get-tuple-element.26.qp_ref, bf16[544,128]{1,0:T(8,128)(2,1)S(1)} %collective-permute-done.7.a_ref, ...), custom_call_target="tpu_custom_call" | custom-call | flops 1879048192 | bytes 4194304 | tf_op jit(solution)/shard_map/pallas_call | solution.py:355
  71.3 1.6 %collective-permute-done.9.a_ref = bf16[544,128]{1,0:T(8,128)(2,1)S(1)} collective-permute-done((bf16[544,128]{1,0:T(8,128)(2,1)S(1)}, bf16[544,128]{1,0:T(8,128)(2,1)S(1)}, u32[]{:S(2)}, u32[]{:S(2)}) %collective-permute-start.9) | collective-permute-done | bytes 139296 | tf_op jit(solution)/shard_map/ppermute | solution.py:377
  72.9 0.0 collective-permute-done.11.b_ref
  72.9 0.8 shard_map.77
  73.7 0.0 copy-start.1
  73.7 0.0 copy-start.2
  73.8 4.4 %collective-permute-start.12 = (f32[512,384]{1,0:T(8,128)S(1)}, f32[512,384]{1,0:T(8,128)S(1)}, u32[]{:S(2)}, u32[]{:S(2)}) collective-permute-start(f32[512,384]{1,0:T(8,128)S(1)} %get-tuple-element.44), channel_id=1, source_target_pairs={{0,32},{32,0},{64,96},{96,64},{128,160},{160,128},{192,224},{224,1... | collective-permute-start | bytes 2359304 | tf_op jit(solution)/shard_map/ppermute | solution.py:377
  78.2 1.9 %collective-permute-done.12.other_ref = f32[512,384]{1,0:T(8,128)S(1)} collective-permute-done((f32[512,384]{1,0:T(8,128)S(1)}, f32[512,384]{1,0:T(8,128)S(1)}, u32[]{:S(2)}, u32[]{:S(2)}) %collective-permute-start.12) | collective-permute-done | bytes 786464 | tf_op jit(solution)/shard_map/ppermute | solution.py:377
  80.1 0.4 shard_map.78
  80.5 2.8 %collective-permute-start.13 = (bf16[512,128]{1,0:T(8,128)(2,1)S(1)}, bf16[512,128]{1,0:T(8,128)(2,1)S(1)}, u32[]{:S(2)}, u32[]{:S(2)}) collective-permute-start(bf16[512,128]{1,0:T(8,128)(2,1)S(1)} %get-tuple-element.46), channel_id=1, source_target_pairs={{0,16},{1,17},{2,18},{3,19},{4,20},{5,21},{6,22},{7,23},{8,24},{9,... | collective-permute-start | bytes 393224 | tf_op jit(solution)/shard_map/ppermute | solution.py:383
  83.2 5.3 %collective-permute-done.13.cross_ref = bf16[512,128]{1,0:T(8,128)(2,1)S(1)} collective-permute-done((bf16[512,128]{1,0:T(8,128)(2,1)S(1)}, bf16[512,128]{1,0:T(8,128)(2,1)S(1)}, u32[]{:S(2)}, u32[]{:S(2)}) %collective-permute-start.13) | collective-permute-done | bytes 131104 | tf_op jit(solution)/shard_map/ppermute | solution.py:383
  88.6 0.0 copy-done.1
  88.6 0.0 copy-done.2
  88.6 1.4 %shard_map.79 = bf16[512,128]{1,0:T(8,128)(2,1)} custom-call(f32[2]{0:T(128)S(1)} %bitcast.10, f32[512,128]{1,0:T(8,128)S(1)} %get-tuple-element.45.own_ref, bf16[512,128]{1,0:T(8,128)(2,1)S(1)} %collective-permute-done.13.cross_ref, f32[1,128]{1,0:T(1,128)S(1)} %bitcast.11), custom_call_target="tpu_custom_call" | custom-call | bytes 4194304 | tf_op jit(solution)/shard_map/pallas_call | solution.py:355
  (3 shorter events, 0.0 us)
Async XLA Ops:
  1.4 11.2 %collective-permute-start = (bf16[32,128]{1,0:T(8,128)(2,1)S(1)}, bf16[32,128]{1,0:T(8,128)(2,1)S(1)}, u32[]{:S(2)}, u32[]{:S(2)}) collective-permute-start(bf16[32,128]{1,0:T(8,128)(2,1)S(1)} %pad_maximum_fusion.2), channel_id=1, source_target_pairs={{0,32},{32,64},{64,96},{96,128},{128,160},{160,192},{192,224},{224... | collective-permute-start | bytes 24584 | tf_op jit(solution)/shard_map/ppermute | solution.py:377
  4.9 18.7 %collective-permute-start.2 = (bf16[16,128]{1,0:T(8,128)(2,1)S(1)}, bf16[16,128]{1,0:T(8,128)(2,1)S(1)}, u32[]{:S(2)}, u32[]{:S(2)}) collective-permute-start(bf16[16,128]{1,0:T(8,128)(2,1)S(1)} %get-tuple-element.47), channel_id=1, source_target_pairs={{0,480},{32,0},{64,32},{96,64},{128,96},{160,128},{192,160},{224,1... | collective-permute-start | bytes 12296 | tf_op jit(solution)/shard_map/ppermute | solution.py:377
  8.3 13.3 %collective-permute-start.3 = (bf16[512,128]{1,0:T(8,128)(2,1)}, bf16[512,128]{1,0:T(8,128)(2,1)S(1)}, u32[]{:S(2)}, u32[]{:S(2)}) collective-permute-start(bf16[512,128]{1,0:T(8,128)(2,1)} %param.9), channel_id=1, source_target_pairs={{0,16},{1,17},{2,18},{3,19},{4,20},{5,21},{6,22},{7,23},{8,24},{9,... | collective-permute-start | bytes 393224 | tf_op jit(solution)/shard_map/ppermute | solution.py:383
  13.5 12.9 %collective-permute-start.1 = (bf16[528,128]{1,0:T(8,128)(2,1)S(1)}, bf16[528,128]{1,0:T(8,128)(2,1)S(1)}, u32[]{:S(2)}, u32[]{:S(2)}) collective-permute-start(bf16[528,128]{1,0:T(8,128)(2,1)S(1)} %pad_maximum_fusion.1), channel_id=1, source_target_pairs={{0,32},{32,0},{64,96},{96,64},{128,160},{160,128},{192,224},{224,1... | collective-permute-start | bytes 405512 | tf_op jit(solution)/shard_map/ppermute | solution.py:377
  21.6 15.7 %collective-permute-start.6 = (bf16[1024,128]{1,0:T(8,128)(2,1)S(1)}, bf16[1024,128]{1,0:T(8,128)(2,1)S(1)}, u32[]{:S(2)}, u32[]{:S(2)}) collective-permute-start(bf16[1024,128]{1,0:T(8,128)(2,1)S(1)} %constant_dynamic-update-slice_fusion.b_ref), channel_id=1, source_target_pairs={{0,64},{32,96},{64,128},{96,160},{128,192},{160,224},{192,256},{22... | collective-permute-start | bytes 786440 | tf_op jit(solution)/shard_map/ppermute | solution.py:377
  24.5 15.2 %collective-permute-start.4 = (bf16[544,128]{1,0:T(8,128)(2,1)S(1)}, bf16[544,128]{1,0:T(8,128)(2,1)S(1)}, u32[]{:S(2)}, u32[]{:S(2)}) collective-permute-start(bf16[544,128]{1,0:T(8,128)(2,1)S(1)} %pad_maximum_fusion.a_ref), channel_id=1, source_target_pairs={{0,64},{32,96},{64,128},{96,160},{128,192},{160,224},{192,256},{22... | collective-permute-start | bytes 417800 | tf_op jit(solution)/shard_map/ppermute | solution.py:377
  26.4 0.9 %copy-start = (bf16[512,128]{1,0:T(8,128)(2,1)S(1)}, bf16[512,128]{1,0:T(8,128)(2,1)}, u32[]{:S(2)}) copy-start(bf16[512,128]{1,0:T(8,128)(2,1)} %own_ref.1) | copy-start | bytes 393220
  27.3 12.2 %copy-start.5 = (s32[8]{0:T(128)S(1)}, s32[8]{0:T(128)}, u32[]{:S(2)}) copy-start(s32[8]{0:T(128)} %param.13) | copy-start | bytes 100
  37.3 10.0 %collective-permute-start.8 = (bf16[1024,128]{1,0:T(8,128)(2,1)S(1)}, bf16[1024,128]{1,0:T(8,128)(2,1)S(1)}, u32[]{:S(2)}, u32[]{:S(2)}) collective-permute-start(bf16[1024,128]{1,0:T(8,128)(2,1)S(1)} %collective-permute-done.6.b_ref), channel_id=1, source_target_pairs={{0,64},{32,96},{64,128},{96,160},{128,192},{160,224},{192,256},{22... | collective-permute-start | bytes 786440 | tf_op jit(solution)/shard_map/ppermute | solution.py:377
  39.7 14.4 %collective-permute-start.5 = (bf16[544,128]{1,0:T(8,128)(2,1)S(1)}, bf16[544,128]{1,0:T(8,128)(2,1)S(1)}, u32[]{:S(2)}, u32[]{:S(2)}) collective-permute-start(bf16[544,128]{1,0:T(8,128)(2,1)S(1)} %collective-permute-done.4.a_ref), channel_id=1, source_target_pairs={{0,64},{32,96},{64,128},{96,160},{128,192},{160,224},{192,256},{22... | collective-permute-start | bytes 417800 | tf_op jit(solution)/shard_map/ppermute | solution.py:377
  46.2 1.2 %copy-start.3 = (f32[1024,384]{1,0:T(8,128)}, f32[1024,384]{1,0:T(8,128)S(1)}, u32[]{:S(2)}) copy-start(f32[1024,384]{1,0:T(8,128)S(1)} %get-tuple-element.34.state_in) | copy-start | bytes 4718596
  47.4 12.8 %collective-permute-start.10 = (bf16[1024,128]{1,0:T(8,128)(2,1)S(1)}, bf16[1024,128]{1,0:T(8,128)(2,1)S(1)}, u32[]{:S(2)}, u32[]{:S(2)}) collective-permute-start(bf16[1024,128]{1,0:T(8,128)(2,1)S(1)} %collective-permute-done.8.b_ref), channel_id=1, source_target_pairs={{0,64},{32,96},{64,128},{96,160},{128,192},{160,224},{192,256},{22... | collective-permute-start | bytes 786440 | tf_op jit(solution)/shard_map/ppermute | solution.py:377
  54.0 9.4 %collective-permute-start.7 = (bf16[544,128]{1,0:T(8,128)(2,1)S(1)}, bf16[544,128]{1,0:T(8,128)(2,1)S(1)}, u32[]{:S(2)}, u32[]{:S(2)}) collective-permute-start(bf16[544,128]{1,0:T(8,128)(2,1)S(1)} %collective-permute-done.5.a_ref), channel_id=1, source_target_pairs={{0,64},{32,96},{64,128},{96,160},{128,192},{160,224},{192,256},{22... | collective-permute-start | bytes 417800 | tf_op jit(solution)/shard_map/ppermute | solution.py:377
  57.5 1.4 %copy-start.4 = (f32[1024,384]{1,0:T(8,128)S(1)}, f32[1024,384]{1,0:T(8,128)}, u32[]{:S(2)}) copy-start(f32[1024,384]{1,0:T(8,128)} %copy-done.3) | copy-start | bytes 4718596
  60.2 12.7 %collective-permute-start.11 = (bf16[1024,128]{1,0:T(8,128)(2,1)S(1)}, bf16[1024,128]{1,0:T(8,128)(2,1)S(1)}, u32[]{:S(2)}, u32[]{:S(2)}) collective-permute-start(bf16[1024,128]{1,0:T(8,128)(2,1)S(1)} %collective-permute-done.10.b_ref), channel_id=1, source_target_pairs={{0,64},{32,96},{64,128},{96,160},{128,192},{160,224},{192,256},{22... | collective-permute-start | bytes 786440 | tf_op jit(solution)/shard_map/ppermute | solution.py:377
  63.4 9.5 %collective-permute-start.9 = (bf16[544,128]{1,0:T(8,128)(2,1)S(1)}, bf16[544,128]{1,0:T(8,128)(2,1)S(1)}, u32[]{:S(2)}, u32[]{:S(2)}) collective-permute-start(bf16[544,128]{1,0:T(8,128)(2,1)S(1)} %collective-permute-done.7.a_ref), channel_id=1, source_target_pairs={{0,64},{32,96},{64,128},{96,160},{128,192},{160,224},{192,256},{22... | collective-permute-start | bytes 417800 | tf_op jit(solution)/shard_map/ppermute | solution.py:377
  73.7 14.9 %copy-start.1 = (f32[1,2]{1,0:T(1,128)S(1)}, f32[1,2]{1,0:T(1,128)}, u32[]{:S(2)}) copy-start(f32[1,2]{1,0:T(1,128)} %param.11) | copy-start | bytes 28
  73.7 14.9 %copy-start.2 = (f32[128]{0:T(128)S(1)}, f32[128]{0:T(128)}, u32[]{:S(2)}) copy-start(f32[128]{0:T(128)} %param.12) | copy-start | bytes 1540
  73.8 6.3 %collective-permute-start.12 = (f32[512,384]{1,0:T(8,128)S(1)}, f32[512,384]{1,0:T(8,128)S(1)}, u32[]{:S(2)}, u32[]{:S(2)}) collective-permute-start(f32[512,384]{1,0:T(8,128)S(1)} %get-tuple-element.44), channel_id=1, source_target_pairs={{0,32},{32,0},{64,96},{96,64},{128,160},{160,128},{192,224},{224,1... | collective-permute-start | bytes 2359304 | tf_op jit(solution)/shard_map/ppermute | solution.py:377
  80.5 8.1 %collective-permute-start.13 = (bf16[512,128]{1,0:T(8,128)(2,1)S(1)}, bf16[512,128]{1,0:T(8,128)(2,1)S(1)}, u32[]{:S(2)}, u32[]{:S(2)}) collective-permute-start(bf16[512,128]{1,0:T(8,128)(2,1)S(1)} %get-tuple-element.46), channel_id=1, source_target_pairs={{0,16},{1,17},{2,18},{3,19},{4,20},{5,21},{6,22},{7,23},{8,24},{9,... | collective-permute-start | bytes 393224 | tf_op jit(solution)/shard_map/ppermute | solution.py:383

commit v4 on v3

--- a/solution.py
+++ b/solution.py
@@ -13,6 +13,7 @@
 FLOOR = -1e20
 HALO = 16
 BAND = 64
+TILES = 4
 GROUP = 128
 WIDE = 256
 REACH = 10
@@ -65,63 +66,91 @@
 
 
 def lay_keys(a_ref, b_ref, kx_ref, vx_ref):
-    keys = b_ref.shape[0] // 2
-    kx_ref[0:HALO, :] = a_ref[keys : keys + HALO, :]
-    kx_ref[HALO : HALO + keys, :] = a_ref[0:keys, :]
-    kx_ref[HALO + keys : 2 * HALO + keys, :] = a_ref[keys + HALO : keys + 2 * HALO, :]
+    keys = a_ref.shape[0]
+    kx_ref[0:HALO, :] = b_ref[2 * keys : 2 * keys + HALO, :]
+    kx_ref[HALO : HALO + keys, :] = a_ref[...]
+    kx_ref[HALO + keys : 2 * HALO + keys, :] = b_ref[2 * keys + HALO :, :]
     kx_ref[2 * HALO + keys :, :] = jnp.zeros_like(kx_ref[2 * HALO + keys :, :])
     vx_ref[0:HALO, :] = jnp.zeros((HALO, 2 * HEAD_DIM), jnp.bfloat16)
     vx_ref[HALO : HALO + keys, 0:HEAD_DIM] = b_ref[0:keys, :]
-    vx_ref[HALO : HALO + keys, HEAD_DIM:] = b_ref[keys:, :]
-    vx_ref[HALO + keys :, :] = jnp.zeros((HALO, 2 * HEAD_DIM), jnp.bfloat16)
-
-
-def near(a, chip_row, block, ends, taps_ref, qp_ref, kx_ref, vx_ref, start_ref, state_ref):
-    keys = vx_ref.shape[0] - 2 * HALO
+    vx_ref[HALO : HALO + keys, HEAD_DIM:] = b_ref[keys : 2 * keys, :]
+    vx_ref[HALO + keys :, :] = jnp.zeros_like(vx_ref[HALO + keys :, :])
+
+
+def near(tiles, chip_row, block, ends, taps_ref, qp_ref, kx_ref, vx_ref, start_ref, state_ref):
+    keys = kx_ref.shape[0] - 128
     query_taps, key_taps = taps_ref.shape[1:]
     rim = (key_taps - 1) // 2
-    low = pl.multiple_of(jnp.clip(a - 32, 0, keys + 2 * HALO - GROUP), 16)
-    rows = pl.ds(pl.multiple_of(block - chip_row + a, 16), BAND)
-    window = kx_ref[pl.ds(low, GROUP), :]
-    shape = (BAND, GROUP)
-    top = block + a
-    one_start = starts_of(top + BAND - 1, ends)
-    one = starts_of(top - 8, ends) == one_start
-
-    @pl.when(one)
-    def _():
-        start_ref[...] = jnp.full(start_ref.shape, one_start, jnp.int32)
-
-    @pl.when(jnp.logical_not(one))
-    def _():
-        position = top - 8 + lax.broadcasted_iota(jnp.int32, start_ref.shape, 0)
-        start_ref[...] = starts_of(position, ends)
-
-    row = top + lax.broadcasted_iota(jnp.int32, shape, 0)
-    col = block - HALO + low + lax.broadcasted_iota(jnp.int32, shape, 1)
-    behind = row - col
-    stacked = jnp.concatenate(
-        [qp_ref[rows, u * HEAD_DIM : (u + 1) * HEAD_DIM] for u in range(query_taps)], axis=0
-    )
-    products = dot_t(stacked, window)
-    scores = []
-    for u in range(query_taps):
-        allowed = (behind >= u) & (col >= start_ref[8 - u : 8 - u + BAND, :])
-        scores.append(jnp.where(allowed, products[u * BAND : (u + 1) * BAND, :], 0.0))
-    conv = None
-    for t in range(key_taps):
-        terms = None
+    half = BAND // 2
+    shape = (half, GROUP)
+    for n, a in enumerate(tiles):
+        top = block + a
+        one_start = starts_of(top + BAND - 1, ends)
+        one = starts_of(top - 8, ends) == one_start
+
+        @pl.when(one)
+        def _(n=n, one_start=one_start):
+            start_ref[n] = jnp.full(start_ref.shape[1:], one_start, jnp.int32)
+
+        @pl.when(jnp.logical_not(one))
+        def _(n=n, top=top):
+            side = lax.broadcasted_iota(jnp.int32, start_ref.shape[1:], 1) >= 64
+            position = top - 8 + lax.broadcasted_iota(jnp.int32, start_ref.shape[1:], 0)
+            start_ref[n] = starts_of(position + jnp.where(side, half, 0), ends)
+
+    lane = lax.broadcasted_iota(jnp.int32, shape, 1)
+    left = lane < 64
+    shift = jnp.where(left, 0, half)
+    step = lax.broadcasted_iota(jnp.int32, shape, 0) + shift
+    place = lane - HALO - shift
+    behind = step - place
+    work = []
+    for n, a in enumerate(tiles):
+        rows = pl.ds(pl.multiple_of(block - chip_row + a, 16), BAND)
+        parts = [
+            (pl.ds(pl.multiple_of(a + m, 16), 64), pl.ds(pl.multiple_of(block - chip_row + a + m, 16), half))
+            for m in (0, half)
+        ]
+        stacked = jnp.concatenate(
+            [
+                qp_ref[part, u * HEAD_DIM : (u + 1) * HEAD_DIM]
+                for _, part in parts
+                for u in range(query_taps)
+            ],
+            axis=0,
+        )
+        window = jnp.concatenate([kx_ref[span, :] for span, _ in parts], axis=0)
+        values = jnp.concatenate([vx_ref[span, :] for span, _ in parts], axis=0)
+        work.append((n, rows, block + a + place, dot_t(stacked, window), values))
+    done = []
+    for n, rows, col, products, values in work:
+        scores = []
         for u in range(query_taps):
-            tap = taps_ref[0, u, t] * SCALE
-            if u == 0 and t == rim:
-                tap = tap + SCALE
-            terms = scores[u] * tap if terms is None else terms + scores[u] * tap
-        if t != rim:
-            terms = pltpu.roll(terms, (t - rim) % GROUP, 1)
-        conv = terms if conv is None else conv + terms
-    inside = (col >= block) & (col < block + keys) & (col >= start_ref[8 : 8 + BAND, :])
-    logits = jnp.where(inside & (behind >= 0) & (behind < REACH), conv, MASKED)
-    absorb([(rows, logits, vx_ref[pl.ds(low, GROUP), :])], state_ref, state_ref)
+            both = [products[(m * query_taps + u) * half :][:half] for m in (0, 1)]
+            allowed = (behind >= u) & (col >= start_ref[n, 8 - u : 8 - u + half, :])
+            scores.append(jnp.where(allowed, jnp.where(left, *both), 0.0))
+        conv = None
+        for t in range(key_taps):
+            terms = None
+            for u in range(query_taps):
+                tap = taps_ref[0, u, t] * SCALE
+                if u == 0 and t == rim:
+                    tap = tap + SCALE
+                terms = scores[u] * tap if terms is None else terms + scores[u] * tap
+            if t != rim:
+                terms = pltpu.roll(terms, (t - rim) % GROUP, 1)
+            conv = terms if conv is None else conv + terms
+        inside = (col >= block) & (col < block + keys) & (col >= start_ref[n, 8 : 8 + half, :])
+        inside = inside & (behind >= 0) & (behind < REACH)
+        logits = jnp.concatenate(
+            [
+                jnp.where(inside & left, conv, MASKED),
+                jnp.where(inside & jnp.logical_not(left), conv, MASKED),
+            ],
+            axis=0,
+        )
+        done.append((rows, logits, values))
+    absorb(done, state_ref, state_ref)
 
 
 def convolve(local, block, first_start, ends, qp_ref, kx_ref, kp_ref):
@@ -272,13 +301,15 @@
     state_ref[:, 2 * HEAD_DIM :] = jnp.where(lane < 64, FLOOR, 0.0)
     lay_keys(a_ref, b_ref, kx_ref, vx_ref)
 
-    @pl.loop(0, keys // BAND + 1)
-    def _(tile):
-        a = tile * BAND
-
-        @pl.when(block - chip_row + a < count)
-        def _():
-            near(a, chip_row, block, ends, taps_ref, qp_ref, kx_ref, vx_ref, start_ref, state_ref)
+    rest = (chip_row, block, ends, taps_ref, qp_ref, kx_ref, vx_ref, start_ref, state_ref)
+
+    @pl.loop(0, keys // (BAND * TILES))
+    def _(step):
+        near([(step * TILES + n) * BAND for n in range(TILES)], *rest)
+
+    @pl.when(block + keys - chip_row < count)
+    def _():
+        near([keys], *rest)
 
     convolve(True, block, 0, ends, qp_ref, kx_ref, kp_ref)
     far(chip_row, block, ends, qp_ref, kp_ref, vx_ref, state_ref, state_ref)
@@ -311,7 +342,7 @@
             @pl.when(block + keys == chip_row)
             def _():
                 near(
-                    keys, chip_row, block, ends, taps_ref, qp_ref, kx_ref, vx_ref, start_ref,
+                    [keys], chip_row, block, ends, taps_ref, qp_ref, kx_ref, vx_ref, start_ref,
                     state_ref,
                 )
 
@@ -358,7 +389,7 @@
         in_specs=specs,
         out_specs=[VMEM] * len(shapes),
         scratch_shapes=scratch,
-        cost_estimate=pl.CostEstimate(flops=flops, bytes_accessed=4 << 20, transcendentals=0),
+        cost_estimate=pl.CostEstimate(flops=8 * flops, bytes_accessed=4 << 20, transcendentals=0),
         compiler_params=pltpu.CompilerParams(vmem_limit_bytes=20 << 20),
     )(*args)
 
@@ -391,8 +422,8 @@
     sibling = permute(
         jnp.concatenate([queries, behind[HALO:]]), [(i, i ^ 1) for i in range(count)]
     )
-    ring_a = jnp.concatenate([key_vectors, behind[:HALO], beyond])
-    ring_b = jnp.concatenate([values, other_values])
+    ring_a = key_vectors
+    ring_b = jnp.concatenate([values, other_values, behind[:HALO], beyond])
     chip = group // 2
 
     def place(hop):
@@ -402,9 +433,9 @@
     state = [((2 * rows, 3 * HEAD_DIM), f32)]
     mark = [((8, 128), f32)]
     scratch = [
-        pltpu.VMEM((BAND + 8, GROUP), jnp.int32),
+        pltpu.VMEM((TILES, BAND // 2 + 8, GROUP), jnp.int32),
         pltpu.VMEM((rows + 128, HEAD_DIM), bf16),
-        pltpu.VMEM((rows + 2 * HALO, 2 * HEAD_DIM), bf16),
+        pltpu.VMEM((rows + 128, 2 * HEAD_DIM), bf16),
         pltpu.VMEM((rows, 2 * width), bf16),
     ]
     flops = 2 * 2 * rows * rows * (2 * width + 2 * HEAD_DIM)
@@ -416,7 +447,7 @@
         + mark,
         [pltpu.VMEM((2 * rows + HALO, HEAD_DIM), f32)] + scratch,
         (place(0), kernel, queries, sibling, behind, ring_a, ring_b),
-        flops=flops,
+        flops=8 * flops,
     )
     for hop in range(1, HOPS + 1):
         ring_a, ring_b = onward(ring_a), onward(ring_b)
@@ -431,7 +462,7 @@
             out,
             scratch + extra,
             (place(hop), kernel, operand, ring_a, ring_b, running),
-            flops=flops,
+            flops=8 * flops,
         )
         if not last:
             running, done = result

time: 90.6 us -> 90.7 us (level)
  waiting for transfers between devices: 8.87 us -> 19.4 us
  starting transfers between devices: 54.8 us -> 49.1 us
  Pallas kernels: 16.7 us -> 13.4 us
  local copies, waits for them, and re-layouts: 6.55 us -> 3.93 us
  other arithmetic: 2.74 us -> 4.05 us
    ppermute x12, waiting for transfers between devices: 3.52 us -> 13.5 us  [permute(): return lax.ppermute(value, 'ctx', pairs)]
    ppermute x12, starting transfers between devices: 50.1 us -> 43.3 us  [permute(): return lax.ppermute(value, 'ctx', pairs)]
    pallas_call x7, Pallas kernels: 16.7 us -> 13.4 us  [call(): pl.pallas_call(kernel, out_shape=shapes, in_specs=specs, out_specs=[VMEM]...]
    unnamed x14 -> x9, local copies, waits for them, and re-layouts: 5.14 us -> 2.5 us
    concatenate x3, other arithmetic: 0.9 us -> 2.2 us  [place(): jnp.concatenate([head, doc_lengths[:7], core[None]]).astype(jnp.int32)]
    ppermute x2, starting transfers between devices: 4.66 us -> 5.74 us  [partner(): lax.ppermute(value, 'head', [(i, i ^ heads // 2) for i in range(heads)])]
  transfers between devices with their start and end apart: 14 -> 14, of which waited for: 3 -> 4; matrix products, arithmetic and copies ran while one was open for 5% -> 7% of each run, Pallas kernels for 16% -> 12%
where the time goes in v4:
time: 90.7 us; the launch traced here: 90.1 us
  starting transfers between devices  49.1 us (54%)
  waiting for transfers between devices  19.4 us (21%)
  Pallas kernels  13.4 us (15%)
  other arithmetic  4.05 us (4%)
  local copies, waits for them, and re-layouts  3.93 us (4%)
    ppermute x12, starting transfers between devices, permute(): return lax.ppermute(value, 'ctx', pairs)  43.3 us
    ppermute x12, waiting for transfers between devices, permute(): return lax.ppermute(value, 'ctx', pairs)  13.5 us
    pallas_call x7, Pallas kernels, call(): pl.pallas_call(kernel, out_shape=shapes, in_specs=specs, out_specs=[VMEM]...  13.4 us
    ppermute x2, waiting for transfers between devices, partner(): lax.ppermute(value, 'head', [(i, i ^ heads // 2) for i in range(heads)])  5.97 us
    ppermute x2, starting transfers between devices, partner(): lax.ppermute(value, 'head', [(i, i ^ heads // 2) for i in range(heads)])  5.74 us
    unnamed x9, local copies, waits for them, and re-layouts  2.5 us
    concatenate x3, other arithmetic, place(): jnp.concatenate([head, doc_lengths[:7], core[None]]).astype(jnp.int32)  2.2 us
  transfers between devices with their start and end apart: 14, of which 4 were waited for; matrix products, arithmetic and copies ran while one was open for 7% of the time, Pallas kernels for 12%

profile of v4, /device:TPU:1, one launch (start us, length us, event | category | flops | bytes accessed | tf_op | source)
XLA Modules:
  0.0 90.1 jit_solution(5202585042803954845)
XLA Ops:
  0.0 4.8 %collective-permute-start.4 = (bf16[512,128]{1,0:T(8,128)(2,1)}, bf16[512,128]{1,0:T(8,128)(2,1)S(1)}, u32[]{:S(2)}, u32[]{:S(2)}) collective-permute-start(bf16[512,128]{1,0:T(8,128)(2,1)} %a_ref.1), channel_id=1, source_target_pairs={{0,64},{32,96},{64,128},{96,160},{128,192},{160,224},{192,256},{22... | collective-permute-start | bytes 393224 | tf_op jit(solution)/shard_map/ppermute | solution.py:408
  4.8 0.7 fusion
  5.6 0.7 slice.24
  6.3 2.9 %collective-permute-start = (bf16[32,128]{1,0:T(8,128)(2,1)S(1)}, bf16[32,128]{1,0:T(8,128)(2,1)S(1)}, u32[]{:S(2)}, u32[]{:S(2)}) collective-permute-start(bf16[32,128]{1,0:T(8,128)(2,1)S(1)} %pad_maximum_fusion.2), channel_id=1, source_target_pairs={{0,32},{32,64},{64,96},{96,128},{128,160},{160,192},{192,224},{224... | collective-permute-start | bytes 24584 | tf_op jit(solution)/shard_map/ppermute | solution.py:408
  9.2 1.0 %collective-permute-start.3 = (bf16[16,128]{1,0:T(8,128)(2,1)S(1)}, bf16[16,128]{1,0:T(8,128)(2,1)S(1)}, u32[]{:S(2)}, u32[]{:S(2)}) collective-permute-start(bf16[16,128]{1,0:T(8,128)(2,1)S(1)} %get-tuple-element.47), channel_id=1, source_target_pairs={{0,480},{32,0},{64,32},{96,64},{128,96},{160,128},{192,160},{224,1... | collective-permute-start | bytes 12296 | tf_op jit(solution)/shard_map/ppermute | solution.py:408
  10.2 3.6 %collective-permute-start.2 = (bf16[512,128]{1,0:T(8,128)(2,1)}, bf16[512,128]{1,0:T(8,128)(2,1)S(1)}, u32[]{:S(2)}, u32[]{:S(2)}) collective-permute-start(bf16[512,128]{1,0:T(8,128)(2,1)} %param.9), channel_id=1, source_target_pairs={{0,16},{1,17},{2,18},{3,19},{4,20},{5,21},{6,22},{7,23},{8,24},{9,... | collective-permute-start | bytes 393224 | tf_op jit(solution)/shard_map/ppermute | solution.py:414
  13.9 0.7 add_add_fusion.4
  14.6 0.7 add_add_fusion.3
  15.4 0.7 add_add_fusion.place_ref
  16.1 0.7 copy.12.taps_ref
  16.8 0.0 collective-permute-done.edge_ref
  16.8 0.9 %pad_maximum_fusion.1 = bf16[528,128]{1,0:T(8,128)(2,1)S(1)} fusion(bf16[16,128]{1,0:T(8,128)(2,1)S(1)} %get-tuple-element.50, bf16[512,128]{1,0:T(8,128)(2,1)} %own_ref.1), kind=kLoop, calls=%fused_computation.1 | loop fusion | flops 270336 | bytes 270336 | tf_op jit(solution)/shard_map/concatenate | solution.py:423
  17.7 6.3 %collective-permute-start.1 = (bf16[528,128]{1,0:T(8,128)(2,1)S(1)}, bf16[528,128]{1,0:T(8,128)(2,1)S(1)}, u32[]{:S(2)}, u32[]{:S(2)}) collective-permute-start(bf16[528,128]{1,0:T(8,128)(2,1)S(1)} %pad_maximum_fusion.1), channel_id=1, source_target_pairs={{0,32},{32,0},{64,96},{96,64},{128,160},{160,128},{192,224},{224,1... | collective-permute-start | bytes 405512 | tf_op jit(solution)/shard_map/ppermute | solution.py:408
  24.0 0.0 collective-permute-done.3
  24.0 0.0 collective-permute-done.2
  24.1 0.9 %pad_maximum_fusion.b_ref = bf16[1056,128]{1,0:T(8,128)(2,1)S(1)} fusion(bf16[16,128]{1,0:T(8,128)(2,1)S(1)} %collective-permute-done.3, bf16[16,128]{1,0:T(8,128)(2,1)S(1)} %get-tuple-element.49, bf16[512,128]{1,0:T(8,128)(2,1)S(1)} %collective-permute-done.2, bf16[512,128]{1,0:T(8,128)(2,1)} %param.9), kind=kLoop, calls=%fused_computation | loop fusion | flops 1081344 | bytes 540672 | tf_op jit(solution)/shard_map/concatenate | solution.py:426
  25.0 1.9 %collective-permute-start.6 = (bf16[1056,128]{1,0:T(8,128)(2,1)S(1)}, bf16[1056,128]{1,0:T(8,128)(2,1)S(1)}, u32[]{:S(2)}, u32[]{:S(2)}) collective-permute-start(bf16[1056,128]{1,0:T(8,128)(2,1)S(1)} %pad_maximum_fusion.b_ref), channel_id=1, source_target_pairs={{0,64},{32,96},{64,128},{96,160},{128,192},{160,224},{192,256},{22... | collective-permute-start | bytes 811016 | tf_op jit(solution)/shard_map/ppermute | solution.py:408
  26.9 0.0 collective-permute-done.1.other_ref
  26.9 0.0 copy-start
  26.9 0.9 copy-done
  27.8 0.0 copy-start.1
  27.8 0.9 %copy-done.1 = bf16[512,128]{1,0:T(8,128)(2,1)S(1)} copy-done((bf16[512,128]{1,0:T(8,128)(2,1)S(1)}, bf16[512,128]{1,0:T(8,128)(2,1)}, u32[]{:S(2)}) %copy-start.1) | copy-done | bytes 131096
  28.7 6.7 %shard_map.73 = (bf16[1536,768]{1,0:T(8,128)(2,1)S(1)}, f32[1024,384]{1,0:T(8,128)S(1)}, f32[8,128]{1,0:T(8,128)}) custom-call(s32[10]{0:T(128)S(1)} %get-tuple-element.52.place_ref, f32[1,6,11]{2,1,0:T(8,128)S(1)} %copy.12.taps_ref, bf16[512,128]{1,0:T(8,128)(2,1)S(1)} %copy-done, bf16[528,128]{1,0:T(8,128)(2,1)S(1)} %collective-permute-done.1.other_ref, ...), custom_call_target="tpu_custom_call" | custom-call | flops 120259084288 | bytes 4194304 | tf_op jit(solution)/shard_map/pallas_call | solution.py:386
  35.4 0.0 collective-permute-done.4.a_ref
  35.4 2.5 %collective-permute-start.5 = (bf16[512,128]{1,0:T(8,128)(2,1)S(1)}, bf16[512,128]{1,0:T(8,128)(2,1)S(1)}, u32[]{:S(2)}, u32[]{:S(2)}) collective-permute-start(bf16[512,128]{1,0:T(8,128)(2,1)S(1)} %collective-permute-done.4.a_ref), channel_id=1, source_target_pairs={{0,64},{32,96},{64,128},{96,160},{128,192},{160,224},{192,256},{22... | collective-permute-start | bytes 393224 | tf_op jit(solution)/shard_map/ppermute | solution.py:408
  37.9 0.0 collective-permute-done.6.b_ref
  38.0 4.0 %collective-permute-start.8 = (bf16[1056,128]{1,0:T(8,128)(2,1)S(1)}, bf16[1056,128]{1,0:T(8,128)(2,1)S(1)}, u32[]{:S(2)}, u32[]{:S(2)}) collective-permute-start(bf16[1056,128]{1,0:T(8,128)(2,1)S(1)} %collective-permute-done.6.b_ref), channel_id=1, source_target_pairs={{0,64},{32,96},{64,128},{96,160},{128,192},{160,224},{192,256},{22... | collective-permute-start | bytes 811016 | tf_op jit(solution)/shard_map/ppermute | solution.py:408
  42.0 1.3 %shard_map.74 = (f32[1024,384]{1,0:T(8,128)S(1)}, f32[8,128]{1,0:T(8,128)}) custom-call(s32[10]{0:T(128)S(1)} %get-tuple-element.54.place_ref, f32[1,6,11]{2,1,0:T(8,128)S(1)} %copy.12.taps_ref, bf16[1536,768]{1,0:T(8,128)(2,1)S(1)} %get-tuple-element.26.qp_ref, bf16[512,128]{1,0:T(8,128)(2,1)S(1)} %collective-permute-done.4.a_ref, ...), custom_call_target="tpu_custom_call" | custom-call | flops 120259084288 | bytes 4194304 | tf_op jit(solution)/shard_map/pallas_call | solution.py:386
  43.3 0.0 collective-permute-done.5.a_ref
  43.3 9.0 %collective-permute-start.7 = (bf16[512,128]{1,0:T(8,128)(2,1)S(1)}, bf16[512,128]{1,0:T(8,128)(2,1)S(1)}, u32[]{:S(2)}, u32[]{:S(2)}) collective-permute-start(bf16[512,128]{1,0:T(8,128)(2,1)S(1)} %collective-permute-done.5.a_ref), channel_id=1, source_target_pairs={{0,64},{32,96},{64,128},{96,160},{128,192},{160,224},{192,256},{22... | collective-permute-start | bytes 393224 | tf_op jit(solution)/shard_map/ppermute | solution.py:408
  52.3 0.0 collective-permute-done.8.b_ref
  52.3 2.3 %collective-permute-start.10 = (bf16[1056,128]{1,0:T(8,128)(2,1)S(1)}, bf16[1056,128]{1,0:T(8,128)(2,1)S(1)}, u32[]{:S(2)}, u32[]{:S(2)}) collective-permute-start(bf16[1056,128]{1,0:T(8,128)(2,1)S(1)} %collective-permute-done.8.b_ref), channel_id=1, source_target_pairs={{0,64},{32,96},{64,128},{96,160},{128,192},{160,224},{192,256},{22... | collective-permute-start | bytes 811016 | tf_op jit(solution)/shard_map/ppermute | solution.py:408
  54.6 1.3 %shard_map.75 = (f32[1024,384]{1,0:T(8,128)S(1)}, f32[8,128]{1,0:T(8,128)}) custom-call(s32[10]{0:T(128)S(1)} %get-tuple-element.53.place_ref, f32[1,6,11]{2,1,0:T(8,128)S(1)} %copy.12.taps_ref, bf16[1536,768]{1,0:T(8,128)(2,1)S(1)} %get-tuple-element.26.qp_ref, bf16[512,128]{1,0:T(8,128)(2,1)S(1)} %collective-permute-done.5.a_ref, ...), custom_call_target="tpu_custom_call" | custom-call | flops 120259084288 | bytes 4194304 | tf_op jit(solution)/shard_map/pallas_call | solution.py:386
  55.9 0.0 collective-permute-done.7.a_ref
  55.9 2.7 %collective-permute-start.9 = (bf16[512,128]{1,0:T(8,128)(2,1)S(1)}, bf16[512,128]{1,0:T(8,128)(2,1)S(1)}, u32[]{:S(2)}, u32[]{:S(2)}) collective-permute-start(bf16[512,128]{1,0:T(8,128)(2,1)S(1)} %collective-permute-done.7.a_ref), channel_id=1, source_target_pairs={{0,64},{32,96},{64,128},{96,160},{128,192},{160,224},{192,256},{22... | collective-permute-start | bytes 393224 | tf_op jit(solution)/shard_map/ppermute | solution.py:408
  58.6 5.0 %collective-permute-done.10.b_ref = bf16[1056,128]{1,0:T(8,128)(2,1)S(1)} collective-permute-done((bf16[1056,128]{1,0:T(8,128)(2,1)S(1)}, bf16[1056,128]{1,0:T(8,128)(2,1)S(1)}, u32[]{:S(2)}, u32[]{:S(2)}) %collective-permute-start.10) | collective-permute-done | bytes 270368 | tf_op jit(solution)/shard_map/ppermute | solution.py:408
  63.6 1.9 %collective-permute-start.11 = (bf16[1056,128]{1,0:T(8,128)(2,1)S(1)}, bf16[1056,128]{1,0:T(8,128)(2,1)S(1)}, u32[]{:S(2)}, u32[]{:S(2)}) collective-permute-start(bf16[1056,128]{1,0:T(8,128)(2,1)S(1)} %collective-permute-done.10.b_ref), channel_id=1, source_target_pairs={{0,64},{32,96},{64,128},{96,160},{128,192},{160,224},{192,256},{22... | collective-permute-start | bytes 811016 | tf_op jit(solution)/shard_map/ppermute | solution.py:408
  65.5 1.5 %shard_map.76 = (f32[1024,384]{1,0:T(8,128)S(1)}, f32[8,128]{1,0:T(8,128)}) custom-call(s32[10]{0:T(128)S(1)} %get-tuple-element.51.place_ref, f32[1,6,11]{2,1,0:T(8,128)S(1)} %copy.12.taps_ref, bf16[1536,768]{1,0:T(8,128)(2,1)S(1)} %get-tuple-element.26.qp_ref, bf16[512,128]{1,0:T(8,128)(2,1)S(1)} %collective-permute-done.7.a_ref, ...), custom_call_target="tpu_custom_call" | custom-call | flops 120259084288 | bytes 4194304 | tf_op jit(solution)/shard_map/pallas_call | solution.py:386
  67.0 0.0 collective-permute-done.9.a_ref
  67.0 6.6 %collective-permute-done.11.b_ref = bf16[1056,128]{1,0:T(8,128)(2,1)S(1)} collective-permute-done((bf16[1056,128]{1,0:T(8,128)(2,1)S(1)}, bf16[1056,128]{1,0:T(8,128)(2,1)S(1)}, u32[]{:S(2)}, u32[]{:S(2)}) %collective-permute-start.11) | collective-permute-done | bytes 270368 | tf_op jit(solution)/shard_map/ppermute | solution.py:408
  73.6 0.8 shard_map.77
  74.4 0.0 copy-start.2
  74.4 0.0 copy-start.3
  74.4 3.9 %collective-permute-start.12 = (f32[512,384]{1,0:T(8,128)S(1)}, f32[512,384]{1,0:T(8,128)S(1)}, u32[]{:S(2)}, u32[]{:S(2)}) collective-permute-start(f32[512,384]{1,0:T(8,128)S(1)} %get-tuple-element.44), channel_id=1, source_target_pairs={{0,32},{32,0},{64,96},{96,64},{128,160},{160,128},{192,224},{224,1... | collective-permute-start | bytes 2359304 | tf_op jit(solution)/shard_map/ppermute | solution.py:408
  78.3 1.9 %collective-permute-done.12.other_ref = f32[512,384]{1,0:T(8,128)S(1)} collective-permute-done((f32[512,384]{1,0:T(8,128)S(1)}, f32[512,384]{1,0:T(8,128)S(1)}, u32[]{:S(2)}, u32[]{:S(2)}) %collective-permute-start.12) | collective-permute-done | bytes 786464 | tf_op jit(solution)/shard_map/ppermute | solution.py:408
  80.2 0.4 shard_map.78
  80.7 2.1 %collective-permute-start.13 = (bf16[512,128]{1,0:T(8,128)(2,1)S(1)}, bf16[512,128]{1,0:T(8,128)(2,1)S(1)}, u32[]{:S(2)}, u32[]{:S(2)}) collective-permute-start(bf16[512,128]{1,0:T(8,128)(2,1)S(1)} %get-tuple-element.46), channel_id=1, source_target_pairs={{0,16},{1,17},{2,18},{3,19},{4,20},{5,21},{6,22},{7,23},{8,24},{9,... | collective-permute-start | bytes 393224 | tf_op jit(solution)/shard_map/ppermute | solution.py:414
  82.8 6.0 %collective-permute-done.13.cross_ref = bf16[512,128]{1,0:T(8,128)(2,1)S(1)} collective-permute-done((bf16[512,128]{1,0:T(8,128)(2,1)S(1)}, bf16[512,128]{1,0:T(8,128)(2,1)S(1)}, u32[]{:S(2)}, u32[]{:S(2)}) %collective-permute-start.13) | collective-permute-done | bytes 131104 | tf_op jit(solution)/shard_map/ppermute | solution.py:414
  88.8 0.0 copy-done.2
  88.8 0.0 copy-done.3
  88.8 1.4 %shard_map.79 = bf16[512,128]{1,0:T(8,128)(2,1)} custom-call(f32[2]{0:T(128)S(1)} %bitcast.10, f32[512,128]{1,0:T(8,128)S(1)} %get-tuple-element.45.own_ref, bf16[512,128]{1,0:T(8,128)(2,1)S(1)} %collective-permute-done.13.cross_ref, f32[1,128]{1,0:T(1,128)S(1)} %bitcast.11), custom_call_target="tpu_custom_call" | custom-call | bytes 4194304 | tf_op jit(solution)/shard_map/pallas_call | solution.py:386
  (2 shorter events, 0.0 us)
Async XLA Ops:
  0.0 35.4 %collective-permute-start.4 = (bf16[512,128]{1,0:T(8,128)(2,1)}, bf16[512,128]{1,0:T(8,128)(2,1)S(1)}, u32[]{:S(2)}, u32[]{:S(2)}) collective-permute-start(bf16[512,128]{1,0:T(8,128)(2,1)} %a_ref.1), channel_id=1, source_target_pairs={{0,64},{32,96},{64,128},{96,160},{128,192},{160,224},{192,256},{22... | collective-permute-start | bytes 393224 | tf_op jit(solution)/shard_map/ppermute | solution.py:408
  6.3 10.5 %collective-permute-start = (bf16[32,128]{1,0:T(8,128)(2,1)S(1)}, bf16[32,128]{1,0:T(8,128)(2,1)S(1)}, u32[]{:S(2)}, u32[]{:S(2)}) collective-permute-start(bf16[32,128]{1,0:T(8,128)(2,1)S(1)} %pad_maximum_fusion.2), channel_id=1, source_target_pairs={{0,32},{32,64},{64,96},{96,128},{128,160},{160,192},{192,224},{224... | collective-permute-start | bytes 24584 | tf_op jit(solution)/shard_map/ppermute | solution.py:408
  9.2 14.8 %collective-permute-start.3 = (bf16[16,128]{1,0:T(8,128)(2,1)S(1)}, bf16[16,128]{1,0:T(8,128)(2,1)S(1)}, u32[]{:S(2)}, u32[]{:S(2)}) collective-permute-start(bf16[16,128]{1,0:T(8,128)(2,1)S(1)} %get-tuple-element.47), channel_id=1, source_target_pairs={{0,480},{32,0},{64,32},{96,64},{128,96},{160,128},{192,160},{224,1... | collective-permute-start | bytes 12296 | tf_op jit(solution)/shard_map/ppermute | solution.py:408
  10.2 13.8 %collective-permute-start.2 = (bf16[512,128]{1,0:T(8,128)(2,1)}, bf16[512,128]{1,0:T(8,128)(2,1)S(1)}, u32[]{:S(2)}, u32[]{:S(2)}) collective-permute-start(bf16[512,128]{1,0:T(8,128)(2,1)} %param.9), channel_id=1, source_target_pairs={{0,16},{1,17},{2,18},{3,19},{4,20},{5,21},{6,22},{7,23},{8,24},{9,... | collective-permute-start | bytes 393224 | tf_op jit(solution)/shard_map/ppermute | solution.py:414
  17.7 9.2 %collective-permute-start.1 = (bf16[528,128]{1,0:T(8,128)(2,1)S(1)}, bf16[528,128]{1,0:T(8,128)(2,1)S(1)}, u32[]{:S(2)}, u32[]{:S(2)}) collective-permute-start(bf16[528,128]{1,0:T(8,128)(2,1)S(1)} %pad_maximum_fusion.1), channel_id=1, source_target_pairs={{0,32},{32,0},{64,96},{96,64},{128,160},{160,128},{192,224},{224,1... | collective-permute-start | bytes 405512 | tf_op jit(solution)/shard_map/ppermute | solution.py:408
  25.0 13.0 %collective-permute-start.6 = (bf16[1056,128]{1,0:T(8,128)(2,1)S(1)}, bf16[1056,128]{1,0:T(8,128)(2,1)S(1)}, u32[]{:S(2)}, u32[]{:S(2)}) collective-permute-start(bf16[1056,128]{1,0:T(8,128)(2,1)S(1)} %pad_maximum_fusion.b_ref), channel_id=1, source_target_pairs={{0,64},{32,96},{64,128},{96,160},{128,192},{160,224},{192,256},{22... | collective-permute-start | bytes 811016 | tf_op jit(solution)/shard_map/ppermute | solution.py:408
  26.9 0.9 %copy-start = (bf16[512,128]{1,0:T(8,128)(2,1)S(1)}, bf16[512,128]{1,0:T(8,128)(2,1)}, u32[]{:S(2)}) copy-start(bf16[512,128]{1,0:T(8,128)(2,1)} %own_ref.1) | copy-start | bytes 393220
  27.8 0.9 %copy-start.1 = (bf16[512,128]{1,0:T(8,128)(2,1)S(1)}, bf16[512,128]{1,0:T(8,128)(2,1)}, u32[]{:S(2)}) copy-start(bf16[512,128]{1,0:T(8,128)(2,1)} %a_ref.1) | copy-start | bytes 393220
  35.4 7.9 %collective-permute-start.5 = (bf16[512,128]{1,0:T(8,128)(2,1)S(1)}, bf16[512,128]{1,0:T(8,128)(2,1)S(1)}, u32[]{:S(2)}, u32[]{:S(2)}) collective-permute-start(bf16[512,128]{1,0:T(8,128)(2,1)S(1)} %collective-permute-done.4.a_ref), channel_id=1, source_target_pairs={{0,64},{32,96},{64,128},{96,160},{128,192},{160,224},{192,256},{22... | collective-permute-start | bytes 393224 | tf_op jit(solution)/shard_map/ppermute | solution.py:408
  38.0 14.3 %collective-permute-start.8 = (bf16[1056,128]{1,0:T(8,128)(2,1)S(1)}, bf16[1056,128]{1,0:T(8,128)(2,1)S(1)}, u32[]{:S(2)}, u32[]{:S(2)}) collective-permute-start(bf16[1056,128]{1,0:T(8,128)(2,1)S(1)} %collective-permute-done.6.b_ref), channel_id=1, source_target_pairs={{0,64},{32,96},{64,128},{96,160},{128,192},{160,224},{192,256},{22... | collective-permute-start | bytes 811016 | tf_op jit(solution)/shard_map/ppermute | solution.py:408
  43.3 12.6 %collective-permute-start.7 = (bf16[512,128]{1,0:T(8,128)(2,1)S(1)}, bf16[512,128]{1,0:T(8,128)(2,1)S(1)}, u32[]{:S(2)}, u32[]{:S(2)}) collective-permute-start(bf16[512,128]{1,0:T(8,128)(2,1)S(1)} %collective-permute-done.5.a_ref), channel_id=1, source_target_pairs={{0,64},{32,96},{64,128},{96,160},{128,192},{160,224},{192,256},{22... | collective-permute-start | bytes 393224 | tf_op jit(solution)/shard_map/ppermute | solution.py:408
  52.3 11.3 %collective-permute-start.10 = (bf16[1056,128]{1,0:T(8,128)(2,1)S(1)}, bf16[1056,128]{1,0:T(8,128)(2,1)S(1)}, u32[]{:S(2)}, u32[]{:S(2)}) collective-permute-start(bf16[1056,128]{1,0:T(8,128)(2,1)S(1)} %collective-permute-done.8.b_ref), channel_id=1, source_target_pairs={{0,64},{32,96},{64,128},{96,160},{128,192},{160,224},{192,256},{22... | collective-permute-start | bytes 811016 | tf_op jit(solution)/shard_map/ppermute | solution.py:408
  55.9 11.0 %collective-permute-start.9 = (bf16[512,128]{1,0:T(8,128)(2,1)S(1)}, bf16[512,128]{1,0:T(8,128)(2,1)S(1)}, u32[]{:S(2)}, u32[]{:S(2)}) collective-permute-start(bf16[512,128]{1,0:T(8,128)(2,1)S(1)} %collective-permute-done.7.a_ref), channel_id=1, source_target_pairs={{0,64},{32,96},{64,128},{96,160},{128,192},{160,224},{192,256},{22... | collective-permute-start | bytes 393224 | tf_op jit(solution)/shard_map/ppermute | solution.py:408
  63.6 10.0 %collective-permute-start.11 = (bf16[1056,128]{1,0:T(8,128)(2,1)S(1)}, bf16[1056,128]{1,0:T(8,128)(2,1)S(1)}, u32[]{:S(2)}, u32[]{:S(2)}) collective-permute-start(bf16[1056,128]{1,0:T(8,128)(2,1)S(1)} %collective-permute-done.10.b_ref), channel_id=1, source_target_pairs={{0,64},{32,96},{64,128},{96,160},{128,192},{160,224},{192,256},{22... | collective-permute-start | bytes 811016 | tf_op jit(solution)/shard_map/ppermute | solution.py:408
  74.4 14.4 %copy-start.2 = (f32[1,2]{1,0:T(1,128)S(1)}, f32[1,2]{1,0:T(1,128)}, u32[]{:S(2)}) copy-start(f32[1,2]{1,0:T(1,128)} %param.11) | copy-start | bytes 28
  74.4 14.3 %copy-start.3 = (f32[128]{0:T(128)S(1)}, f32[128]{0:T(128)}, u32[]{:S(2)}) copy-start(f32[128]{0:T(128)} %param.12) | copy-start | bytes 1540
  74.4 5.8 %collective-permute-start.12 = (f32[512,384]{1,0:T(8,128)S(1)}, f32[512,384]{1,0:T(8,128)S(1)}, u32[]{:S(2)}, u32[]{:S(2)}) collective-permute-start(f32[512,384]{1,0:T(8,128)S(1)} %get-tuple-element.44), channel_id=1, source_target_pairs={{0,32},{32,0},{64,96},{96,64},{128,160},{160,128},{192,224},{224,1... | collective-permute-start | bytes 2359304 | tf_op jit(solution)/shard_map/ppermute | solution.py:408
  80.7 8.1 %collective-permute-start.13 = (bf16[512,128]{1,0:T(8,128)(2,1)S(1)}, bf16[512,128]{1,0:T(8,128)(2,1)S(1)}, u32[]{:S(2)}, u32[]{:S(2)}) collective-permute-start(bf16[512,128]{1,0:T(8,128)(2,1)S(1)} %get-tuple-element.46), channel_id=1, source_target_pairs={{0,16},{1,17},{2,18},{3,19},{4,20},{5,21},{6,22},{7,23},{8,24},{9,... | collective-permute-start | bytes 393224 | tf_op jit(solution)/shard_map/ppermute | solution.py:414

commit v5 on v4

--- a/solution.py
+++ b/solution.py
@@ -66,9 +66,10 @@
 
 
 def lay_keys(a_ref, b_ref, kx_ref, vx_ref):
-    keys = a_ref.shape[0]
+    keys = kx_ref.shape[0] - 128
     kx_ref[0:HALO, :] = b_ref[2 * keys : 2 * keys + HALO, :]
-    kx_ref[HALO : HALO + keys, :] = a_ref[...]
+    if a_ref is not None:
+        kx_ref[HALO : HALO + keys, :] = a_ref[...]
     kx_ref[HALO + keys : 2 * HALO + keys, :] = b_ref[2 * keys + HALO :, :]
     kx_ref[2 * HALO + keys :, :] = jnp.zeros_like(kx_ref[2 * HALO + keys :, :])
     vx_ref[0:HALO, :] = jnp.zeros((HALO, 2 * HEAD_DIM), jnp.bfloat16)
@@ -79,7 +80,7 @@
 
 def near(tiles, chip_row, block, ends, taps_ref, qp_ref, kx_ref, vx_ref, start_ref, state_ref):
     keys = kx_ref.shape[0] - 128
-    query_taps, key_taps = taps_ref.shape[1:]
+    query_taps, _, key_taps = taps_ref.shape
     rim = (key_taps - 1) // 2
     half = BAND // 2
     shape = (half, GROUP)
@@ -133,7 +134,7 @@
         for t in range(key_taps):
             terms = None
             for u in range(query_taps):
-                tap = taps_ref[0, u, t] * SCALE
+                tap = taps_ref[u, 0, t] * SCALE
                 if u == 0 and t == rim:
                     tap = tap + SCALE
                 terms = scores[u] * tap if terms is None else terms + scores[u] * tap
@@ -212,22 +213,23 @@
     whole()
 
 
-def far(chip_row, block, ends, qp_ref, kp_ref, vx_ref, source_ref, state_ref):
+def far(tiles_at_once, chip_row, block, ends, qp_ref, kp_ref, vx_ref, source_ref, state_ref):
     keys = kp_ref.shape[0]
     width = qp_ref.shape[1]
-
-    @pl.loop(0, state_ref.shape[0] // (2 * WIDE))
+    span = tiles_at_once * WIDE
+
+    @pl.loop(0, state_ref.shape[0] // span)
     def _(tile):
-        first = tile * 2 * WIDE
+        first = tile * span
         top = chip_row + first
-        needed = (top + 2 * WIDE - 1 >= block + REACH) & (block + keys > starts_of(top, ends))
+        needed = (top + span - 1 >= block + REACH) & (block + keys > starts_of(top, ends))
 
         @pl.when(needed)
         def _():
             tiles = []
             shape = (WIDE, GROUP)
             col = lax.broadcasted_iota(jnp.int32, (WIDE, keys), 1)
-            for half in (0, WIDE):
+            for half in range(0, span, WIDE):
                 rows = pl.ds(pl.multiple_of(first + half, WIDE), WIDE)
                 query = qp_ref[rows, :]
                 conv = dot_t(query, kp_ref[:, 0:width]) + dot_t(query, kp_ref[:, width:])
@@ -242,41 +244,44 @@
 
             @pl.when(jnp.logical_not(needed))
             def _():
-                rows = pl.ds(pl.multiple_of(first, WIDE), 2 * WIDE)
+                rows = pl.ds(pl.multiple_of(first, WIDE), span)
                 state_ref[rows, :] = source_ref[rows, :]
 
 
-def ends_of(place_ref):
-    ends = [place_ref[2]]
+def place_of(hop, rows, docs_ref):
+    group = lax.axis_index("ctx")
+    core = group & 1
+    chip = group >> 1
+    ends = [docs_ref[0]]
     for d in range(1, 7):
-        ends.append(ends[-1] + place_ref[2 + d])
-    return ends
+        ends.append(ends[-1] + docs_ref[d])
+    return chip * 2 * rows, core, (chip - hop) * 2 * rows + core * rows, ends
 
 
 def local_kernel(
-    place_ref, taps_ref, own_ref, other_ref, edge_ref, a_ref, b_ref,
+    docs_ref, taps_ref, own_ref, other_ref, edge_ref, a_ref, b_ref,
     qp_ref, state_ref, done_ref,
-    qx_ref, start_ref, kx_ref, vx_ref, kp_ref,
+    qx_ref, copied, start_ref, kx_ref, vx_ref, kp_ref,
 ):
-    chip_row, block = place_ref[0], place_ref[1]
-    core = place_ref[9]
-    ends = ends_of(place_ref)
     keys = kp_ref.shape[0]
-    taps, key_taps = taps_ref.shape[1:]
+    chip_row, core, block, ends = place_of(0, keys, docs_ref)
+    taken = pltpu.make_async_copy(a_ref, kx_ref.at[pl.ds(HALO, keys), :], copied)
+    taken.start()
+    taps, _, key_taps = taps_ref.shape
     rim = (key_taps - 1) // 2
     done_ref[...] = jnp.zeros(done_ref.shape, jnp.float32)
 
     @pl.when(core == 0)
     def _():
         qx_ref[0:HALO, :] = edge_ref[HALO:, :].astype(jnp.float32)
-        qx_ref[HALO : HALO + keys, :] = own_ref[...].astype(jnp.float32)
+        qx_ref[HALO : HALO + keys, :] = own_ref[0:keys, :].astype(jnp.float32)
         qx_ref[HALO + keys :, :] = other_ref[0:keys, :].astype(jnp.float32)
 
     @pl.when(core != 0)
     def _():
         qx_ref[0:HALO, :] = other_ref[keys:, :].astype(jnp.float32)
         qx_ref[HALO : HALO + keys, :] = other_ref[0:keys, :].astype(jnp.float32)
-        qx_ref[HALO + keys :, :] = own_ref[...].astype(jnp.float32)
+        qx_ref[HALO + keys :, :] = own_ref[0:keys, :].astype(jnp.float32)
 
     count = state_ref.shape[0]
     for u in range(taps):
@@ -287,7 +292,7 @@
     for u in range(taps):
         base = jnp.zeros(lane.shape, jnp.float32)
         for t in range(key_taps):
-            tap = taps_ref[0, u, t] * SCALE
+            tap = taps_ref[u, 0, t] * SCALE
             if u == 0 and t == rim:
                 tap = tap + SCALE
             base = jnp.where(lane == HALO + rim - t, tap, base)
@@ -299,8 +304,8 @@
     lane = lax.broadcasted_iota(jnp.int32, (count, 128), 1)
     state_ref[:, 0 : 2 * HEAD_DIM] = jnp.zeros((count, 2 * HEAD_DIM), jnp.float32)
     state_ref[:, 2 * HEAD_DIM :] = jnp.where(lane < 64, FLOOR, 0.0)
-    lay_keys(a_ref, b_ref, kx_ref, vx_ref)
-
+    lay_keys(None, b_ref, kx_ref, vx_ref)
+    taken.wait()
     rest = (chip_row, block, ends, taps_ref, qp_ref, kx_ref, vx_ref, start_ref, state_ref)
 
     @pl.loop(0, keys // (BAND * TILES))
@@ -312,18 +317,18 @@
         near([keys], *rest)
 
     convolve(True, block, 0, ends, qp_ref, kx_ref, kp_ref)
-    far(chip_row, block, ends, qp_ref, kp_ref, vx_ref, state_ref, state_ref)
-
-
-def hop_kernel(first, last, place_ref, taps_ref, qp_ref, a_ref, b_ref, state_in, *rest):
+    far(2, chip_row, block, ends, qp_ref, kp_ref, vx_ref, state_ref, state_ref)
+
+
+def hop_kernel(hop, last, docs_ref, taps_ref, qp_ref, a_ref, b_ref, state_in, *rest):
     if last:
         keep_ref, send_ref, start_ref, kx_ref, vx_ref, kp_ref, state_ref = rest
     else:
         state_ref, done_ref, start_ref, kx_ref, vx_ref, kp_ref = rest
         done_ref[...] = jnp.zeros(done_ref.shape, jnp.float32)
-    chip_row, block = place_ref[0], place_ref[1]
-    ends = ends_of(place_ref)
     keys = kp_ref.shape[0]
+    chip_row, core, block, ends = place_of(hop, keys, docs_ref)
+    first = hop == 1
     first_start = starts_of(chip_row, ends)
     active = block + keys > first_start
     if first:
@@ -348,10 +353,9 @@
 
         convolve(False, block, first_start, ends, qp_ref, kx_ref, kp_ref)
         source = state_ref if first else state_in
-        far(chip_row, block, ends, qp_ref, kp_ref, vx_ref, source, state_ref)
+        far(2 if last else 4, chip_row, block, ends, qp_ref, kp_ref, vx_ref, source, state_ref)
 
     if last:
-        core = place_ref[9]
         for ref, side in ((keep_ref, core), (send_ref, 1 - core)):
             ref[...] = state_ref[pl.ds(pl.multiple_of(side * keys, keys), keys), :]
 
@@ -399,8 +403,6 @@
     bf16, f32 = jnp.bfloat16, jnp.float32
     count = lax.axis_size("ctx")
     heads = lax.axis_size("head")
-    group = lax.axis_index("ctx")
-    core = group % 2
     taps = kernel.shape[1]
     width = taps * HEAD_DIM
 
@@ -419,17 +421,11 @@
     other_values = partner(values)
     beyond = step(key_vectors[:HALO], -1)
     behind = step(jnp.concatenate([key_vectors[rows - HALO :], queries[rows - HALO :]]), 1)
-    sibling = permute(
-        jnp.concatenate([queries, behind[HALO:]]), [(i, i ^ 1) for i in range(count)]
-    )
+    mine = jnp.concatenate([queries, behind[HALO:]])
+    sibling = permute(mine, [(i, i ^ 1) for i in range(count)])
+    by_tap = jnp.transpose(kernel, (1, 0, 2))
     ring_a = key_vectors
     ring_b = jnp.concatenate([values, other_values, behind[:HALO], beyond])
-    chip = group // 2
-
-    def place(hop):
-        head = jnp.stack([chip * 2 * rows, (chip - hop) * 2 * rows + core * rows])
-        return jnp.concatenate([head, doc_lengths[:7], core[None]]).astype(jnp.int32)
-
     state = [((2 * rows, 3 * HEAD_DIM), f32)]
     mark = [((8, 128), f32)]
     scratch = [
@@ -441,12 +437,12 @@
     flops = 2 * 2 * rows * rows * (2 * width + 2 * HEAD_DIM)
     operand, running, done = call(
         local_kernel,
-        [SMEM, SMEM] + [VMEM] * 5,
+        [SMEM, SMEM, VMEM, VMEM, VMEM, pl.BlockSpec(memory_space=pltpu.HBM), VMEM],
         [((2 * rows + 2 * taps * GROUP * 256 // width, width), bf16)]
         + state
         + mark,
-        [pltpu.VMEM((2 * rows + HALO, HEAD_DIM), f32)] + scratch,
-        (place(0), kernel, queries, sibling, behind, ring_a, ring_b),
+        [pltpu.VMEM((2 * rows + HALO, HEAD_DIM), f32), pltpu.SemaphoreType.DMA] + scratch,
+        (doc_lengths, by_tap, mine, sibling, behind, ring_a, ring_b),
         flops=8 * flops,
     )
     for hop in range(1, HOPS + 1):
@@ -457,11 +453,11 @@
         out = [((rows, 3 * HEAD_DIM), f32)] * 2 if last else state + mark
         extra = [pltpu.VMEM(shape, dtype) for shape, dtype in state] if last else []
         result = call(
-            functools.partial(hop_kernel, hop == 1, last),
+            functools.partial(hop_kernel, hop, last),
             [SMEM, SMEM] + [VMEM] * 4,
             out,
             scratch + extra,
-            (place(hop), kernel, operand, ring_a, ring_b, running),
+            (doc_lengths, by_tap, operand, ring_a, ring_b, running),
             flops=8 * flops,
         )
         if not last:

time: 90.7 us -> 88.7 us (0.978)
  starting transfers between devices: 49.1 us -> 55.3 us
  waiting for transfers between devices: 19.4 us -> 13.6 us
  other arithmetic: 4.05 us -> 1.85 us
    ppermute x2, starting transfers between devices: 5.74 us -> 9.8 us  [partner(): lax.ppermute(value, 'head', [(i, i ^ heads // 2) for i in range(heads)])]
    ppermute x12, waiting for transfers between devices: 13.5 us -> 10 us  [permute(): return lax.ppermute(value, 'ctx', pairs)]
    ppermute x2, waiting for transfers between devices: 5.97 us -> 3.56 us  [partner(): lax.ppermute(value, 'head', [(i, i ^ heads // 2) for i in range(heads)])]
    concatenate x4 -> x1, other arithmetic: 3.12 us -> 0.92 us  [body(): mine = jnp.concatenate([queries, behind[HALO:]])]
    ppermute x12, starting transfers between devices: 43.3 us -> 45.5 us  [permute(): return lax.ppermute(value, 'ctx', pairs)]
    unnamed x9 -> x10, local copies, waits for them, and re-layouts: 2.5 us -> 2.25 us
  transfers between devices with their start and end apart: 14 -> 14, of which waited for: 4 -> 5; matrix products, arithmetic and copies ran while one was open for 7% -> 2% of each run, Pallas kernels for 12% -> 12%
where the time goes in v5:
time: 88.7 us; the launch traced here: 88.1 us
  starting transfers between devices  55.3 us (62%)
  waiting for transfers between devices  13.6 us (15%)
  Pallas kernels  13.6 us (15%)
  local copies, waits for them, and re-layouts  3.65 us (4%)
  other arithmetic  1.85 us (2%)
    ppermute x12, starting transfers between devices, permute(): return lax.ppermute(value, 'ctx', pairs)  45.5 us
    pallas_call x7, Pallas kernels, call(): pl.pallas_call(kernel, out_shape=shapes, in_specs=specs, out_specs=[VMEM]...  13.6 us
    ppermute x12, waiting for transfers between devices, permute(): return lax.ppermute(value, 'ctx', pairs)  10 us
    ppermute x2, starting transfers between devices, partner(): lax.ppermute(value, 'head', [(i, i ^ heads // 2) for i in range(heads)])  9.8 us
    ppermute x2, waiting for transfers between devices, partner(): lax.ppermute(value, 'head', [(i, i ^ heads // 2) for i in range(heads)])  3.56 us
    unnamed x10, local copies, waits for them, and re-layouts  2.25 us
  transfers between devices with their start and end apart: 14, of which 5 were waited for; matrix products, arithmetic and copies ran while one was open for 2% of the time, Pallas kernels for 12%

profile of v5, /device:TPU:1, one launch (start us, length us, event | category | flops | bytes accessed | tf_op | source)
XLA Modules:
  0.0 88.1 jit_solution(8533524034367652176)
XLA Ops:
  0.0 0.7 fusion
  0.7 0.7 slice.16
  1.4 3.5 %collective-permute-start = (bf16[32,128]{1,0:T(8,128)(2,1)S(1)}, bf16[32,128]{1,0:T(8,128)(2,1)S(1)}, u32[]{:S(2)}, u32[]{:S(2)}) collective-permute-start(bf16[32,128]{1,0:T(8,128)(2,1)S(1)} %pad_maximum_fusion.2), channel_id=1, source_target_pairs={{0,32},{32,64},{64,96},{96,128},{128,160},{160,192},{192,224},{224... | collective-permute-start | bytes 24584 | tf_op jit(solution)/shard_map/ppermute | solution.py:410
  4.9 4.0 %collective-permute-start.4 = (bf16[512,128]{1,0:T(8,128)(2,1)}, bf16[512,128]{1,0:T(8,128)(2,1)S(1)}, u32[]{:S(2)}, u32[]{:S(2)}) collective-permute-start(bf16[512,128]{1,0:T(8,128)(2,1)} %a_ref.1), channel_id=1, source_target_pairs={{0,64},{32,96},{64,128},{96,160},{128,192},{160,224},{192,256},{22... | collective-permute-start | bytes 393224 | tf_op jit(solution)/shard_map/ppermute | solution.py:410
  8.9 1.3 %collective-permute-start.3 = (bf16[16,128]{1,0:T(8,128)(2,1)S(1)}, bf16[16,128]{1,0:T(8,128)(2,1)S(1)}, u32[]{:S(2)}, u32[]{:S(2)}) collective-permute-start(bf16[16,128]{1,0:T(8,128)(2,1)S(1)} %get-tuple-element.47), channel_id=1, source_target_pairs={{0,480},{32,0},{64,32},{96,64},{128,96},{160,128},{192,160},{224,1... | collective-permute-start | bytes 12296 | tf_op jit(solution)/shard_map/ppermute | solution.py:410
  10.2 3.3 %collective-permute-start.2 = (bf16[512,128]{1,0:T(8,128)(2,1)}, bf16[512,128]{1,0:T(8,128)(2,1)S(1)}, u32[]{:S(2)}, u32[]{:S(2)}) collective-permute-start(bf16[512,128]{1,0:T(8,128)(2,1)} %param.9), channel_id=1, source_target_pairs={{0,16},{1,17},{2,18},{3,19},{4,20},{5,21},{6,22},{7,23},{8,24},{9,... | collective-permute-start | bytes 393224 | tf_op jit(solution)/shard_map/ppermute | solution.py:416
  13.6 0.0 collective-permute-done.edge_ref
  13.6 0.9 %pad_maximum_fusion.1.own_ref = bf16[528,128]{1,0:T(8,128)(2,1)S(1)} fusion(bf16[16,128]{1,0:T(8,128)(2,1)S(1)} %get-tuple-element.50, bf16[512,128]{1,0:T(8,128)(2,1)} %param.7), kind=kLoop, calls=%fused_computation.1 | loop fusion | flops 270336 | bytes 270336 | tf_op jit(solution)/shard_map/concatenate | solution.py:424
  14.5 6.6 %collective-permute-start.1 = (bf16[528,128]{1,0:T(8,128)(2,1)S(1)}, bf16[528,128]{1,0:T(8,128)(2,1)S(1)}, u32[]{:S(2)}, u32[]{:S(2)}) collective-permute-start(bf16[528,128]{1,0:T(8,128)(2,1)S(1)} %pad_maximum_fusion.1.own_ref), channel_id=1, source_target_pairs={{0,32},{32,0},{64,96},{96,64},{128,160},{160,128},{192,224},{224,1... | collective-permute-start | bytes 405512 | tf_op jit(solution)/shard_map/ppermute | solution.py:410
  21.1 0.0 collective-permute-done.3
  21.1 0.0 collective-permute-done.2
  21.1 0.9 %pad_maximum_fusion.b_ref = bf16[1056,128]{1,0:T(8,128)(2,1)S(1)} fusion(bf16[16,128]{1,0:T(8,128)(2,1)S(1)} %collective-permute-done.3, bf16[16,128]{1,0:T(8,128)(2,1)S(1)} %get-tuple-element.49, bf16[512,128]{1,0:T(8,128)(2,1)S(1)} %collective-permute-done.2, bf16[512,128]{1,0:T(8,128)(2,1)} %param.9), kind=kLoop, calls=%fused_computation | loop fusion | flops 1081344 | bytes 540672 | tf_op jit(solution)/shard_map/concatenate | solution.py:428
  22.1 1.9 %collective-permute-start.6 = (bf16[1056,128]{1,0:T(8,128)(2,1)S(1)}, bf16[1056,128]{1,0:T(8,128)(2,1)S(1)}, u32[]{:S(2)}, u32[]{:S(2)}) collective-permute-start(bf16[1056,128]{1,0:T(8,128)(2,1)S(1)} %pad_maximum_fusion.b_ref), channel_id=1, source_target_pairs={{0,64},{32,96},{64,128},{96,160},{128,192},{160,224},{192,256},{22... | collective-permute-start | bytes 811016 | tf_op jit(solution)/shard_map/ppermute | solution.py:410
  24.0 0.0 collective-permute-done.1.other_ref
  24.0 0.0 copy-start
  24.0 0.9 %copy-done = bf16[512,128]{1,0:T(8,128)(2,1)S(1)} copy-done((bf16[512,128]{1,0:T(8,128)(2,1)S(1)}, bf16[512,128]{1,0:T(8,128)(2,1)}, u32[]{:S(2)}) %copy-start) | copy-done | bytes 131096
  24.9 0.0 copy-start.3
  24.9 0.7 copy-done.3
  25.6 0.0 copy-start.4
  25.6 0.7 copy-done.4
  26.2 6.9 %shard_map.73 = (bf16[1536,768]{1,0:T(8,128)(2,1)S(1)}, f32[1024,384]{1,0:T(8,128)S(1)}, f32[8,128]{1,0:T(8,128)}) custom-call(s32[8]{0:T(128)S(1)} %copy-done.4, f32[6,1,11]{2,1,0:T(1,128)S(1)} %bitcast.5, bf16[528,128]{1,0:T(8,128)(2,1)S(1)} %pad_maximum_fusion.1.own_ref, bf16[528,128]{1,0:T(8,128)(2,1)S(1)} %collective-permute-done.1.other_ref, ...), custom_call_target="tpu_custom_call" | custom-call | flops 120259084288 | bytes 4194304 | tf_op jit(solution)/shard_map/pallas_call | solution.py:390
  33.1 0.0 collective-permute-done.4.a_ref
  33.1 2.5 %collective-permute-start.5 = (bf16[512,128]{1,0:T(8,128)(2,1)S(1)}, bf16[512,128]{1,0:T(8,128)(2,1)S(1)}, u32[]{:S(2)}, u32[]{:S(2)}) collective-permute-start(bf16[512,128]{1,0:T(8,128)(2,1)S(1)} %collective-permute-done.4.a_ref), channel_id=1, source_target_pairs={{0,64},{32,96},{64,128},{96,160},{128,192},{160,224},{192,256},{22... | collective-permute-start | bytes 393224 | tf_op jit(solution)/shard_map/ppermute | solution.py:410
  35.6 0.0 collective-permute-done.6.b_ref
  35.7 4.1 %collective-permute-start.8 = (bf16[1056,128]{1,0:T(8,128)(2,1)S(1)}, bf16[1056,128]{1,0:T(8,128)(2,1)S(1)}, u32[]{:S(2)}, u32[]{:S(2)}) collective-permute-start(bf16[1056,128]{1,0:T(8,128)(2,1)S(1)} %collective-permute-done.6.b_ref), channel_id=1, source_target_pairs={{0,64},{32,96},{64,128},{96,160},{128,192},{160,224},{192,256},{22... | collective-permute-start | bytes 811016 | tf_op jit(solution)/shard_map/ppermute | solution.py:410
  39.8 1.3 %shard_map.74 = (f32[1024,384]{1,0:T(8,128)S(1)}, f32[8,128]{1,0:T(8,128)}) custom-call(s32[8]{0:T(128)S(1)} %copy-done.4, f32[6,1,11]{2,1,0:T(1,128)S(1)} %bitcast.6, bf16[1536,768]{1,0:T(8,128)(2,1)S(1)} %get-tuple-element.26.qp_ref, bf16[512,128]{1,0:T(8,128)(2,1)S(1)} %collective-permute-done.4.a_ref, ...), custom_call_target="tpu_custom_call" | custom-call | flops 120259084288 | bytes 4194304 | tf_op jit(solution)/shard_map/pallas_call | solution.py:390
  41.1 0.0 collective-permute-done.5.a_ref
  41.1 8.3 %collective-permute-start.7 = (bf16[512,128]{1,0:T(8,128)(2,1)S(1)}, bf16[512,128]{1,0:T(8,128)(2,1)S(1)}, u32[]{:S(2)}, u32[]{:S(2)}) collective-permute-start(bf16[512,128]{1,0:T(8,128)(2,1)S(1)} %collective-permute-done.5.a_ref), channel_id=1, source_target_pairs={{0,64},{32,96},{64,128},{96,160},{128,192},{160,224},{192,256},{22... | collective-permute-start | bytes 393224 | tf_op jit(solution)/shard_map/ppermute | solution.py:410
  49.4 0.0 collective-permute-done.8.b_ref
  49.4 1.9 %collective-permute-start.10 = (bf16[1056,128]{1,0:T(8,128)(2,1)S(1)}, bf16[1056,128]{1,0:T(8,128)(2,1)S(1)}, u32[]{:S(2)}, u32[]{:S(2)}) collective-permute-start(bf16[1056,128]{1,0:T(8,128)(2,1)S(1)} %collective-permute-done.8.b_ref), channel_id=1, source_target_pairs={{0,64},{32,96},{64,128},{96,160},{128,192},{160,224},{192,256},{22... | collective-permute-start | bytes 811016 | tf_op jit(solution)/shard_map/ppermute | solution.py:410
  51.4 1.5 %shard_map.75 = (f32[1024,384]{1,0:T(8,128)S(1)}, f32[8,128]{1,0:T(8,128)}) custom-call(s32[8]{0:T(128)S(1)} %copy-done.4, f32[6,1,11]{2,1,0:T(1,128)S(1)} %bitcast.7, bf16[1536,768]{1,0:T(8,128)(2,1)S(1)} %get-tuple-element.26.qp_ref, bf16[512,128]{1,0:T(8,128)(2,1)S(1)} %collective-permute-done.5.a_ref, ...), custom_call_target="tpu_custom_call" | custom-call | flops 120259084288 | bytes 4194304 | tf_op jit(solution)/shard_map/pallas_call | solution.py:390
  52.9 0.0 collective-permute-done.7.a_ref
  52.9 2.7 %collective-permute-start.9 = (bf16[512,128]{1,0:T(8,128)(2,1)S(1)}, bf16[512,128]{1,0:T(8,128)(2,1)S(1)}, u32[]{:S(2)}, u32[]{:S(2)}) collective-permute-start(bf16[512,128]{1,0:T(8,128)(2,1)S(1)} %collective-permute-done.7.a_ref), channel_id=1, source_target_pairs={{0,64},{32,96},{64,128},{96,160},{128,192},{160,224},{192,256},{22... | collective-permute-start | bytes 393224 | tf_op jit(solution)/shard_map/ppermute | solution.py:410
  55.6 2.3 %collective-permute-done.10.b_ref = bf16[1056,128]{1,0:T(8,128)(2,1)S(1)} collective-permute-done((bf16[1056,128]{1,0:T(8,128)(2,1)S(1)}, bf16[1056,128]{1,0:T(8,128)(2,1)S(1)}, u32[]{:S(2)}, u32[]{:S(2)}) %collective-permute-start.10) | collective-permute-done | bytes 270368 | tf_op jit(solution)/shard_map/ppermute | solution.py:410
  57.8 3.1 %collective-permute-start.11 = (bf16[1056,128]{1,0:T(8,128)(2,1)S(1)}, bf16[1056,128]{1,0:T(8,128)(2,1)S(1)}, u32[]{:S(2)}, u32[]{:S(2)}) collective-permute-start(bf16[1056,128]{1,0:T(8,128)(2,1)S(1)} %collective-permute-done.10.b_ref), channel_id=1, source_target_pairs={{0,64},{32,96},{64,128},{96,160},{128,192},{160,224},{192,256},{22... | collective-permute-start | bytes 811016 | tf_op jit(solution)/shard_map/ppermute | solution.py:410
  61.0 1.3 %shard_map.76 = (f32[1024,384]{1,0:T(8,128)S(1)}, f32[8,128]{1,0:T(8,128)}) custom-call(s32[8]{0:T(128)S(1)} %copy-done.4, f32[6,1,11]{2,1,0:T(1,128)S(1)} %bitcast.8, bf16[1536,768]{1,0:T(8,128)(2,1)S(1)} %get-tuple-element.26.qp_ref, bf16[512,128]{1,0:T(8,128)(2,1)S(1)} %collective-permute-done.7.a_ref, ...), custom_call_target="tpu_custom_call" | custom-call | flops 120259084288 | bytes 4194304 | tf_op jit(solution)/shard_map/pallas_call | solution.py:390
  62.3 1.0 %collective-permute-done.9.a_ref = bf16[512,128]{1,0:T(8,128)(2,1)S(1)} collective-permute-done((bf16[512,128]{1,0:T(8,128)(2,1)S(1)}, bf16[512,128]{1,0:T(8,128)(2,1)S(1)}, u32[]{:S(2)}, u32[]{:S(2)}) %collective-permute-start.9) | collective-permute-done | bytes 131104 | tf_op jit(solution)/shard_map/ppermute | solution.py:410
  63.2 4.9 %collective-permute-done.11.b_ref = bf16[1056,128]{1,0:T(8,128)(2,1)S(1)} collective-permute-done((bf16[1056,128]{1,0:T(8,128)(2,1)S(1)}, bf16[1056,128]{1,0:T(8,128)(2,1)S(1)}, u32[]{:S(2)}, u32[]{:S(2)}) %collective-permute-start.11) | collective-permute-done | bytes 270368 | tf_op jit(solution)/shard_map/ppermute | solution.py:410
  68.1 0.8 shard_map.77
  68.9 0.0 copy-start.1
  69.0 0.0 copy-start.2
  69.0 5.5 %collective-permute-start.12 = (f32[512,384]{1,0:T(8,128)S(1)}, f32[512,384]{1,0:T(8,128)S(1)}, u32[]{:S(2)}, u32[]{:S(2)}) collective-permute-start(f32[512,384]{1,0:T(8,128)S(1)} %get-tuple-element.44), channel_id=1, source_target_pairs={{0,32},{32,0},{64,96},{96,64},{128,160},{160,128},{192,224},{224,1... | collective-permute-start | bytes 2359304 | tf_op jit(solution)/shard_map/ppermute | solution.py:410
  74.5 1.9 %collective-permute-done.12.other_ref = f32[512,384]{1,0:T(8,128)S(1)} collective-permute-done((f32[512,384]{1,0:T(8,128)S(1)}, f32[512,384]{1,0:T(8,128)S(1)}, u32[]{:S(2)}, u32[]{:S(2)}) %collective-permute-start.12) | collective-permute-done | bytes 786464 | tf_op jit(solution)/shard_map/ppermute | solution.py:410
  76.3 0.4 shard_map.78
  76.8 6.5 %collective-permute-start.13 = (bf16[512,128]{1,0:T(8,128)(2,1)S(1)}, bf16[512,128]{1,0:T(8,128)(2,1)S(1)}, u32[]{:S(2)}, u32[]{:S(2)}) collective-permute-start(bf16[512,128]{1,0:T(8,128)(2,1)S(1)} %get-tuple-element.46), channel_id=1, source_target_pairs={{0,16},{1,17},{2,18},{3,19},{4,20},{5,21},{6,22},{7,23},{8,24},{9,... | collective-permute-start | bytes 393224 | tf_op jit(solution)/shard_map/ppermute | solution.py:416
  83.2 3.6 %collective-permute-done.13.cross_ref = bf16[512,128]{1,0:T(8,128)(2,1)S(1)} collective-permute-done((bf16[512,128]{1,0:T(8,128)(2,1)S(1)}, bf16[512,128]{1,0:T(8,128)(2,1)S(1)}, u32[]{:S(2)}, u32[]{:S(2)}) %collective-permute-start.13) | collective-permute-done | bytes 131104 | tf_op jit(solution)/shard_map/ppermute | solution.py:416
  86.8 0.0 copy-done.1
  86.8 0.0 copy-done.2
  86.8 1.4 %shard_map.79 = bf16[512,128]{1,0:T(8,128)(2,1)} custom-call(f32[2]{0:T(128)S(1)} %bitcast.3, f32[512,128]{1,0:T(8,128)S(1)} %get-tuple-element.45.own_ref, bf16[512,128]{1,0:T(8,128)(2,1)S(1)} %collective-permute-done.13.cross_ref, f32[1,128]{1,0:T(1,128)S(1)} %bitcast.4), custom_call_target="tpu_custom_call" | custom-call | bytes 4194304 | tf_op jit(solution)/shard_map/pallas_call | solution.py:390
  (2 shorter events, 0.0 us)
Async XLA Ops:
  1.4 12.2 %collective-permute-start = (bf16[32,128]{1,0:T(8,128)(2,1)S(1)}, bf16[32,128]{1,0:T(8,128)(2,1)S(1)}, u32[]{:S(2)}, u32[]{:S(2)}) collective-permute-start(bf16[32,128]{1,0:T(8,128)(2,1)S(1)} %pad_maximum_fusion.2), channel_id=1, source_target_pairs={{0,32},{32,64},{64,96},{96,128},{128,160},{160,192},{192,224},{224... | collective-permute-start | bytes 24584 | tf_op jit(solution)/shard_map/ppermute | solution.py:410
  4.9 28.2 %collective-permute-start.4 = (bf16[512,128]{1,0:T(8,128)(2,1)}, bf16[512,128]{1,0:T(8,128)(2,1)S(1)}, u32[]{:S(2)}, u32[]{:S(2)}) collective-permute-start(bf16[512,128]{1,0:T(8,128)(2,1)} %a_ref.1), channel_id=1, source_target_pairs={{0,64},{32,96},{64,128},{96,160},{128,192},{160,224},{192,256},{22... | collective-permute-start | bytes 393224 | tf_op jit(solution)/shard_map/ppermute | solution.py:410
  8.9 12.2 %collective-permute-start.3 = (bf16[16,128]{1,0:T(8,128)(2,1)S(1)}, bf16[16,128]{1,0:T(8,128)(2,1)S(1)}, u32[]{:S(2)}, u32[]{:S(2)}) collective-permute-start(bf16[16,128]{1,0:T(8,128)(2,1)S(1)} %get-tuple-element.47), channel_id=1, source_target_pairs={{0,480},{32,0},{64,32},{96,64},{128,96},{160,128},{192,160},{224,1... | collective-permute-start | bytes 12296 | tf_op jit(solution)/shard_map/ppermute | solution.py:410
  10.2 10.9 %collective-permute-start.2 = (bf16[512,128]{1,0:T(8,128)(2,1)}, bf16[512,128]{1,0:T(8,128)(2,1)S(1)}, u32[]{:S(2)}, u32[]{:S(2)}) collective-permute-start(bf16[512,128]{1,0:T(8,128)(2,1)} %param.9), channel_id=1, source_target_pairs={{0,16},{1,17},{2,18},{3,19},{4,20},{5,21},{6,22},{7,23},{8,24},{9,... | collective-permute-start | bytes 393224 | tf_op jit(solution)/shard_map/ppermute | solution.py:416
  14.5 9.5 %collective-permute-start.1 = (bf16[528,128]{1,0:T(8,128)(2,1)S(1)}, bf16[528,128]{1,0:T(8,128)(2,1)S(1)}, u32[]{:S(2)}, u32[]{:S(2)}) collective-permute-start(bf16[528,128]{1,0:T(8,128)(2,1)S(1)} %pad_maximum_fusion.1.own_ref), channel_id=1, source_target_pairs={{0,32},{32,0},{64,96},{96,64},{128,160},{160,128},{192,224},{224,1... | collective-permute-start | bytes 405512 | tf_op jit(solution)/shard_map/ppermute | solution.py:410
  22.1 13.6 %collective-permute-start.6 = (bf16[1056,128]{1,0:T(8,128)(2,1)S(1)}, bf16[1056,128]{1,0:T(8,128)(2,1)S(1)}, u32[]{:S(2)}, u32[]{:S(2)}) collective-permute-start(bf16[1056,128]{1,0:T(8,128)(2,1)S(1)} %pad_maximum_fusion.b_ref), channel_id=1, source_target_pairs={{0,64},{32,96},{64,128},{96,160},{128,192},{160,224},{192,256},{22... | collective-permute-start | bytes 811016 | tf_op jit(solution)/shard_map/ppermute | solution.py:410
  24.0 0.9 %copy-start = (bf16[512,128]{1,0:T(8,128)(2,1)S(1)}, bf16[512,128]{1,0:T(8,128)(2,1)}, u32[]{:S(2)}) copy-start(bf16[512,128]{1,0:T(8,128)(2,1)} %a_ref.1) | copy-start | bytes 393220
  24.9 0.7 copy-start.3
  25.6 0.7 copy-start.4
  33.1 8.0 %collective-permute-start.5 = (bf16[512,128]{1,0:T(8,128)(2,1)S(1)}, bf16[512,128]{1,0:T(8,128)(2,1)S(1)}, u32[]{:S(2)}, u32[]{:S(2)}) collective-permute-start(bf16[512,128]{1,0:T(8,128)(2,1)S(1)} %collective-permute-done.4.a_ref), channel_id=1, source_target_pairs={{0,64},{32,96},{64,128},{96,160},{128,192},{160,224},{192,256},{22... | collective-permute-start | bytes 393224 | tf_op jit(solution)/shard_map/ppermute | solution.py:410
  35.7 13.8 %collective-permute-start.8 = (bf16[1056,128]{1,0:T(8,128)(2,1)S(1)}, bf16[1056,128]{1,0:T(8,128)(2,1)S(1)}, u32[]{:S(2)}, u32[]{:S(2)}) collective-permute-start(bf16[1056,128]{1,0:T(8,128)(2,1)S(1)} %collective-permute-done.6.b_ref), channel_id=1, source_target_pairs={{0,64},{32,96},{64,128},{96,160},{128,192},{160,224},{192,256},{22... | collective-permute-start | bytes 811016 | tf_op jit(solution)/shard_map/ppermute | solution.py:410
  41.1 11.8 %collective-permute-start.7 = (bf16[512,128]{1,0:T(8,128)(2,1)S(1)}, bf16[512,128]{1,0:T(8,128)(2,1)S(1)}, u32[]{:S(2)}, u32[]{:S(2)}) collective-permute-start(bf16[512,128]{1,0:T(8,128)(2,1)S(1)} %collective-permute-done.5.a_ref), channel_id=1, source_target_pairs={{0,64},{32,96},{64,128},{96,160},{128,192},{160,224},{192,256},{22... | collective-permute-start | bytes 393224 | tf_op jit(solution)/shard_map/ppermute | solution.py:410
  49.4 8.4 %collective-permute-start.10 = (bf16[1056,128]{1,0:T(8,128)(2,1)S(1)}, bf16[1056,128]{1,0:T(8,128)(2,1)S(1)}, u32[]{:S(2)}, u32[]{:S(2)}) collective-permute-start(bf16[1056,128]{1,0:T(8,128)(2,1)S(1)} %collective-permute-done.8.b_ref), channel_id=1, source_target_pairs={{0,64},{32,96},{64,128},{96,160},{128,192},{160,224},{192,256},{22... | collective-permute-start | bytes 811016 | tf_op jit(solution)/shard_map/ppermute | solution.py:410
  52.9 10.3 %collective-permute-start.9 = (bf16[512,128]{1,0:T(8,128)(2,1)S(1)}, bf16[512,128]{1,0:T(8,128)(2,1)S(1)}, u32[]{:S(2)}, u32[]{:S(2)}) collective-permute-start(bf16[512,128]{1,0:T(8,128)(2,1)S(1)} %collective-permute-done.7.a_ref), channel_id=1, source_target_pairs={{0,64},{32,96},{64,128},{96,160},{128,192},{160,224},{192,256},{22... | collective-permute-start | bytes 393224 | tf_op jit(solution)/shard_map/ppermute | solution.py:410
  57.8 10.3 %collective-permute-start.11 = (bf16[1056,128]{1,0:T(8,128)(2,1)S(1)}, bf16[1056,128]{1,0:T(8,128)(2,1)S(1)}, u32[]{:S(2)}, u32[]{:S(2)}) collective-permute-start(bf16[1056,128]{1,0:T(8,128)(2,1)S(1)} %collective-permute-done.10.b_ref), channel_id=1, source_target_pairs={{0,64},{32,96},{64,128},{96,160},{128,192},{160,224},{192,256},{22... | collective-permute-start | bytes 811016 | tf_op jit(solution)/shard_map/ppermute | solution.py:410
  68.9 17.9 %copy-start.1 = (f32[1,2]{1,0:T(1,128)S(1)}, f32[1,2]{1,0:T(1,128)}, u32[]{:S(2)}) copy-start(f32[1,2]{1,0:T(1,128)} %param.11) | copy-start | bytes 28
  69.0 17.8 %copy-start.2 = (f32[128]{0:T(128)S(1)}, f32[128]{0:T(128)}, u32[]{:S(2)}) copy-start(f32[128]{0:T(128)} %param.12) | copy-start | bytes 1540
  69.0 7.4 %collective-permute-start.12 = (f32[512,384]{1,0:T(8,128)S(1)}, f32[512,384]{1,0:T(8,128)S(1)}, u32[]{:S(2)}, u32[]{:S(2)}) collective-permute-start(f32[512,384]{1,0:T(8,128)S(1)} %get-tuple-element.44), channel_id=1, source_target_pairs={{0,32},{32,0},{64,96},{96,64},{128,160},{160,128},{192,224},{224,1... | collective-permute-start | bytes 2359304 | tf_op jit(solution)/shard_map/ppermute | solution.py:410
  76.8 10.0 %collective-permute-start.13 = (bf16[512,128]{1,0:T(8,128)(2,1)S(1)}, bf16[512,128]{1,0:T(8,128)(2,1)S(1)}, u32[]{:S(2)}, u32[]{:S(2)}) collective-permute-start(bf16[512,128]{1,0:T(8,128)(2,1)S(1)} %get-tuple-element.46), channel_id=1, source_target_pairs={{0,16},{1,17},{2,18},{3,19},{4,20},{5,21},{6,22},{7,23},{8,24},{9,... | collective-permute-start | bytes 393224 | tf_op jit(solution)/shard_map/ppermute | solution.py:416

commit v6 on v5

--- a/solution.py
+++ b/solution.py
@@ -308,16 +308,20 @@
     taken.wait()
     rest = (chip_row, block, ends, taps_ref, qp_ref, kx_ref, vx_ref, start_ref, state_ref)
 
-    @pl.loop(0, keys // (BAND * TILES))
-    def _(step):
-        near([(step * TILES + n) * BAND for n in range(TILES)], *rest)
-
-    @pl.when(block + keys - chip_row < count)
+    tiles = [n * BAND for n in range(keys // BAND)]
+    past = block + keys - chip_row < count
+    near(tiles[:TILES], *rest)
+
+    @pl.when(past)
     def _():
-        near([keys], *rest)
+        near(tiles[TILES:] + [keys], *rest)
+
+    @pl.when(jnp.logical_not(past))
+    def _():
+        near(tiles[TILES:], *rest)
 
     convolve(True, block, 0, ends, qp_ref, kx_ref, kp_ref)
-    far(2, chip_row, block, ends, qp_ref, kp_ref, vx_ref, state_ref, state_ref)
+    far(4, chip_row, block, ends, qp_ref, kp_ref, vx_ref, state_ref, state_ref)
 
 
 def hop_kernel(hop, last, docs_ref, taps_ref, qp_ref, a_ref, b_ref, state_in, *rest):
@@ -429,7 +433,7 @@
     state = [((2 * rows, 3 * HEAD_DIM), f32)]
     mark = [((8, 128), f32)]
     scratch = [
-        pltpu.VMEM((TILES, BAND // 2 + 8, GROUP), jnp.int32),
+        pltpu.VMEM((TILES + 1, BAND // 2 + 8, GROUP), jnp.int32),
         pltpu.VMEM((rows + 128, HEAD_DIM), bf16),
         pltpu.VMEM((rows + 128, 2 * HEAD_DIM), bf16),
         pltpu.VMEM((rows, 2 * width), bf16),

time: 88.7 us -> 88 us (level)
  starting transfers between devices: 55.3 us -> 47.5 us
  waiting for transfers between devices: 13.6 us -> 19.8 us
    ppermute x2, starting transfers between devices: 9.8 us -> 5.27 us  [partner(): lax.ppermute(value, 'head', [(i, i ^ heads // 2) for i in range(heads)])]
    ppermute x12, waiting for transfers between devices: 10 us -> 13.6 us  [permute(): return lax.ppermute(value, 'ctx', pairs)]
    ppermute x12, starting transfers between devices: 45.5 us -> 42.2 us  [permute(): return lax.ppermute(value, 'ctx', pairs)]
    ppermute x2, waiting for transfers between devices: 3.56 us -> 6.18 us  [partner(): lax.ppermute(value, 'head', [(i, i ^ heads // 2) for i in range(heads)])]
  transfers between devices with their start and end apart: 14 -> 14, of which waited for: 5 -> 4; matrix products, arithmetic and copies ran while one was open for 2% -> 2% of each run, Pallas kernels for 12% -> 13%
where the time goes in v6:
time: 88 us; the launch traced here: 87.3 us
  starting transfers between devices  47.5 us (54%)
  waiting for transfers between devices  19.8 us (22%)
  Pallas kernels  14.3 us (16%)
  local copies, waits for them, and re-layouts  3.65 us (4%)
  other arithmetic  1.85 us (2%)
    ppermute x12, starting transfers between devices, permute(): return lax.ppermute(value, 'ctx', pairs)  42.2 us
    pallas_call x7, Pallas kernels, call(): pl.pallas_call(kernel, out_shape=shapes, in_specs=specs, out_specs=[VMEM]...  14.3 us
    ppermute x12, waiting for transfers between devices, permute(): return lax.ppermute(value, 'ctx', pairs)  13.6 us
    ppermute x2, waiting for transfers between devices, partner(): lax.ppermute(value, 'head', [(i, i ^ heads // 2) for i in range(heads)])  6.18 us
    ppermute x2, starting transfers between devices, partner(): lax.ppermute(value, 'head', [(i, i ^ heads // 2) for i in range(heads)])  5.27 us
    unnamed x10, local copies, waits for them, and re-layouts  2.25 us
  transfers between devices with their start and end apart: 14, of which 4 were waited for; matrix products, arithmetic and copies ran while one was open for 2% of the time, Pallas kernels for 13%

profile of v6, /device:TPU:1, one launch (start us, length us, event | category | flops | bytes accessed | tf_op | source)
XLA Modules:
  0.0 87.3 jit_solution(9670041143985012755)
XLA Ops:
  0.0 0.7 fusion
  0.7 0.7 slice.16
  1.4 3.5 %collective-permute-start = (bf16[32,128]{1,0:T(8,128)(2,1)S(1)}, bf16[32,128]{1,0:T(8,128)(2,1)S(1)}, u32[]{:S(2)}, u32[]{:S(2)}) collective-permute-start(bf16[32,128]{1,0:T(8,128)(2,1)S(1)} %pad_maximum_fusion.2), channel_id=1, source_target_pairs={{0,32},{32,64},{64,96},{96,128},{128,160},{160,192},{192,224},{224... | collective-permute-start | bytes 24584 | tf_op jit(solution)/shard_map/ppermute | solution.py:414
  4.9 4.0 %collective-permute-start.4 = (bf16[512,128]{1,0:T(8,128)(2,1)}, bf16[512,128]{1,0:T(8,128)(2,1)S(1)}, u32[]{:S(2)}, u32[]{:S(2)}) collective-permute-start(bf16[512,128]{1,0:T(8,128)(2,1)} %a_ref.1), channel_id=1, source_target_pairs={{0,64},{32,96},{64,128},{96,160},{128,192},{160,224},{192,256},{22... | collective-permute-start | bytes 393224 | tf_op jit(solution)/shard_map/ppermute | solution.py:414
  8.9 1.3 %collective-permute-start.3 = (bf16[16,128]{1,0:T(8,128)(2,1)S(1)}, bf16[16,128]{1,0:T(8,128)(2,1)S(1)}, u32[]{:S(2)}, u32[]{:S(2)}) collective-permute-start(bf16[16,128]{1,0:T(8,128)(2,1)S(1)} %get-tuple-element.47), channel_id=1, source_target_pairs={{0,480},{32,0},{64,32},{96,64},{128,96},{160,128},{192,160},{224,1... | collective-permute-start | bytes 12296 | tf_op jit(solution)/shard_map/ppermute | solution.py:414
  10.2 3.3 %collective-permute-start.2 = (bf16[512,128]{1,0:T(8,128)(2,1)}, bf16[512,128]{1,0:T(8,128)(2,1)S(1)}, u32[]{:S(2)}, u32[]{:S(2)}) collective-permute-start(bf16[512,128]{1,0:T(8,128)(2,1)} %param.9), channel_id=1, source_target_pairs={{0,16},{1,17},{2,18},{3,19},{4,20},{5,21},{6,22},{7,23},{8,24},{9,... | collective-permute-start | bytes 393224 | tf_op jit(solution)/shard_map/ppermute | solution.py:420
  13.6 0.0 collective-permute-done.edge_ref
  13.6 0.9 %pad_maximum_fusion.1.own_ref = bf16[528,128]{1,0:T(8,128)(2,1)S(1)} fusion(bf16[16,128]{1,0:T(8,128)(2,1)S(1)} %get-tuple-element.50, bf16[512,128]{1,0:T(8,128)(2,1)} %param.7), kind=kLoop, calls=%fused_computation.1 | loop fusion | flops 270336 | bytes 270336 | tf_op jit(solution)/shard_map/concatenate | solution.py:428
  14.5 6.6 %collective-permute-start.1 = (bf16[528,128]{1,0:T(8,128)(2,1)S(1)}, bf16[528,128]{1,0:T(8,128)(2,1)S(1)}, u32[]{:S(2)}, u32[]{:S(2)}) collective-permute-start(bf16[528,128]{1,0:T(8,128)(2,1)S(1)} %pad_maximum_fusion.1.own_ref), channel_id=1, source_target_pairs={{0,32},{32,0},{64,96},{96,64},{128,160},{160,128},{192,224},{224,1... | collective-permute-start | bytes 405512 | tf_op jit(solution)/shard_map/ppermute | solution.py:414
  21.1 0.0 collective-permute-done.3
  21.1 0.0 collective-permute-done.2
  21.1 0.9 %pad_maximum_fusion.b_ref = bf16[1056,128]{1,0:T(8,128)(2,1)S(1)} fusion(bf16[16,128]{1,0:T(8,128)(2,1)S(1)} %collective-permute-done.3, bf16[16,128]{1,0:T(8,128)(2,1)S(1)} %get-tuple-element.49, bf16[512,128]{1,0:T(8,128)(2,1)S(1)} %collective-permute-done.2, bf16[512,128]{1,0:T(8,128)(2,1)} %param.9), kind=kLoop, calls=%fused_computation | loop fusion | flops 1081344 | bytes 540672 | tf_op jit(solution)/shard_map/concatenate | solution.py:432
  22.1 1.9 %collective-permute-start.6 = (bf16[1056,128]{1,0:T(8,128)(2,1)S(1)}, bf16[1056,128]{1,0:T(8,128)(2,1)S(1)}, u32[]{:S(2)}, u32[]{:S(2)}) collective-permute-start(bf16[1056,128]{1,0:T(8,128)(2,1)S(1)} %pad_maximum_fusion.b_ref), channel_id=1, source_target_pairs={{0,64},{32,96},{64,128},{96,160},{128,192},{160,224},{192,256},{22... | collective-permute-start | bytes 811016 | tf_op jit(solution)/shard_map/ppermute | solution.py:414
  24.0 0.0 collective-permute-done.1.other_ref
  24.0 0.0 copy-start
  24.0 0.9 %copy-done = bf16[512,128]{1,0:T(8,128)(2,1)S(1)} copy-done((bf16[512,128]{1,0:T(8,128)(2,1)S(1)}, bf16[512,128]{1,0:T(8,128)(2,1)}, u32[]{:S(2)}) %copy-start) | copy-done | bytes 131096
  24.9 0.0 copy-start.3
  24.9 0.7 copy-done.3
  25.6 0.0 copy-start.4
  25.6 0.7 copy-done.4
  26.2 7.9 %shard_map.73 = (bf16[1536,768]{1,0:T(8,128)(2,1)S(1)}, f32[1024,384]{1,0:T(8,128)S(1)}, f32[8,128]{1,0:T(8,128)}) custom-call(s32[8]{0:T(128)S(1)} %copy-done.4, f32[6,1,11]{2,1,0:T(1,128)S(1)} %bitcast.5, bf16[528,128]{1,0:T(8,128)(2,1)S(1)} %pad_maximum_fusion.1.own_ref, bf16[528,128]{1,0:T(8,128)(2,1)S(1)} %collective-permute-done.1.other_ref, ...), custom_call_target="tpu_custom_call" | custom-call | flops 120259084288 | bytes 4194304 | tf_op jit(solution)/shard_map/pallas_call | solution.py:394
  34.1 0.0 collective-permute-done.4.a_ref
  34.1 2.5 %collective-permute-start.5 = (bf16[512,128]{1,0:T(8,128)(2,1)S(1)}, bf16[512,128]{1,0:T(8,128)(2,1)S(1)}, u32[]{:S(2)}, u32[]{:S(2)}) collective-permute-start(bf16[512,128]{1,0:T(8,128)(2,1)S(1)} %collective-permute-done.4.a_ref), channel_id=1, source_target_pairs={{0,64},{32,96},{64,128},{96,160},{128,192},{160,224},{192,256},{22... | collective-permute-start | bytes 393224 | tf_op jit(solution)/shard_map/ppermute | solution.py:414
  36.6 0.0 collective-permute-done.6.b_ref
  36.7 3.7 %collective-permute-start.8 = (bf16[1056,128]{1,0:T(8,128)(2,1)S(1)}, bf16[1056,128]{1,0:T(8,128)(2,1)S(1)}, u32[]{:S(2)}, u32[]{:S(2)}) collective-permute-start(bf16[1056,128]{1,0:T(8,128)(2,1)S(1)} %collective-permute-done.6.b_ref), channel_id=1, source_target_pairs={{0,64},{32,96},{64,128},{96,160},{128,192},{160,224},{192,256},{22... | collective-permute-start | bytes 811016 | tf_op jit(solution)/shard_map/ppermute | solution.py:414
  40.4 1.3 %shard_map.74 = (f32[1024,384]{1,0:T(8,128)S(1)}, f32[8,128]{1,0:T(8,128)}) custom-call(s32[8]{0:T(128)S(1)} %copy-done.4, f32[6,1,11]{2,1,0:T(1,128)S(1)} %bitcast.6, bf16[1536,768]{1,0:T(8,128)(2,1)S(1)} %get-tuple-element.26.qp_ref, bf16[512,128]{1,0:T(8,128)(2,1)S(1)} %collective-permute-done.4.a_ref, ...), custom_call_target="tpu_custom_call" | custom-call | flops 120259084288 | bytes 4194304 | tf_op jit(solution)/shard_map/pallas_call | solution.py:394
  41.7 0.0 collective-permute-done.5.a_ref
  41.7 8.3 %collective-permute-start.7 = (bf16[512,128]{1,0:T(8,128)(2,1)S(1)}, bf16[512,128]{1,0:T(8,128)(2,1)S(1)}, u32[]{:S(2)}, u32[]{:S(2)}) collective-permute-start(bf16[512,128]{1,0:T(8,128)(2,1)S(1)} %collective-permute-done.5.a_ref), channel_id=1, source_target_pairs={{0,64},{32,96},{64,128},{96,160},{128,192},{160,224},{192,256},{22... | collective-permute-start | bytes 393224 | tf_op jit(solution)/shard_map/ppermute | solution.py:414
  50.0 0.0 collective-permute-done.8.b_ref
  50.0 2.5 %collective-permute-start.10 = (bf16[1056,128]{1,0:T(8,128)(2,1)S(1)}, bf16[1056,128]{1,0:T(8,128)(2,1)S(1)}, u32[]{:S(2)}, u32[]{:S(2)}) collective-permute-start(bf16[1056,128]{1,0:T(8,128)(2,1)S(1)} %collective-permute-done.8.b_ref), channel_id=1, source_target_pairs={{0,64},{32,96},{64,128},{96,160},{128,192},{160,224},{192,256},{22... | collective-permute-start | bytes 811016 | tf_op jit(solution)/shard_map/ppermute | solution.py:414
  52.5 1.3 %shard_map.75 = (f32[1024,384]{1,0:T(8,128)S(1)}, f32[8,128]{1,0:T(8,128)}) custom-call(s32[8]{0:T(128)S(1)} %copy-done.4, f32[6,1,11]{2,1,0:T(1,128)S(1)} %bitcast.7, bf16[1536,768]{1,0:T(8,128)(2,1)S(1)} %get-tuple-element.26.qp_ref, bf16[512,128]{1,0:T(8,128)(2,1)S(1)} %collective-permute-done.5.a_ref, ...), custom_call_target="tpu_custom_call" | custom-call | flops 120259084288 | bytes 4194304 | tf_op jit(solution)/shard_map/pallas_call | solution.py:394
  53.8 0.0 collective-permute-done.7.a_ref
  53.8 3.1 %collective-permute-start.9 = (bf16[512,128]{1,0:T(8,128)(2,1)S(1)}, bf16[512,128]{1,0:T(8,128)(2,1)S(1)}, u32[]{:S(2)}, u32[]{:S(2)}) collective-permute-start(bf16[512,128]{1,0:T(8,128)(2,1)S(1)} %collective-permute-done.7.a_ref), channel_id=1, source_target_pairs={{0,64},{32,96},{64,128},{96,160},{128,192},{160,224},{192,256},{22... | collective-permute-start | bytes 393224 | tf_op jit(solution)/shard_map/ppermute | solution.py:414
  56.9 3.9 %collective-permute-done.10.b_ref = bf16[1056,128]{1,0:T(8,128)(2,1)S(1)} collective-permute-done((bf16[1056,128]{1,0:T(8,128)(2,1)S(1)}, bf16[1056,128]{1,0:T(8,128)(2,1)S(1)}, u32[]{:S(2)}, u32[]{:S(2)}) %collective-permute-start.10) | collective-permute-done | bytes 270368 | tf_op jit(solution)/shard_map/ppermute | solution.py:414
  60.8 1.9 %collective-permute-start.11 = (bf16[1056,128]{1,0:T(8,128)(2,1)S(1)}, bf16[1056,128]{1,0:T(8,128)(2,1)S(1)}, u32[]{:S(2)}, u32[]{:S(2)}) collective-permute-start(bf16[1056,128]{1,0:T(8,128)(2,1)S(1)} %collective-permute-done.10.b_ref), channel_id=1, source_target_pairs={{0,64},{32,96},{64,128},{96,160},{128,192},{160,224},{192,256},{22... | collective-permute-start | bytes 811016 | tf_op jit(solution)/shard_map/ppermute | solution.py:414
  62.7 1.3 %shard_map.76 = (f32[1024,384]{1,0:T(8,128)S(1)}, f32[8,128]{1,0:T(8,128)}) custom-call(s32[8]{0:T(128)S(1)} %copy-done.4, f32[6,1,11]{2,1,0:T(1,128)S(1)} %bitcast.8, bf16[1536,768]{1,0:T(8,128)(2,1)S(1)} %get-tuple-element.26.qp_ref, bf16[512,128]{1,0:T(8,128)(2,1)S(1)} %collective-permute-done.7.a_ref, ...), custom_call_target="tpu_custom_call" | custom-call | flops 120259084288 | bytes 4194304 | tf_op jit(solution)/shard_map/pallas_call | solution.py:394
  64.0 0.0 collective-permute-done.9.a_ref
  64.0 7.8 %collective-permute-done.11.b_ref = bf16[1056,128]{1,0:T(8,128)(2,1)S(1)} collective-permute-done((bf16[1056,128]{1,0:T(8,128)(2,1)S(1)}, bf16[1056,128]{1,0:T(8,128)(2,1)S(1)}, u32[]{:S(2)}, u32[]{:S(2)}) %collective-permute-start.11) | collective-permute-done | bytes 270368 | tf_op jit(solution)/shard_map/ppermute | solution.py:414
  71.8 0.8 shard_map.77
  72.6 0.0 copy-start.1
  72.6 0.0 copy-start.2
  72.6 2.9 %collective-permute-start.12 = (f32[512,384]{1,0:T(8,128)S(1)}, f32[512,384]{1,0:T(8,128)S(1)}, u32[]{:S(2)}, u32[]{:S(2)}) collective-permute-start(f32[512,384]{1,0:T(8,128)S(1)} %get-tuple-element.44), channel_id=1, source_target_pairs={{0,32},{32,0},{64,96},{96,64},{128,160},{160,128},{192,224},{224,1... | collective-permute-start | bytes 2359304 | tf_op jit(solution)/shard_map/ppermute | solution.py:414
  75.5 1.9 %collective-permute-done.12.other_ref = f32[512,384]{1,0:T(8,128)S(1)} collective-permute-done((f32[512,384]{1,0:T(8,128)S(1)}, f32[512,384]{1,0:T(8,128)S(1)}, u32[]{:S(2)}, u32[]{:S(2)}) %collective-permute-start.12) | collective-permute-done | bytes 786464 | tf_op jit(solution)/shard_map/ppermute | solution.py:414
  77.4 0.4 shard_map.78
  77.8 1.9 %collective-permute-start.13 = (bf16[512,128]{1,0:T(8,128)(2,1)S(1)}, bf16[512,128]{1,0:T(8,128)(2,1)S(1)}, u32[]{:S(2)}, u32[]{:S(2)}) collective-permute-start(bf16[512,128]{1,0:T(8,128)(2,1)S(1)} %get-tuple-element.46), channel_id=1, source_target_pairs={{0,16},{1,17},{2,18},{3,19},{4,20},{5,21},{6,22},{7,23},{8,24},{9,... | collective-permute-start | bytes 393224 | tf_op jit(solution)/shard_map/ppermute | solution.py:420
  79.8 6.2 %collective-permute-done.13.cross_ref = bf16[512,128]{1,0:T(8,128)(2,1)S(1)} collective-permute-done((bf16[512,128]{1,0:T(8,128)(2,1)S(1)}, bf16[512,128]{1,0:T(8,128)(2,1)S(1)}, u32[]{:S(2)}, u32[]{:S(2)}) %collective-permute-start.13) | collective-permute-done | bytes 131104 | tf_op jit(solution)/shard_map/ppermute | solution.py:420
  86.0 0.0 copy-done.1
  86.0 0.0 copy-done.2
  86.0 1.4 %shard_map.79 = bf16[512,128]{1,0:T(8,128)(2,1)} custom-call(f32[2]{0:T(128)S(1)} %bitcast.3, f32[512,128]{1,0:T(8,128)S(1)} %get-tuple-element.45.own_ref, bf16[512,128]{1,0:T(8,128)(2,1)S(1)} %collective-permute-done.13.cross_ref, f32[1,128]{1,0:T(1,128)S(1)} %bitcast.4), custom_call_target="tpu_custom_call" | custom-call | bytes 4194304 | tf_op jit(solution)/shard_map/pallas_call | solution.py:394
  (2 shorter events, 0.0 us)
Async XLA Ops:
  1.4 12.2 %collective-permute-start = (bf16[32,128]{1,0:T(8,128)(2,1)S(1)}, bf16[32,128]{1,0:T(8,128)(2,1)S(1)}, u32[]{:S(2)}, u32[]{:S(2)}) collective-permute-start(bf16[32,128]{1,0:T(8,128)(2,1)S(1)} %pad_maximum_fusion.2), channel_id=1, source_target_pairs={{0,32},{32,64},{64,96},{96,128},{128,160},{160,192},{192,224},{224... | collective-permute-start | bytes 24584 | tf_op jit(solution)/shard_map/ppermute | solution.py:414
  4.9 29.2 %collective-permute-start.4 = (bf16[512,128]{1,0:T(8,128)(2,1)}, bf16[512,128]{1,0:T(8,128)(2,1)S(1)}, u32[]{:S(2)}, u32[]{:S(2)}) collective-permute-start(bf16[512,128]{1,0:T(8,128)(2,1)} %a_ref.1), channel_id=1, source_target_pairs={{0,64},{32,96},{64,128},{96,160},{128,192},{160,224},{192,256},{22... | collective-permute-start | bytes 393224 | tf_op jit(solution)/shard_map/ppermute | solution.py:414
  8.9 12.2 %collective-permute-start.3 = (bf16[16,128]{1,0:T(8,128)(2,1)S(1)}, bf16[16,128]{1,0:T(8,128)(2,1)S(1)}, u32[]{:S(2)}, u32[]{:S(2)}) collective-permute-start(bf16[16,128]{1,0:T(8,128)(2,1)S(1)} %get-tuple-element.47), channel_id=1, source_target_pairs={{0,480},{32,0},{64,32},{96,64},{128,96},{160,128},{192,160},{224,1... | collective-permute-start | bytes 12296 | tf_op jit(solution)/shard_map/ppermute | solution.py:414
  10.2 10.9 %collective-permute-start.2 = (bf16[512,128]{1,0:T(8,128)(2,1)}, bf16[512,128]{1,0:T(8,128)(2,1)S(1)}, u32[]{:S(2)}, u32[]{:S(2)}) collective-permute-start(bf16[512,128]{1,0:T(8,128)(2,1)} %param.9), channel_id=1, source_target_pairs={{0,16},{1,17},{2,18},{3,19},{4,20},{5,21},{6,22},{7,23},{8,24},{9,... | collective-permute-start | bytes 393224 | tf_op jit(solution)/shard_map/ppermute | solution.py:420
  14.5 9.5 %collective-permute-start.1 = (bf16[528,128]{1,0:T(8,128)(2,1)S(1)}, bf16[528,128]{1,0:T(8,128)(2,1)S(1)}, u32[]{:S(2)}, u32[]{:S(2)}) collective-permute-start(bf16[528,128]{1,0:T(8,128)(2,1)S(1)} %pad_maximum_fusion.1.own_ref), channel_id=1, source_target_pairs={{0,32},{32,0},{64,96},{96,64},{128,160},{160,128},{192,224},{224,1... | collective-permute-start | bytes 405512 | tf_op jit(solution)/shard_map/ppermute | solution.py:414
  22.1 14.6 %collective-permute-start.6 = (bf16[1056,128]{1,0:T(8,128)(2,1)S(1)}, bf16[1056,128]{1,0:T(8,128)(2,1)S(1)}, u32[]{:S(2)}, u32[]{:S(2)}) collective-permute-start(bf16[1056,128]{1,0:T(8,128)(2,1)S(1)} %pad_maximum_fusion.b_ref), channel_id=1, source_target_pairs={{0,64},{32,96},{64,128},{96,160},{128,192},{160,224},{192,256},{22... | collective-permute-start | bytes 811016 | tf_op jit(solution)/shard_map/ppermute | solution.py:414
  24.0 0.9 %copy-start = (bf16[512,128]{1,0:T(8,128)(2,1)S(1)}, bf16[512,128]{1,0:T(8,128)(2,1)}, u32[]{:S(2)}) copy-start(bf16[512,128]{1,0:T(8,128)(2,1)} %a_ref.1) | copy-start | bytes 393220
  24.9 0.7 copy-start.3
  25.6 0.7 copy-start.4
  34.1 7.6 %collective-permute-start.5 = (bf16[512,128]{1,0:T(8,128)(2,1)S(1)}, bf16[512,128]{1,0:T(8,128)(2,1)S(1)}, u32[]{:S(2)}, u32[]{:S(2)}) collective-permute-start(bf16[512,128]{1,0:T(8,128)(2,1)S(1)} %collective-permute-done.4.a_ref), channel_id=1, source_target_pairs={{0,64},{32,96},{64,128},{96,160},{128,192},{160,224},{192,256},{22... | collective-permute-start | bytes 393224 | tf_op jit(solution)/shard_map/ppermute | solution.py:414
  36.7 13.4 %collective-permute-start.8 = (bf16[1056,128]{1,0:T(8,128)(2,1)S(1)}, bf16[1056,128]{1,0:T(8,128)(2,1)S(1)}, u32[]{:S(2)}, u32[]{:S(2)}) collective-permute-start(bf16[1056,128]{1,0:T(8,128)(2,1)S(1)} %collective-permute-done.6.b_ref), channel_id=1, source_target_pairs={{0,64},{32,96},{64,128},{96,160},{128,192},{160,224},{192,256},{22... | collective-permute-start | bytes 811016 | tf_op jit(solution)/shard_map/ppermute | solution.py:414
  41.7 12.1 %collective-permute-start.7 = (bf16[512,128]{1,0:T(8,128)(2,1)S(1)}, bf16[512,128]{1,0:T(8,128)(2,1)S(1)}, u32[]{:S(2)}, u32[]{:S(2)}) collective-permute-start(bf16[512,128]{1,0:T(8,128)(2,1)S(1)} %collective-permute-done.5.a_ref), channel_id=1, source_target_pairs={{0,64},{32,96},{64,128},{96,160},{128,192},{160,224},{192,256},{22... | collective-permute-start | bytes 393224 | tf_op jit(solution)/shard_map/ppermute | solution.py:414
  50.0 10.7 %collective-permute-start.10 = (bf16[1056,128]{1,0:T(8,128)(2,1)S(1)}, bf16[1056,128]{1,0:T(8,128)(2,1)S(1)}, u32[]{:S(2)}, u32[]{:S(2)}) collective-permute-start(bf16[1056,128]{1,0:T(8,128)(2,1)S(1)} %collective-permute-done.8.b_ref), channel_id=1, source_target_pairs={{0,64},{32,96},{64,128},{96,160},{128,192},{160,224},{192,256},{22... | collective-permute-start | bytes 811016 | tf_op jit(solution)/shard_map/ppermute | solution.py:414
  53.8 10.2 %collective-permute-start.9 = (bf16[512,128]{1,0:T(8,128)(2,1)S(1)}, bf16[512,128]{1,0:T(8,128)(2,1)S(1)}, u32[]{:S(2)}, u32[]{:S(2)}) collective-permute-start(bf16[512,128]{1,0:T(8,128)(2,1)S(1)} %collective-permute-done.7.a_ref), channel_id=1, source_target_pairs={{0,64},{32,96},{64,128},{96,160},{128,192},{160,224},{192,256},{22... | collective-permute-start | bytes 393224 | tf_op jit(solution)/shard_map/ppermute | solution.py:414
  60.8 11.0 %collective-permute-start.11 = (bf16[1056,128]{1,0:T(8,128)(2,1)S(1)}, bf16[1056,128]{1,0:T(8,128)(2,1)S(1)}, u32[]{:S(2)}, u32[]{:S(2)}) collective-permute-start(bf16[1056,128]{1,0:T(8,128)(2,1)S(1)} %collective-permute-done.10.b_ref), channel_id=1, source_target_pairs={{0,64},{32,96},{64,128},{96,160},{128,192},{160,224},{192,256},{22... | collective-permute-start | bytes 811016 | tf_op jit(solution)/shard_map/ppermute | solution.py:414
  72.6 13.3 %copy-start.1 = (f32[1,2]{1,0:T(1,128)S(1)}, f32[1,2]{1,0:T(1,128)}, u32[]{:S(2)}) copy-start(f32[1,2]{1,0:T(1,128)} %param.11) | copy-start | bytes 28
  72.6 13.3 %copy-start.2 = (f32[128]{0:T(128)S(1)}, f32[128]{0:T(128)}, u32[]{:S(2)}) copy-start(f32[128]{0:T(128)} %param.12) | copy-start | bytes 1540
  72.6 4.8 %collective-permute-start.12 = (f32[512,384]{1,0:T(8,128)S(1)}, f32[512,384]{1,0:T(8,128)S(1)}, u32[]{:S(2)}, u32[]{:S(2)}) collective-permute-start(f32[512,384]{1,0:T(8,128)S(1)} %get-tuple-element.44), channel_id=1, source_target_pairs={{0,32},{32,0},{64,96},{96,64},{128,160},{160,128},{192,224},{224,1... | collective-permute-start | bytes 2359304 | tf_op jit(solution)/shard_map/ppermute | solution.py:414
  77.8 8.1 %collective-permute-start.13 = (bf16[512,128]{1,0:T(8,128)(2,1)S(1)}, bf16[512,128]{1,0:T(8,128)(2,1)S(1)}, u32[]{:S(2)}, u32[]{:S(2)}) collective-permute-start(bf16[512,128]{1,0:T(8,128)(2,1)S(1)} %get-tuple-element.46), channel_id=1, source_target_pairs={{0,16},{1,17},{2,18},{3,19},{4,20},{5,21},{6,22},{7,23},{8,24},{9,... | collective-permute-start | bytes 393224 | tf_op jit(solution)/shard_map/ppermute | solution.py:420

commit v7 on v6

--- a/solution.py
+++ b/solution.py
@@ -451,7 +451,9 @@
     )
     for hop in range(1, HOPS + 1):
         ring_a, ring_b = onward(ring_a), onward(ring_b)
-        ring_a, _ = lax.optimization_barrier((ring_a, done))
+        if hop > 1:
+            ring_a, _ = lax.optimization_barrier((ring_a, before))
+        before = done
         ring_b, _ = lax.optimization_barrier((ring_b, done))
         last = hop == HOPS
         out = [((rows, 3 * HEAD_DIM), f32)] * 2 if last else state + mark

time: 88 us -> 88.8 us (level)
  starting transfers between devices: 47.5 us -> 53.6 us
  waiting for transfers between devices: 19.8 us -> 15 us
    ppermute x12, starting transfers between devices: 42.2 us -> 46 us  [permute(): return lax.ppermute(value, 'ctx', pairs)]
    ppermute x12, waiting for transfers between devices: 13.6 us -> 11.2 us  [permute(): return lax.ppermute(value, 'ctx', pairs)]
    ppermute x2, starting transfers between devices: 5.27 us -> 7.65 us  [partner(): lax.ppermute(value, 'head', [(i, i ^ heads // 2) for i in range(heads)])]
    ppermute x2, waiting for transfers between devices: 6.18 us -> 3.81 us  [partner(): lax.ppermute(value, 'head', [(i, i ^ heads // 2) for i in range(heads)])]
where the time goes in v7:
time: 88.8 us; the launch traced here: 88.3 us
  starting transfers between devices  53.6 us (60%)
  waiting for transfers between devices  15 us (17%)
  Pallas kernels  14 us (16%)
  local copies, waits for them, and re-layouts  3.65 us (4%)
  other arithmetic  1.85 us (2%)
    ppermute x12, starting transfers between devices, permute(): return lax.ppermute(value, 'ctx', pairs)  46 us
    pallas_call x7, Pallas kernels, call(): pl.pallas_call(kernel, out_shape=shapes, in_specs=specs, out_specs=[VMEM]...  14 us
    ppermute x12, waiting for transfers between devices, permute(): return lax.ppermute(value, 'ctx', pairs)  11.2 us
    ppermute x2, starting transfers between devices, partner(): lax.ppermute(value, 'head', [(i, i ^ heads // 2) for i in range(heads)])  7.65 us
    ppermute x2, waiting for transfers between devices, partner(): lax.ppermute(value, 'head', [(i, i ^ heads // 2) for i in range(heads)])  3.81 us
    unnamed x10, local copies, waits for them, and re-layouts  2.25 us
  transfers between devices with their start and end apart: 14, of which 4 were waited for; matrix products, arithmetic and copies ran while one was open for 2% of the time, Pallas kernels for 13%

profile of v7, /device:TPU:1, one launch (start us, length us, event | category | flops | bytes accessed | tf_op | source)
XLA Modules:
  0.0 88.3 jit_solution(11812993226751200139)
XLA Ops:
  0.0 0.7 fusion
  0.7 0.7 slice.16
  1.4 3.5 %collective-permute-start = (bf16[32,128]{1,0:T(8,128)(2,1)S(1)}, bf16[32,128]{1,0:T(8,128)(2,1)S(1)}, u32[]{:S(2)}, u32[]{:S(2)}) collective-permute-start(bf16[32,128]{1,0:T(8,128)(2,1)S(1)} %pad_maximum_fusion.2), channel_id=1, source_target_pairs={{0,32},{32,64},{64,96},{96,128},{128,160},{160,192},{192,224},{224... | collective-permute-start | bytes 24584 | tf_op jit(solution)/shard_map/ppermute | solution.py:414
  4.9 4.0 %collective-permute-start.4 = (bf16[512,128]{1,0:T(8,128)(2,1)}, bf16[512,128]{1,0:T(8,128)(2,1)S(1)}, u32[]{:S(2)}, u32[]{:S(2)}) collective-permute-start(bf16[512,128]{1,0:T(8,128)(2,1)} %a_ref.1), channel_id=1, source_target_pairs={{0,64},{32,96},{64,128},{96,160},{128,192},{160,224},{192,256},{22... | collective-permute-start | bytes 393224 | tf_op jit(solution)/shard_map/ppermute | solution.py:414
  8.9 1.3 %collective-permute-start.3 = (bf16[16,128]{1,0:T(8,128)(2,1)S(1)}, bf16[16,128]{1,0:T(8,128)(2,1)S(1)}, u32[]{:S(2)}, u32[]{:S(2)}) collective-permute-start(bf16[16,128]{1,0:T(8,128)(2,1)S(1)} %get-tuple-element.41), channel_id=1, source_target_pairs={{0,480},{32,0},{64,32},{96,64},{128,96},{160,128},{192,160},{224,1... | collective-permute-start | bytes 12296 | tf_op jit(solution)/shard_map/ppermute | solution.py:414
  10.2 3.3 %collective-permute-start.2 = (bf16[512,128]{1,0:T(8,128)(2,1)}, bf16[512,128]{1,0:T(8,128)(2,1)S(1)}, u32[]{:S(2)}, u32[]{:S(2)}) collective-permute-start(bf16[512,128]{1,0:T(8,128)(2,1)} %param.9), channel_id=1, source_target_pairs={{0,16},{1,17},{2,18},{3,19},{4,20},{5,21},{6,22},{7,23},{8,24},{9,... | collective-permute-start | bytes 393224 | tf_op jit(solution)/shard_map/ppermute | solution.py:420
  13.6 0.0 collective-permute-done.edge_ref
  13.6 0.9 %pad_maximum_fusion.1.own_ref = bf16[528,128]{1,0:T(8,128)(2,1)S(1)} fusion(bf16[16,128]{1,0:T(8,128)(2,1)S(1)} %get-tuple-element.44, bf16[512,128]{1,0:T(8,128)(2,1)} %param.7), kind=kLoop, calls=%fused_computation.1 | loop fusion | flops 270336 | bytes 270336 | tf_op jit(solution)/shard_map/concatenate | solution.py:428
  14.5 6.6 %collective-permute-start.1 = (bf16[528,128]{1,0:T(8,128)(2,1)S(1)}, bf16[528,128]{1,0:T(8,128)(2,1)S(1)}, u32[]{:S(2)}, u32[]{:S(2)}) collective-permute-start(bf16[528,128]{1,0:T(8,128)(2,1)S(1)} %pad_maximum_fusion.1.own_ref), channel_id=1, source_target_pairs={{0,32},{32,0},{64,96},{96,64},{128,160},{160,128},{192,224},{224,1... | collective-permute-start | bytes 405512 | tf_op jit(solution)/shard_map/ppermute | solution.py:414
  21.1 0.0 collective-permute-done.3
  21.1 0.0 collective-permute-done.2
  21.1 0.9 %pad_maximum_fusion.b_ref = bf16[1056,128]{1,0:T(8,128)(2,1)S(1)} fusion(bf16[16,128]{1,0:T(8,128)(2,1)S(1)} %collective-permute-done.3, bf16[16,128]{1,0:T(8,128)(2,1)S(1)} %get-tuple-element.43, bf16[512,128]{1,0:T(8,128)(2,1)S(1)} %collective-permute-done.2, bf16[512,128]{1,0:T(8,128)(2,1)} %param.9), kind=kLoop, calls=%fused_computation | loop fusion | flops 1081344 | bytes 540672 | tf_op jit(solution)/shard_map/concatenate | solution.py:432
  22.1 1.9 %collective-permute-start.7 = (bf16[1056,128]{1,0:T(8,128)(2,1)S(1)}, bf16[1056,128]{1,0:T(8,128)(2,1)S(1)}, u32[]{:S(2)}, u32[]{:S(2)}) collective-permute-start(bf16[1056,128]{1,0:T(8,128)(2,1)S(1)} %pad_maximum_fusion.b_ref), channel_id=1, source_target_pairs={{0,64},{32,96},{64,128},{96,160},{128,192},{160,224},{192,256},{22... | collective-permute-start | bytes 811016 | tf_op jit(solution)/shard_map/ppermute | solution.py:414
  24.0 0.0 collective-permute-done.4.a_ref
  24.0 2.9 %collective-permute-start.5 = (bf16[512,128]{1,0:T(8,128)(2,1)S(1)}, bf16[512,128]{1,0:T(8,128)(2,1)S(1)}, u32[]{:S(2)}, u32[]{:S(2)}) collective-permute-start(bf16[512,128]{1,0:T(8,128)(2,1)S(1)} %collective-permute-done.4.a_ref), channel_id=1, source_target_pairs={{0,64},{32,96},{64,128},{96,160},{128,192},{160,224},{192,256},{22... | collective-permute-start | bytes 393224 | tf_op jit(solution)/shard_map/ppermute | solution.py:414
  26.9 0.0 collective-permute-done.1.other_ref
  26.9 0.0 copy-start
  26.9 0.9 %copy-done = bf16[512,128]{1,0:T(8,128)(2,1)S(1)} copy-done((bf16[512,128]{1,0:T(8,128)(2,1)S(1)}, bf16[512,128]{1,0:T(8,128)(2,1)}, u32[]{:S(2)}) %copy-start) | copy-done | bytes 131096
  27.8 0.0 copy-start.3
  27.8 0.7 copy-done.3
  28.5 0.0 copy-start.4
  28.5 0.7 copy-done.4
  29.2 7.5 %shard_map.73 = (bf16[1536,768]{1,0:T(8,128)(2,1)S(1)}, f32[1024,384]{1,0:T(8,128)S(1)}, f32[8,128]{1,0:T(8,128)}) custom-call(s32[8]{0:T(128)S(1)} %copy-done.4, f32[6,1,11]{2,1,0:T(1,128)S(1)} %bitcast.5, bf16[528,128]{1,0:T(8,128)(2,1)S(1)} %pad_maximum_fusion.1.own_ref, bf16[528,128]{1,0:T(8,128)(2,1)S(1)} %collective-permute-done.1.other_ref, ...), custom_call_target="tpu_custom_call" | custom-call | flops 120259084288 | bytes 4194304 | tf_op jit(solution)/shard_map/pallas_call | solution.py:394
  36.6 0.0 collective-permute-done.5.a_ref
  36.6 3.7 %collective-permute-start.6 = (bf16[512,128]{1,0:T(8,128)(2,1)S(1)}, bf16[512,128]{1,0:T(8,128)(2,1)S(1)}, u32[]{:S(2)}, u32[]{:S(2)}) collective-permute-start(bf16[512,128]{1,0:T(8,128)(2,1)S(1)} %collective-permute-done.5.a_ref), channel_id=1, source_target_pairs={{0,64},{32,96},{64,128},{96,160},{128,192},{160,224},{192,256},{22... | collective-permute-start | bytes 393224 | tf_op jit(solution)/shard_map/ppermute | solution.py:414
  40.4 0.0 collective-permute-done.7.b_ref
  40.4 4.3 %collective-permute-start.9 = (bf16[1056,128]{1,0:T(8,128)(2,1)S(1)}, bf16[1056,128]{1,0:T(8,128)(2,1)S(1)}, u32[]{:S(2)}, u32[]{:S(2)}) collective-permute-start(bf16[1056,128]{1,0:T(8,128)(2,1)S(1)} %collective-permute-done.7.b_ref), channel_id=1, source_target_pairs={{0,64},{32,96},{64,128},{96,160},{128,192},{160,224},{192,256},{22... | collective-permute-start | bytes 811016 | tf_op jit(solution)/shard_map/ppermute | solution.py:414
  44.7 1.3 %shard_map.74 = (f32[1024,384]{1,0:T(8,128)S(1)}, f32[8,128]{1,0:T(8,128)}) custom-call(s32[8]{0:T(128)S(1)} %copy-done.4, f32[6,1,11]{2,1,0:T(1,128)S(1)} %bitcast.6, bf16[1536,768]{1,0:T(8,128)(2,1)S(1)} %get-tuple-element.23.qp_ref, bf16[512,128]{1,0:T(8,128)(2,1)S(1)} %collective-permute-done.4.a_ref, ...), custom_call_target="tpu_custom_call" | custom-call | flops 120259084288 | bytes 4194304 | tf_op jit(solution)/shard_map/pallas_call | solution.py:394
  46.0 0.0 collective-permute-done.6.a_ref
  46.0 5.9 %collective-permute-start.8 = (bf16[512,128]{1,0:T(8,128)(2,1)S(1)}, bf16[512,128]{1,0:T(8,128)(2,1)S(1)}, u32[]{:S(2)}, u32[]{:S(2)}) collective-permute-start(bf16[512,128]{1,0:T(8,128)(2,1)S(1)} %collective-permute-done.6.a_ref), channel_id=1, source_target_pairs={{0,64},{32,96},{64,128},{96,160},{128,192},{160,224},{192,256},{22... | collective-permute-start | bytes 393224 | tf_op jit(solution)/shard_map/ppermute | solution.py:414
  52.0 0.0 collective-permute-done.9.b_ref
  52.0 3.2 %collective-permute-start.10 = (bf16[1056,128]{1,0:T(8,128)(2,1)S(1)}, bf16[1056,128]{1,0:T(8,128)(2,1)S(1)}, u32[]{:S(2)}, u32[]{:S(2)}) collective-permute-start(bf16[1056,128]{1,0:T(8,128)(2,1)S(1)} %collective-permute-done.9.b_ref), channel_id=1, source_target_pairs={{0,64},{32,96},{64,128},{96,160},{128,192},{160,224},{192,256},{22... | collective-permute-start | bytes 811016 | tf_op jit(solution)/shard_map/ppermute | solution.py:414
  55.2 1.3 %shard_map.75 = (f32[1024,384]{1,0:T(8,128)S(1)}, f32[8,128]{1,0:T(8,128)}) custom-call(s32[8]{0:T(128)S(1)} %copy-done.4, f32[6,1,11]{2,1,0:T(1,128)S(1)} %bitcast.7, bf16[1536,768]{1,0:T(8,128)(2,1)S(1)} %get-tuple-element.23.qp_ref, bf16[512,128]{1,0:T(8,128)(2,1)S(1)} %collective-permute-done.5.a_ref, ...), custom_call_target="tpu_custom_call" | custom-call | flops 120259084288 | bytes 4194304 | tf_op jit(solution)/shard_map/pallas_call | solution.py:394
  56.5 0.0 collective-permute-done.8.a_ref
  56.5 4.6 %collective-permute-done.10.b_ref = bf16[1056,128]{1,0:T(8,128)(2,1)S(1)} collective-permute-done((bf16[1056,128]{1,0:T(8,128)(2,1)S(1)}, bf16[1056,128]{1,0:T(8,128)(2,1)S(1)}, u32[]{:S(2)}, u32[]{:S(2)}) %collective-permute-start.10) | collective-permute-done | bytes 270368 | tf_op jit(solution)/shard_map/ppermute | solution.py:414
  61.2 2.5 %collective-permute-start.11 = (bf16[1056,128]{1,0:T(8,128)(2,1)S(1)}, bf16[1056,128]{1,0:T(8,128)(2,1)S(1)}, u32[]{:S(2)}, u32[]{:S(2)}) collective-permute-start(bf16[1056,128]{1,0:T(8,128)(2,1)S(1)} %collective-permute-done.10.b_ref), channel_id=1, source_target_pairs={{0,64},{32,96},{64,128},{96,160},{128,192},{160,224},{192,256},{22... | collective-permute-start | bytes 811016 | tf_op jit(solution)/shard_map/ppermute | solution.py:414
  63.7 1.3 %shard_map.76 = (f32[1024,384]{1,0:T(8,128)S(1)}, f32[8,128]{1,0:T(8,128)}) custom-call(s32[8]{0:T(128)S(1)} %copy-done.4, f32[6,1,11]{2,1,0:T(1,128)S(1)} %bitcast.8, bf16[1536,768]{1,0:T(8,128)(2,1)S(1)} %get-tuple-element.23.qp_ref, bf16[512,128]{1,0:T(8,128)(2,1)S(1)} %collective-permute-done.6.a_ref, ...), custom_call_target="tpu_custom_call" | custom-call | flops 120259084288 | bytes 4194304 | tf_op jit(solution)/shard_map/pallas_call | solution.py:394
  65.0 4.6 %collective-permute-done.11.b_ref = bf16[1056,128]{1,0:T(8,128)(2,1)S(1)} collective-permute-done((bf16[1056,128]{1,0:T(8,128)(2,1)S(1)}, bf16[1056,128]{1,0:T(8,128)(2,1)S(1)}, u32[]{:S(2)}, u32[]{:S(2)}) %collective-permute-start.11) | collective-permute-done | bytes 270368 | tf_op jit(solution)/shard_map/ppermute | solution.py:414
  69.6 0.8 shard_map.77
  70.4 0.0 copy-start.1
  70.4 0.0 copy-start.2
  70.4 6.0 %collective-permute-start.12 = (f32[512,384]{1,0:T(8,128)S(1)}, f32[512,384]{1,0:T(8,128)S(1)}, u32[]{:S(2)}, u32[]{:S(2)}) collective-permute-start(f32[512,384]{1,0:T(8,128)S(1)} %get-tuple-element.38), channel_id=1, source_target_pairs={{0,32},{32,0},{64,96},{96,64},{128,160},{160,128},{192,224},{224,1... | collective-permute-start | bytes 2359304 | tf_op jit(solution)/shard_map/ppermute | solution.py:414
  76.5 1.9 %collective-permute-done.12.other_ref = f32[512,384]{1,0:T(8,128)S(1)} collective-permute-done((f32[512,384]{1,0:T(8,128)S(1)}, f32[512,384]{1,0:T(8,128)S(1)}, u32[]{:S(2)}, u32[]{:S(2)}) %collective-permute-start.12) | collective-permute-done | bytes 786464 | tf_op jit(solution)/shard_map/ppermute | solution.py:414
  78.4 0.4 shard_map.78
  78.8 4.3 %collective-permute-start.13 = (bf16[512,128]{1,0:T(8,128)(2,1)S(1)}, bf16[512,128]{1,0:T(8,128)(2,1)S(1)}, u32[]{:S(2)}, u32[]{:S(2)}) collective-permute-start(bf16[512,128]{1,0:T(8,128)(2,1)S(1)} %get-tuple-element.40), channel_id=1, source_target_pairs={{0,16},{1,17},{2,18},{3,19},{4,20},{5,21},{6,22},{7,23},{8,24},{9,... | collective-permute-start | bytes 393224 | tf_op jit(solution)/shard_map/ppermute | solution.py:420
  83.1 3.8 %collective-permute-done.13.cross_ref = bf16[512,128]{1,0:T(8,128)(2,1)S(1)} collective-permute-done((bf16[512,128]{1,0:T(8,128)(2,1)S(1)}, bf16[512,128]{1,0:T(8,128)(2,1)S(1)}, u32[]{:S(2)}, u32[]{:S(2)}) %collective-permute-start.13) | collective-permute-done | bytes 131104 | tf_op jit(solution)/shard_map/ppermute | solution.py:420
  86.9 0.0 copy-done.1
  86.9 0.0 copy-done.2
  86.9 1.4 %shard_map.79 = bf16[512,128]{1,0:T(8,128)(2,1)} custom-call(f32[2]{0:T(128)S(1)} %bitcast.3, f32[512,128]{1,0:T(8,128)S(1)} %get-tuple-element.39.own_ref, bf16[512,128]{1,0:T(8,128)(2,1)S(1)} %collective-permute-done.13.cross_ref, f32[1,128]{1,0:T(1,128)S(1)} %bitcast.4), custom_call_target="tpu_custom_call" | custom-call | bytes 4194304 | tf_op jit(solution)/shard_map/pallas_call | solution.py:394
  (2 shorter events, 0.0 us)
Async XLA Ops:
  1.4 12.2 %collective-permute-start = (bf16[32,128]{1,0:T(8,128)(2,1)S(1)}, bf16[32,128]{1,0:T(8,128)(2,1)S(1)}, u32[]{:S(2)}, u32[]{:S(2)}) collective-permute-start(bf16[32,128]{1,0:T(8,128)(2,1)S(1)} %pad_maximum_fusion.2), channel_id=1, source_target_pairs={{0,32},{32,64},{64,96},{96,128},{128,160},{160,192},{192,224},{224... | collective-permute-start | bytes 24584 | tf_op jit(solution)/shard_map/ppermute | solution.py:414
  4.9 19.1 %collective-permute-start.4 = (bf16[512,128]{1,0:T(8,128)(2,1)}, bf16[512,128]{1,0:T(8,128)(2,1)S(1)}, u32[]{:S(2)}, u32[]{:S(2)}) collective-permute-start(bf16[512,128]{1,0:T(8,128)(2,1)} %a_ref.1), channel_id=1, source_target_pairs={{0,64},{32,96},{64,128},{96,160},{128,192},{160,224},{192,256},{22... | collective-permute-start | bytes 393224 | tf_op jit(solution)/shard_map/ppermute | solution.py:414
  8.9 12.2 %collective-permute-start.3 = (bf16[16,128]{1,0:T(8,128)(2,1)S(1)}, bf16[16,128]{1,0:T(8,128)(2,1)S(1)}, u32[]{:S(2)}, u32[]{:S(2)}) collective-permute-start(bf16[16,128]{1,0:T(8,128)(2,1)S(1)} %get-tuple-element.41), channel_id=1, source_target_pairs={{0,480},{32,0},{64,32},{96,64},{128,96},{160,128},{192,160},{224,1... | collective-permute-start | bytes 12296 | tf_op jit(solution)/shard_map/ppermute | solution.py:414
  10.2 10.9 %collective-permute-start.2 = (bf16[512,128]{1,0:T(8,128)(2,1)}, bf16[512,128]{1,0:T(8,128)(2,1)S(1)}, u32[]{:S(2)}, u32[]{:S(2)}) collective-permute-start(bf16[512,128]{1,0:T(8,128)(2,1)} %param.9), channel_id=1, source_target_pairs={{0,16},{1,17},{2,18},{3,19},{4,20},{5,21},{6,22},{7,23},{8,24},{9,... | collective-permute-start | bytes 393224 | tf_op jit(solution)/shard_map/ppermute | solution.py:420
  14.5 12.4 %collective-permute-start.1 = (bf16[528,128]{1,0:T(8,128)(2,1)S(1)}, bf16[528,128]{1,0:T(8,128)(2,1)S(1)}, u32[]{:S(2)}, u32[]{:S(2)}) collective-permute-start(bf16[528,128]{1,0:T(8,128)(2,1)S(1)} %pad_maximum_fusion.1.own_ref), channel_id=1, source_target_pairs={{0,32},{32,0},{64,96},{96,64},{128,160},{160,128},{192,224},{224,1... | collective-permute-start | bytes 405512 | tf_op jit(solution)/shard_map/ppermute | solution.py:414
  22.1 18.3 %collective-permute-start.7 = (bf16[1056,128]{1,0:T(8,128)(2,1)S(1)}, bf16[1056,128]{1,0:T(8,128)(2,1)S(1)}, u32[]{:S(2)}, u32[]{:S(2)}) collective-permute-start(bf16[1056,128]{1,0:T(8,128)(2,1)S(1)} %pad_maximum_fusion.b_ref), channel_id=1, source_target_pairs={{0,64},{32,96},{64,128},{96,160},{128,192},{160,224},{192,256},{22... | collective-permute-start | bytes 811016 | tf_op jit(solution)/shard_map/ppermute | solution.py:414
  24.0 12.6 %collective-permute-start.5 = (bf16[512,128]{1,0:T(8,128)(2,1)S(1)}, bf16[512,128]{1,0:T(8,128)(2,1)S(1)}, u32[]{:S(2)}, u32[]{:S(2)}) collective-permute-start(bf16[512,128]{1,0:T(8,128)(2,1)S(1)} %collective-permute-done.4.a_ref), channel_id=1, source_target_pairs={{0,64},{32,96},{64,128},{96,160},{128,192},{160,224},{192,256},{22... | collective-permute-start | bytes 393224 | tf_op jit(solution)/shard_map/ppermute | solution.py:414
  26.9 0.9 %copy-start = (bf16[512,128]{1,0:T(8,128)(2,1)S(1)}, bf16[512,128]{1,0:T(8,128)(2,1)}, u32[]{:S(2)}) copy-start(bf16[512,128]{1,0:T(8,128)(2,1)} %a_ref.1) | copy-start | bytes 393220
  27.8 0.7 copy-start.3
  28.5 0.7 copy-start.4
  36.6 9.4 %collective-permute-start.6 = (bf16[512,128]{1,0:T(8,128)(2,1)S(1)}, bf16[512,128]{1,0:T(8,128)(2,1)S(1)}, u32[]{:S(2)}, u32[]{:S(2)}) collective-permute-start(bf16[512,128]{1,0:T(8,128)(2,1)S(1)} %collective-permute-done.5.a_ref), channel_id=1, source_target_pairs={{0,64},{32,96},{64,128},{96,160},{128,192},{160,224},{192,256},{22... | collective-permute-start | bytes 393224 | tf_op jit(solution)/shard_map/ppermute | solution.py:414
  40.4 11.6 %collective-permute-start.9 = (bf16[1056,128]{1,0:T(8,128)(2,1)S(1)}, bf16[1056,128]{1,0:T(8,128)(2,1)S(1)}, u32[]{:S(2)}, u32[]{:S(2)}) collective-permute-start(bf16[1056,128]{1,0:T(8,128)(2,1)S(1)} %collective-permute-done.7.b_ref), channel_id=1, source_target_pairs={{0,64},{32,96},{64,128},{96,160},{128,192},{160,224},{192,256},{22... | collective-permute-start | bytes 811016 | tf_op jit(solution)/shard_map/ppermute | solution.py:414
  46.0 10.5 %collective-permute-start.8 = (bf16[512,128]{1,0:T(8,128)(2,1)S(1)}, bf16[512,128]{1,0:T(8,128)(2,1)S(1)}, u32[]{:S(2)}, u32[]{:S(2)}) collective-permute-start(bf16[512,128]{1,0:T(8,128)(2,1)S(1)} %collective-permute-done.6.a_ref), channel_id=1, source_target_pairs={{0,64},{32,96},{64,128},{96,160},{128,192},{160,224},{192,256},{22... | collective-permute-start | bytes 393224 | tf_op jit(solution)/shard_map/ppermute | solution.py:414
  52.0 9.2 %collective-permute-start.10 = (bf16[1056,128]{1,0:T(8,128)(2,1)S(1)}, bf16[1056,128]{1,0:T(8,128)(2,1)S(1)}, u32[]{:S(2)}, u32[]{:S(2)}) collective-permute-start(bf16[1056,128]{1,0:T(8,128)(2,1)S(1)} %collective-permute-done.9.b_ref), channel_id=1, source_target_pairs={{0,64},{32,96},{64,128},{96,160},{128,192},{160,224},{192,256},{22... | collective-permute-start | bytes 811016 | tf_op jit(solution)/shard_map/ppermute | solution.py:414
  61.2 8.4 %collective-permute-start.11 = (bf16[1056,128]{1,0:T(8,128)(2,1)S(1)}, bf16[1056,128]{1,0:T(8,128)(2,1)S(1)}, u32[]{:S(2)}, u32[]{:S(2)}) collective-permute-start(bf16[1056,128]{1,0:T(8,128)(2,1)S(1)} %collective-permute-done.10.b_ref), channel_id=1, source_target_pairs={{0,64},{32,96},{64,128},{96,160},{128,192},{160,224},{192,256},{22... | collective-permute-start | bytes 811016 | tf_op jit(solution)/shard_map/ppermute | solution.py:414
  70.4 16.5 %copy-start.1 = (f32[1,2]{1,0:T(1,128)S(1)}, f32[1,2]{1,0:T(1,128)}, u32[]{:S(2)}) copy-start(f32[1,2]{1,0:T(1,128)} %param.11) | copy-start | bytes 28
  70.4 16.5 %copy-start.2 = (f32[128]{0:T(128)S(1)}, f32[128]{0:T(128)}, u32[]{:S(2)}) copy-start(f32[128]{0:T(128)} %param.12) | copy-start | bytes 1540
  70.4 7.9 %collective-permute-start.12 = (f32[512,384]{1,0:T(8,128)S(1)}, f32[512,384]{1,0:T(8,128)S(1)}, u32[]{:S(2)}, u32[]{:S(2)}) collective-permute-start(f32[512,384]{1,0:T(8,128)S(1)} %get-tuple-element.38), channel_id=1, source_target_pairs={{0,32},{32,0},{64,96},{96,64},{128,160},{160,128},{192,224},{224,1... | collective-permute-start | bytes 2359304 | tf_op jit(solution)/shard_map/ppermute | solution.py:414
  78.8 8.1 %collective-permute-start.13 = (bf16[512,128]{1,0:T(8,128)(2,1)S(1)}, bf16[512,128]{1,0:T(8,128)(2,1)S(1)}, u32[]{:S(2)}, u32[]{:S(2)}) collective-permute-start(bf16[512,128]{1,0:T(8,128)(2,1)S(1)} %get-tuple-element.40), channel_id=1, source_target_pairs={{0,16},{1,17},{2,18},{3,19},{4,20},{5,21},{6,22},{7,23},{8,24},{9,... | collective-permute-start | bytes 393224 | tf_op jit(solution)/shard_map/ppermute | solution.py:420

commit v8 on v6

--- a/solution.py
+++ b/solution.py
@@ -357,7 +357,7 @@
 
         convolve(False, block, first_start, ends, qp_ref, kx_ref, kp_ref)
         source = state_ref if first else state_in
-        far(2 if last else 4, chip_row, block, ends, qp_ref, kp_ref, vx_ref, source, state_ref)
+        far(4, chip_row, block, ends, qp_ref, kp_ref, vx_ref, source, state_ref)
 
     if last:
         for ref, side in ((keep_ref, core), (send_ref, 1 - core)):

time: 88 us -> 87.8 us (level)
  starting transfers between devices: 47.5 us -> 54.1 us
  waiting for transfers between devices: 19.8 us -> 13.8 us
    ppermute x12, starting transfers between devices: 42.2 us -> 47 us  [permute(): return lax.ppermute(value, 'ctx', pairs)]
    ppermute x12, waiting for transfers between devices: 13.6 us -> 9.4 us  [permute(): return lax.ppermute(value, 'ctx', pairs)]
    ppermute x2, starting transfers between devices: 5.27 us -> 7.07 us  [partner(): lax.ppermute(value, 'head', [(i, i ^ heads // 2) for i in range(heads)])]
    ppermute x2, waiting for transfers between devices: 6.18 us -> 4.38 us  [partner(): lax.ppermute(value, 'head', [(i, i ^ heads // 2) for i in range(heads)])]
where the time goes in v8:
time: 87.8 us; the launch traced here: 87.6 us
  starting transfers between devices  54.1 us (62%)
  Pallas kernels  14 us (16%)
  waiting for transfers between devices  13.8 us (16%)
  local copies, waits for them, and re-layouts  3.65 us (4%)
  other arithmetic  1.85 us (2%)
    ppermute x12, starting transfers between devices, permute(): return lax.ppermute(value, 'ctx', pairs)  47 us
    pallas_call x7, Pallas kernels, call(): pl.pallas_call(kernel, out_shape=shapes, in_specs=specs, out_specs=[VMEM]...  14 us
    ppermute x12, waiting for transfers between devices, permute(): return lax.ppermute(value, 'ctx', pairs)  9.4 us
    ppermute x2, starting transfers between devices, partner(): lax.ppermute(value, 'head', [(i, i ^ heads // 2) for i in range(heads)])  7.07 us
    ppermute x2, waiting for transfers between devices, partner(): lax.ppermute(value, 'head', [(i, i ^ heads // 2) for i in range(heads)])  4.38 us
    unnamed x10, local copies, waits for them, and re-layouts  2.25 us
  transfers between devices with their start and end apart: 14, of which 4 were waited for; matrix products, arithmetic and copies ran while one was open for 2% of the time, Pallas kernels for 13%

profile of v8, /device:TPU:1, one launch (start us, length us, event | category | flops | bytes accessed | tf_op | source)
XLA Modules:
  0.0 87.6 jit_solution(8852816718464251764)
XLA Ops:
  0.0 0.7 fusion
  0.7 0.7 slice.16
  1.4 3.5 %collective-permute-start = (bf16[32,128]{1,0:T(8,128)(2,1)S(1)}, bf16[32,128]{1,0:T(8,128)(2,1)S(1)}, u32[]{:S(2)}, u32[]{:S(2)}) collective-permute-start(bf16[32,128]{1,0:T(8,128)(2,1)S(1)} %pad_maximum_fusion.2), channel_id=1, source_target_pairs={{0,32},{32,64},{64,96},{96,128},{128,160},{160,192},{192,224},{224... | collective-permute-start | bytes 24584 | tf_op jit(solution)/shard_map/ppermute | solution.py:414
  4.9 4.0 %collective-permute-start.4 = (bf16[512,128]{1,0:T(8,128)(2,1)}, bf16[512,128]{1,0:T(8,128)(2,1)S(1)}, u32[]{:S(2)}, u32[]{:S(2)}) collective-permute-start(bf16[512,128]{1,0:T(8,128)(2,1)} %a_ref.1), channel_id=1, source_target_pairs={{0,64},{32,96},{64,128},{96,160},{128,192},{160,224},{192,256},{22... | collective-permute-start | bytes 393224 | tf_op jit(solution)/shard_map/ppermute | solution.py:414
  8.9 1.3 %collective-permute-start.3 = (bf16[16,128]{1,0:T(8,128)(2,1)S(1)}, bf16[16,128]{1,0:T(8,128)(2,1)S(1)}, u32[]{:S(2)}, u32[]{:S(2)}) collective-permute-start(bf16[16,128]{1,0:T(8,128)(2,1)S(1)} %get-tuple-element.47), channel_id=1, source_target_pairs={{0,480},{32,0},{64,32},{96,64},{128,96},{160,128},{192,160},{224,1... | collective-permute-start | bytes 12296 | tf_op jit(solution)/shard_map/ppermute | solution.py:414
  10.2 3.3 %collective-permute-start.2 = (bf16[512,128]{1,0:T(8,128)(2,1)}, bf16[512,128]{1,0:T(8,128)(2,1)S(1)}, u32[]{:S(2)}, u32[]{:S(2)}) collective-permute-start(bf16[512,128]{1,0:T(8,128)(2,1)} %param.9), channel_id=1, source_target_pairs={{0,16},{1,17},{2,18},{3,19},{4,20},{5,21},{6,22},{7,23},{8,24},{9,... | collective-permute-start | bytes 393224 | tf_op jit(solution)/shard_map/ppermute | solution.py:420
  13.6 0.0 collective-permute-done.edge_ref
  13.6 0.9 %pad_maximum_fusion.1.own_ref = bf16[528,128]{1,0:T(8,128)(2,1)S(1)} fusion(bf16[16,128]{1,0:T(8,128)(2,1)S(1)} %get-tuple-element.50, bf16[512,128]{1,0:T(8,128)(2,1)} %param.7), kind=kLoop, calls=%fused_computation.1 | loop fusion | flops 270336 | bytes 270336 | tf_op jit(solution)/shard_map/concatenate | solution.py:428
  14.5 6.6 %collective-permute-start.1 = (bf16[528,128]{1,0:T(8,128)(2,1)S(1)}, bf16[528,128]{1,0:T(8,128)(2,1)S(1)}, u32[]{:S(2)}, u32[]{:S(2)}) collective-permute-start(bf16[528,128]{1,0:T(8,128)(2,1)S(1)} %pad_maximum_fusion.1.own_ref), channel_id=1, source_target_pairs={{0,32},{32,0},{64,96},{96,64},{128,160},{160,128},{192,224},{224,1... | collective-permute-start | bytes 405512 | tf_op jit(solution)/shard_map/ppermute | solution.py:414
  21.1 0.0 collective-permute-done.3
  21.1 0.0 collective-permute-done.2
  21.1 0.9 %pad_maximum_fusion.b_ref = bf16[1056,128]{1,0:T(8,128)(2,1)S(1)} fusion(bf16[16,128]{1,0:T(8,128)(2,1)S(1)} %collective-permute-done.3, bf16[16,128]{1,0:T(8,128)(2,1)S(1)} %get-tuple-element.49, bf16[512,128]{1,0:T(8,128)(2,1)S(1)} %collective-permute-done.2, bf16[512,128]{1,0:T(8,128)(2,1)} %param.9), kind=kLoop, calls=%fused_computation | loop fusion | flops 1081344 | bytes 540672 | tf_op jit(solution)/shard_map/concatenate | solution.py:432
  22.1 1.9 %collective-permute-start.6 = (bf16[1056,128]{1,0:T(8,128)(2,1)S(1)}, bf16[1056,128]{1,0:T(8,128)(2,1)S(1)}, u32[]{:S(2)}, u32[]{:S(2)}) collective-permute-start(bf16[1056,128]{1,0:T(8,128)(2,1)S(1)} %pad_maximum_fusion.b_ref), channel_id=1, source_target_pairs={{0,64},{32,96},{64,128},{96,160},{128,192},{160,224},{192,256},{22... | collective-permute-start | bytes 811016 | tf_op jit(solution)/shard_map/ppermute | solution.py:414
  24.0 0.0 collective-permute-done.1.other_ref
  24.0 0.0 copy-start
  24.0 0.9 %copy-done = bf16[512,128]{1,0:T(8,128)(2,1)S(1)} copy-done((bf16[512,128]{1,0:T(8,128)(2,1)S(1)}, bf16[512,128]{1,0:T(8,128)(2,1)}, u32[]{:S(2)}) %copy-start) | copy-done | bytes 131096
  24.9 0.0 copy-start.3
  24.9 0.7 copy-done.3
  25.6 0.0 copy-start.4
  25.6 0.7 copy-done.4
  26.2 7.5 %shard_map.73 = (bf16[1536,768]{1,0:T(8,128)(2,1)S(1)}, f32[1024,384]{1,0:T(8,128)S(1)}, f32[8,128]{1,0:T(8,128)}) custom-call(s32[8]{0:T(128)S(1)} %copy-done.4, f32[6,1,11]{2,1,0:T(1,128)S(1)} %bitcast.5, bf16[528,128]{1,0:T(8,128)(2,1)S(1)} %pad_maximum_fusion.1.own_ref, bf16[528,128]{1,0:T(8,128)(2,1)S(1)} %collective-permute-done.1.other_ref, ...), custom_call_target="tpu_custom_call" | custom-call | flops 120259084288 | bytes 4194304 | tf_op jit(solution)/shard_map/pallas_call | solution.py:394
  33.7 0.0 collective-permute-done.4.a_ref
  33.7 3.3 %collective-permute-start.5 = (bf16[512,128]{1,0:T(8,128)(2,1)S(1)}, bf16[512,128]{1,0:T(8,128)(2,1)S(1)}, u32[]{:S(2)}, u32[]{:S(2)}) collective-permute-start(bf16[512,128]{1,0:T(8,128)(2,1)S(1)} %collective-permute-done.4.a_ref), channel_id=1, source_target_pairs={{0,64},{32,96},{64,128},{96,160},{128,192},{160,224},{192,256},{22... | collective-permute-start | bytes 393224 | tf_op jit(solution)/shard_map/ppermute | solution.py:414
  37.0 0.0 collective-permute-done.6.b_ref
  37.0 3.4 %collective-permute-start.8 = (bf16[1056,128]{1,0:T(8,128)(2,1)S(1)}, bf16[1056,128]{1,0:T(8,128)(2,1)S(1)}, u32[]{:S(2)}, u32[]{:S(2)}) collective-permute-start(bf16[1056,128]{1,0:T(8,128)(2,1)S(1)} %collective-permute-done.6.b_ref), channel_id=1, source_target_pairs={{0,64},{32,96},{64,128},{96,160},{128,192},{160,224},{192,256},{22... | collective-permute-start | bytes 811016 | tf_op jit(solution)/shard_map/ppermute | solution.py:414
  40.4 1.3 %shard_map.74 = (f32[1024,384]{1,0:T(8,128)S(1)}, f32[8,128]{1,0:T(8,128)}) custom-call(s32[8]{0:T(128)S(1)} %copy-done.4, f32[6,1,11]{2,1,0:T(1,128)S(1)} %bitcast.6, bf16[1536,768]{1,0:T(8,128)(2,1)S(1)} %get-tuple-element.26.qp_ref, bf16[512,128]{1,0:T(8,128)(2,1)S(1)} %collective-permute-done.4.a_ref, ...), custom_call_target="tpu_custom_call" | custom-call | flops 120259084288 | bytes 4194304 | tf_op jit(solution)/shard_map/pallas_call | solution.py:394
  41.7 0.0 collective-permute-done.5.a_ref
  41.7 8.3 %collective-permute-start.7 = (bf16[512,128]{1,0:T(8,128)(2,1)S(1)}, bf16[512,128]{1,0:T(8,128)(2,1)S(1)}, u32[]{:S(2)}, u32[]{:S(2)}) collective-permute-start(bf16[512,128]{1,0:T(8,128)(2,1)S(1)} %collective-permute-done.5.a_ref), channel_id=1, source_target_pairs={{0,64},{32,96},{64,128},{96,160},{128,192},{160,224},{192,256},{22... | collective-permute-start | bytes 393224 | tf_op jit(solution)/shard_map/ppermute | solution.py:414
  50.0 0.0 collective-permute-done.8.b_ref
  50.0 2.1 %collective-permute-start.10 = (bf16[1056,128]{1,0:T(8,128)(2,1)S(1)}, bf16[1056,128]{1,0:T(8,128)(2,1)S(1)}, u32[]{:S(2)}, u32[]{:S(2)}) collective-permute-start(bf16[1056,128]{1,0:T(8,128)(2,1)S(1)} %collective-permute-done.8.b_ref), channel_id=1, source_target_pairs={{0,64},{32,96},{64,128},{96,160},{128,192},{160,224},{192,256},{22... | collective-permute-start | bytes 811016 | tf_op jit(solution)/shard_map/ppermute | solution.py:414
  52.1 1.3 %shard_map.75 = (f32[1024,384]{1,0:T(8,128)S(1)}, f32[8,128]{1,0:T(8,128)}) custom-call(s32[8]{0:T(128)S(1)} %copy-done.4, f32[6,1,11]{2,1,0:T(1,128)S(1)} %bitcast.7, bf16[1536,768]{1,0:T(8,128)(2,1)S(1)} %get-tuple-element.26.qp_ref, bf16[512,128]{1,0:T(8,128)(2,1)S(1)} %collective-permute-done.5.a_ref, ...), custom_call_target="tpu_custom_call" | custom-call | flops 120259084288 | bytes 4194304 | tf_op jit(solution)/shard_map/pallas_call | solution.py:394
  53.5 0.0 collective-permute-done.7.a_ref
  53.5 3.0 %collective-permute-start.9 = (bf16[512,128]{1,0:T(8,128)(2,1)S(1)}, bf16[512,128]{1,0:T(8,128)(2,1)S(1)}, u32[]{:S(2)}, u32[]{:S(2)}) collective-permute-start(bf16[512,128]{1,0:T(8,128)(2,1)S(1)} %collective-permute-done.7.a_ref), channel_id=1, source_target_pairs={{0,64},{32,96},{64,128},{96,160},{128,192},{160,224},{192,256},{22... | collective-permute-start | bytes 393224 | tf_op jit(solution)/shard_map/ppermute | solution.py:414
  56.5 3.1 %collective-permute-done.10.b_ref = bf16[1056,128]{1,0:T(8,128)(2,1)S(1)} collective-permute-done((bf16[1056,128]{1,0:T(8,128)(2,1)S(1)}, bf16[1056,128]{1,0:T(8,128)(2,1)S(1)}, u32[]{:S(2)}, u32[]{:S(2)}) %collective-permute-start.10) | collective-permute-done | bytes 270368 | tf_op jit(solution)/shard_map/ppermute | solution.py:414
  59.6 2.7 %collective-permute-start.11 = (bf16[1056,128]{1,0:T(8,128)(2,1)S(1)}, bf16[1056,128]{1,0:T(8,128)(2,1)S(1)}, u32[]{:S(2)}, u32[]{:S(2)}) collective-permute-start(bf16[1056,128]{1,0:T(8,128)(2,1)S(1)} %collective-permute-done.10.b_ref), channel_id=1, source_target_pairs={{0,64},{32,96},{64,128},{96,160},{128,192},{160,224},{192,256},{22... | collective-permute-start | bytes 811016 | tf_op jit(solution)/shard_map/ppermute | solution.py:414
  62.3 1.3 %shard_map.76 = (f32[1024,384]{1,0:T(8,128)S(1)}, f32[8,128]{1,0:T(8,128)}) custom-call(s32[8]{0:T(128)S(1)} %copy-done.4, f32[6,1,11]{2,1,0:T(1,128)S(1)} %bitcast.8, bf16[1536,768]{1,0:T(8,128)(2,1)S(1)} %get-tuple-element.26.qp_ref, bf16[512,128]{1,0:T(8,128)(2,1)S(1)} %collective-permute-done.7.a_ref, ...), custom_call_target="tpu_custom_call" | custom-call | flops 120259084288 | bytes 4194304 | tf_op jit(solution)/shard_map/pallas_call | solution.py:394
  63.7 0.0 collective-permute-done.9.a_ref
  63.7 4.4 %collective-permute-done.11.b_ref = bf16[1056,128]{1,0:T(8,128)(2,1)S(1)} collective-permute-done((bf16[1056,128]{1,0:T(8,128)(2,1)S(1)}, bf16[1056,128]{1,0:T(8,128)(2,1)S(1)}, u32[]{:S(2)}, u32[]{:S(2)}) %collective-permute-start.11) | collective-permute-done | bytes 270368 | tf_op jit(solution)/shard_map/ppermute | solution.py:414
  68.0 0.8 shard_map.77
  68.9 0.0 copy-start.1
  68.9 0.0 copy-start.2
  68.9 6.9 %collective-permute-start.12 = (f32[512,384]{1,0:T(8,128)S(1)}, f32[512,384]{1,0:T(8,128)S(1)}, u32[]{:S(2)}, u32[]{:S(2)}) collective-permute-start(f32[512,384]{1,0:T(8,128)S(1)} %get-tuple-element.44), channel_id=1, source_target_pairs={{0,32},{32,0},{64,96},{96,64},{128,160},{160,128},{192,224},{224,1... | collective-permute-start | bytes 2359304 | tf_op jit(solution)/shard_map/ppermute | solution.py:414
  75.8 1.9 %collective-permute-done.12.other_ref = f32[512,384]{1,0:T(8,128)S(1)} collective-permute-done((f32[512,384]{1,0:T(8,128)S(1)}, f32[512,384]{1,0:T(8,128)S(1)}, u32[]{:S(2)}, u32[]{:S(2)}) %collective-permute-start.12) | collective-permute-done | bytes 786464 | tf_op jit(solution)/shard_map/ppermute | solution.py:414
  77.7 0.4 shard_map.78
  78.1 3.7 %collective-permute-start.13 = (bf16[512,128]{1,0:T(8,128)(2,1)S(1)}, bf16[512,128]{1,0:T(8,128)(2,1)S(1)}, u32[]{:S(2)}, u32[]{:S(2)}) collective-permute-start(bf16[512,128]{1,0:T(8,128)(2,1)S(1)} %get-tuple-element.46), channel_id=1, source_target_pairs={{0,16},{1,17},{2,18},{3,19},{4,20},{5,21},{6,22},{7,23},{8,24},{9,... | collective-permute-start | bytes 393224 | tf_op jit(solution)/shard_map/ppermute | solution.py:420
  81.8 4.4 %collective-permute-done.13.cross_ref = bf16[512,128]{1,0:T(8,128)(2,1)S(1)} collective-permute-done((bf16[512,128]{1,0:T(8,128)(2,1)S(1)}, bf16[512,128]{1,0:T(8,128)(2,1)S(1)}, u32[]{:S(2)}, u32[]{:S(2)}) %collective-permute-start.13) | collective-permute-done | bytes 131104 | tf_op jit(solution)/shard_map/ppermute | solution.py:420
  86.2 0.0 copy-done.1
  86.2 0.0 copy-done.2
  86.2 1.4 %shard_map.79 = bf16[512,128]{1,0:T(8,128)(2,1)} custom-call(f32[2]{0:T(128)S(1)} %bitcast.3, f32[512,128]{1,0:T(8,128)S(1)} %get-tuple-element.45.own_ref, bf16[512,128]{1,0:T(8,128)(2,1)S(1)} %collective-permute-done.13.cross_ref, f32[1,128]{1,0:T(1,128)S(1)} %bitcast.4), custom_call_target="tpu_custom_call" | custom-call | bytes 4194304 | tf_op jit(solution)/shard_map/pallas_call | solution.py:394
  (2 shorter events, 0.0 us)
Async XLA Ops:
  1.4 12.2 %collective-permute-start = (bf16[32,128]{1,0:T(8,128)(2,1)S(1)}, bf16[32,128]{1,0:T(8,128)(2,1)S(1)}, u32[]{:S(2)}, u32[]{:S(2)}) collective-permute-start(bf16[32,128]{1,0:T(8,128)(2,1)S(1)} %pad_maximum_fusion.2), channel_id=1, source_target_pairs={{0,32},{32,64},{64,96},{96,128},{128,160},{160,192},{192,224},{224... | collective-permute-start | bytes 24584 | tf_op jit(solution)/shard_map/ppermute | solution.py:414
  4.9 28.9 %collective-permute-start.4 = (bf16[512,128]{1,0:T(8,128)(2,1)}, bf16[512,128]{1,0:T(8,128)(2,1)S(1)}, u32[]{:S(2)}, u32[]{:S(2)}) collective-permute-start(bf16[512,128]{1,0:T(8,128)(2,1)} %a_ref.1), channel_id=1, source_target_pairs={{0,64},{32,96},{64,128},{96,160},{128,192},{160,224},{192,256},{22... | collective-permute-start | bytes 393224 | tf_op jit(solution)/shard_map/ppermute | solution.py:414
  8.9 12.2 %collective-permute-start.3 = (bf16[16,128]{1,0:T(8,128)(2,1)S(1)}, bf16[16,128]{1,0:T(8,128)(2,1)S(1)}, u32[]{:S(2)}, u32[]{:S(2)}) collective-permute-start(bf16[16,128]{1,0:T(8,128)(2,1)S(1)} %get-tuple-element.47), channel_id=1, source_target_pairs={{0,480},{32,0},{64,32},{96,64},{128,96},{160,128},{192,160},{224,1... | collective-permute-start | bytes 12296 | tf_op jit(solution)/shard_map/ppermute | solution.py:414
  10.2 10.9 %collective-permute-start.2 = (bf16[512,128]{1,0:T(8,128)(2,1)}, bf16[512,128]{1,0:T(8,128)(2,1)S(1)}, u32[]{:S(2)}, u32[]{:S(2)}) collective-permute-start(bf16[512,128]{1,0:T(8,128)(2,1)} %param.9), channel_id=1, source_target_pairs={{0,16},{1,17},{2,18},{3,19},{4,20},{5,21},{6,22},{7,23},{8,24},{9,... | collective-permute-start | bytes 393224 | tf_op jit(solution)/shard_map/ppermute | solution.py:420
  14.5 9.5 %collective-permute-start.1 = (bf16[528,128]{1,0:T(8,128)(2,1)S(1)}, bf16[528,128]{1,0:T(8,128)(2,1)S(1)}, u32[]{:S(2)}, u32[]{:S(2)}) collective-permute-start(bf16[528,128]{1,0:T(8,128)(2,1)S(1)} %pad_maximum_fusion.1.own_ref), channel_id=1, source_target_pairs={{0,32},{32,0},{64,96},{96,64},{128,160},{160,128},{192,224},{224,1... | collective-permute-start | bytes 405512 | tf_op jit(solution)/shard_map/ppermute | solution.py:414
  22.1 15.0 %collective-permute-start.6 = (bf16[1056,128]{1,0:T(8,128)(2,1)S(1)}, bf16[1056,128]{1,0:T(8,128)(2,1)S(1)}, u32[]{:S(2)}, u32[]{:S(2)}) collective-permute-start(bf16[1056,128]{1,0:T(8,128)(2,1)S(1)} %pad_maximum_fusion.b_ref), channel_id=1, source_target_pairs={{0,64},{32,96},{64,128},{96,160},{128,192},{160,224},{192,256},{22... | collective-permute-start | bytes 811016 | tf_op jit(solution)/shard_map/ppermute | solution.py:414
  24.0 0.9 %copy-start = (bf16[512,128]{1,0:T(8,128)(2,1)S(1)}, bf16[512,128]{1,0:T(8,128)(2,1)}, u32[]{:S(2)}) copy-start(bf16[512,128]{1,0:T(8,128)(2,1)} %a_ref.1) | copy-start | bytes 393220
  24.9 0.7 copy-start.3
  25.6 0.7 copy-start.4
  33.7 7.9 %collective-permute-start.5 = (bf16[512,128]{1,0:T(8,128)(2,1)S(1)}, bf16[512,128]{1,0:T(8,128)(2,1)S(1)}, u32[]{:S(2)}, u32[]{:S(2)}) collective-permute-start(bf16[512,128]{1,0:T(8,128)(2,1)S(1)} %collective-permute-done.4.a_ref), channel_id=1, source_target_pairs={{0,64},{32,96},{64,128},{96,160},{128,192},{160,224},{192,256},{22... | collective-permute-start | bytes 393224 | tf_op jit(solution)/shard_map/ppermute | solution.py:414
  37.0 13.0 %collective-permute-start.8 = (bf16[1056,128]{1,0:T(8,128)(2,1)S(1)}, bf16[1056,128]{1,0:T(8,128)(2,1)S(1)}, u32[]{:S(2)}, u32[]{:S(2)}) collective-permute-start(bf16[1056,128]{1,0:T(8,128)(2,1)S(1)} %collective-permute-done.6.b_ref), channel_id=1, source_target_pairs={{0,64},{32,96},{64,128},{96,160},{128,192},{160,224},{192,256},{22... | collective-permute-start | bytes 811016 | tf_op jit(solution)/shard_map/ppermute | solution.py:414
  41.7 11.8 %collective-permute-start.7 = (bf16[512,128]{1,0:T(8,128)(2,1)S(1)}, bf16[512,128]{1,0:T(8,128)(2,1)S(1)}, u32[]{:S(2)}, u32[]{:S(2)}) collective-permute-start(bf16[512,128]{1,0:T(8,128)(2,1)S(1)} %collective-permute-done.5.a_ref), channel_id=1, source_target_pairs={{0,64},{32,96},{64,128},{96,160},{128,192},{160,224},{192,256},{22... | collective-permute-start | bytes 393224 | tf_op jit(solution)/shard_map/ppermute | solution.py:414
  50.0 9.6 %collective-permute-start.10 = (bf16[1056,128]{1,0:T(8,128)(2,1)S(1)}, bf16[1056,128]{1,0:T(8,128)(2,1)S(1)}, u32[]{:S(2)}, u32[]{:S(2)}) collective-permute-start(bf16[1056,128]{1,0:T(8,128)(2,1)S(1)} %collective-permute-done.8.b_ref), channel_id=1, source_target_pairs={{0,64},{32,96},{64,128},{96,160},{128,192},{160,224},{192,256},{22... | collective-permute-start | bytes 811016 | tf_op jit(solution)/shard_map/ppermute | solution.py:414
  53.5 10.2 %collective-permute-start.9 = (bf16[512,128]{1,0:T(8,128)(2,1)S(1)}, bf16[512,128]{1,0:T(8,128)(2,1)S(1)}, u32[]{:S(2)}, u32[]{:S(2)}) collective-permute-start(bf16[512,128]{1,0:T(8,128)(2,1)S(1)} %collective-permute-done.7.a_ref), channel_id=1, source_target_pairs={{0,64},{32,96},{64,128},{96,160},{128,192},{160,224},{192,256},{22... | collective-permute-start | bytes 393224 | tf_op jit(solution)/shard_map/ppermute | solution.py:414
  59.6 8.4 %collective-permute-start.11 = (bf16[1056,128]{1,0:T(8,128)(2,1)S(1)}, bf16[1056,128]{1,0:T(8,128)(2,1)S(1)}, u32[]{:S(2)}, u32[]{:S(2)}) collective-permute-start(bf16[1056,128]{1,0:T(8,128)(2,1)S(1)} %collective-permute-done.10.b_ref), channel_id=1, source_target_pairs={{0,64},{32,96},{64,128},{96,160},{128,192},{160,224},{192,256},{22... | collective-permute-start | bytes 811016 | tf_op jit(solution)/shard_map/ppermute | solution.py:414
  68.9 17.3 %copy-start.1 = (f32[1,2]{1,0:T(1,128)S(1)}, f32[1,2]{1,0:T(1,128)}, u32[]{:S(2)}) copy-start(f32[1,2]{1,0:T(1,128)} %param.11) | copy-start | bytes 28
  68.9 17.3 %copy-start.2 = (f32[128]{0:T(128)S(1)}, f32[128]{0:T(128)}, u32[]{:S(2)}) copy-start(f32[128]{0:T(128)} %param.12) | copy-start | bytes 1540
  68.9 8.8 %collective-permute-start.12 = (f32[512,384]{1,0:T(8,128)S(1)}, f32[512,384]{1,0:T(8,128)S(1)}, u32[]{:S(2)}, u32[]{:S(2)}) collective-permute-start(f32[512,384]{1,0:T(8,128)S(1)} %get-tuple-element.44), channel_id=1, source_target_pairs={{0,32},{32,0},{64,96},{96,64},{128,160},{160,128},{192,224},{224,1... | collective-permute-start | bytes 2359304 | tf_op jit(solution)/shard_map/ppermute | solution.py:414
  78.1 8.1 %collective-permute-start.13 = (bf16[512,128]{1,0:T(8,128)(2,1)S(1)}, bf16[512,128]{1,0:T(8,128)(2,1)S(1)}, u32[]{:S(2)}, u32[]{:S(2)}) collective-permute-start(bf16[512,128]{1,0:T(8,128)(2,1)S(1)} %get-tuple-element.46), channel_id=1, source_target_pairs={{0,16},{1,17},{2,18},{3,19},{4,20},{5,21},{6,22},{7,23},{8,24},{9,... | collective-permute-start | bytes 393224 | tf_op jit(solution)/shard_map/ppermute | solution.py:420
